TPU v7x, 128 devices: a whole 4x4x4 slice. The times are simulated.
128 devices in a mesh: shot: 16 (over y_hi, x, core), surf: 8 (over y_lo, z).
Axes of the slice: x: 4, y: 4 (y_hi: 2, y_lo: 2; y = y_hi * 2 + y_lo), z: 4, core: 2. Of those that a mesh axis runs over, the one named last changes fastest.
Arguments:
- shot_spec: bfloat16 [2, 16, 2048, 2048], P(None, None, 'shot', 'surf'), may hold values from -6 to 6
- recv_spec: bfloat16 [2, 16, 1536, 2048], P(None, None, 'shot', 'surf'), may hold values from -0.09375 to 0.09375
- wavelet: float32 [2, 16], replicated, may hold values from -4 to 4
Outputs:
- multiples: bfloat16 [2, 16, 2048, 1536], P(None, None, 'shot', 'surf')
All inputs are finite; a program needn't handle non-finite values.
Results may differ from a plain program's by a relative error of at most 0.019.
Values may be sent and summed in bfloat16 or wider, within the bound.
No kernel may reach another device: no remote copies, remote signals or barrier semaphores. Data moves between devices by JAX's collectives and lax.ppermute only.
A program may use at most 128 MiB of HBM per device.

v0:
```python
import jax
import jax.numpy as jnp
from jax import lax
from jax.sharding import PartitionSpec as P


def complex_product(left_factor, right_factor):
    product_form = "qpu,qou->qpo"
    real_term = jnp.einsum(
        product_form, left_factor[0], right_factor[0], preferred_element_type=jnp.float32
    ) - jnp.einsum(
        product_form, left_factor[1], right_factor[1], preferred_element_type=jnp.float32
    )
    imaginary_term = jnp.einsum(
        product_form, left_factor[0], right_factor[1], preferred_element_type=jnp.float32
    ) + jnp.einsum(
        product_form, left_factor[1], right_factor[0], preferred_element_type=jnp.float32
    )
    return jnp.stack([real_term, imaginary_term])


def apply_wavelet(wave, summed):
    w_real = wave[0][:, None, None]
    w_imag = wave[1][:, None, None]
    output_real = w_real * summed[0] - w_imag * summed[1]
    out_imag = w_real * summed[1] + w_imag * summed[0]
    return jnp.stack([output_real, out_imag]).astype(jnp.bfloat16)


def on_device(shot_spec, recv_spec, wavelet):
    terms = complex_product(shot_spec, lax.all_gather(recv_spec, "shot", axis=2, tiled=True))
    summed = lax.psum_scatter(
        terms.astype(jnp.bfloat16), "surf", scatter_dimension=3, tiled=True
    ).astype(jnp.float32)
    return apply_wavelet(wavelet, summed)


def solution(mesh):
    in_specs = (P(None, None, "shot", "surf"), P(None, None, "shot", "surf"), P())
    out_specs = P(None, None, "shot", "surf")
    return jax.shard_map(
        on_device, mesh=mesh, in_specs=in_specs, out_specs=out_specs, check_vma=False
    )
```

profile of v0, /device:TPU:1, one launch (start us, length us, event | category | flops | bytes accessed | tf_op | source)
XLA Modules:
  0.0 383.6 jit_solution(6933201634032005596)
XLA Ops:
  6.5 0.0 all-gather.2.cloned.1.call-start
  6.5 0.7 all-gather.2.cloned.1.call-update
  7.3 0.0 copy-start
  7.3 0.0 reduce-scatter.2.cloned.1.call-start
  7.3 155.1 %all-gather.2.cloned.1.call-done = bf16[2,16,1536,256]{3,2,1,0:T(8,128)(2,1)} async-done(((bf16[2,16,96,256]{3,2,1,0:T(8,128)(2,1)}), bf16[2,16,1536,256]{3,2,1,0:T(8,128)(2,1)}) %all-gather.2.cloned.1.call-update) | async-done | bytes 25165840 | tf_op jit(solution)/shard_map/all_gather | solution.py:31
  162.4 13.5 %fusion.1 = f32[16,128,1536]{2,1,0:T(8,128)} fusion(bf16[2,16,1536,256]{3,2,1,0:T(8,128)(2,1)} %all-gather.2.cloned.1.call-done, bf16[2,16,128,256]{3,2,1,0:T(8,128)(2,1)} %param.3), kind=kOutput, calls=%fused_computation.6 | convolution fusion | flops 1610612736 | bytes 26214400 | tf_op jit(solution)/shard_map/qpu,qou->qpo/dot_general | solution.py:9
  176.0 0.0 copy-done
  176.0 13.4 %fusion = f32[16,128,1536]{2,1,0:T(8,128)} fusion(bf16[2,16,1536,256]{3,2,1,0:T(8,128)(2,1)} %all-gather.2.cloned.1.call-done, bf16[2,16,128,256]{3,2,1,0:T(8,128)(2,1)S(1)} %copy-done), kind=kOutput, calls=%fused_computation.5 | convolution fusion | flops 1610612736 | bytes 26214400 | tf_op jit(solution)/shard_map/qpu,qou->qpo/dot_general | solution.py:16
  189.3 12.9 %fusion.4 = bf16[1,16,128,1536]{3,2,1,0:T(8,128)(2,1)} fusion(f32[16,128,1536]{2,1,0:T(8,128)} %fusion.1, bf16[2,16,1536,256]{3,2,1,0:T(8,128)(2,1)} %all-gather.2.cloned.1.call-done, bf16[2,16,128,256]{3,2,1,0:T(8,128)(2,1)S(1)} %copy-done), kind=kOutput, calls=%fused_computation.9 | convolution fusion | flops 1616904192 | bytes 32505856 | tf_op jit(solution)/shard_map/qpu,qou->qpo/dot_general | solution.py:11
  202.3 13.0 %fusion.5 = bf16[1,16,128,1536]{3,2,1,0:T(8,128)(2,1)} fusion(f32[16,128,1536]{2,1,0:T(8,128)} %fusion, bf16[2,16,1536,256]{3,2,1,0:T(8,128)(2,1)} %all-gather.2.cloned.1.call-done, bf16[2,16,128,256]{3,2,1,0:T(8,128)(2,1)S(1)} %copy-done), kind=kOutput, calls=%fused_computation.10 | convolution fusion | flops 1616904192 | bytes 32505856 | tf_op jit(solution)/shard_map/qpu,qou->qpo/dot_general | solution.py:14
  215.2 10.5 %pad_maximum_fusion = bf16[2,16,128,1536]{3,2,1,0:T(8,128)(2,1)} fusion(bf16[1,16,128,1536]{3,2,1,0:T(8,128)(2,1)} %fusion.5, bf16[1,16,128,1536]{3,2,1,0:T(8,128)(2,1)} %fusion.4), kind=kLoop, calls=%fused_computation.2 | loop fusion | flops 6291456 | bytes 25165824 | tf_op jit(solution)/shard_map/stack | solution.py:19
  225.7 16.8 %copy.5 = bf16[2,16,128,1536]{2,1,0,3:T(8,128)(2,1)} copy(bf16[2,16,128,1536]{3,2,1,0:T(8,128)(2,1)} %pad_maximum_fusion) | data formatting | bytes 25165824 | tf_op jit(solution)/shard_map/stack | solution.py:19
  242.5 0.0 copy-start.1
  242.5 0.0 reduce-scatter.2.cloned.1.call-update
  242.5 0.7 copy-done.1
  243.2 129.3 %reduce-scatter.2.cloned.1.call-done = bf16[2,16,128,192]{2,1,0,3:T(8,128)(2,1)} async-done(((bf16[2,16,128,1536]{2,1,0,3:T(8,128)(2,1)}), bf16[2,16,128,192]{2,1,0,3:T(8,128)(2,1)}) %reduce-scatter.2.cloned.1.call-update) | async-done | bytes 1572880 | tf_op jit(solution)/shard_map/reduce_scatter | solution.py:32
  372.5 1.8 convert_element_type.2
  374.4 0.5 subtract_convert_fusion.1
  374.8 0.1 pad_maximum_fusion.1
  375.0 1.8 copy.6
  (1 shorter events, 0.0 us)
Async XLA Ops:
  6.5 155.9 %all-gather.2.cloned.1.call-start = ((), (), s32[]{:S(2)}) async-start(), calls=%async_computation.1 | async-start | bytes 26738688 | tf_op jit(solution)/shard_map/all_gather | solution.py:31
  7.3 168.7 %copy-start = (bf16[2,16,128,256]{3,2,1,0:T(8,128)(2,1)S(1)}, bf16[2,16,128,256]{3,2,1,0:T(8,128)(2,1)}, u32[]{:S(2)}) copy-start(bf16[2,16,128,256]{3,2,1,0:T(8,128)(2,1)} %param.3) | copy-start | bytes 6291460
  7.3 365.2 %reduce-scatter.2.cloned.1.call-start = ((), (), s32[]{:S(2)}) async-start(), calls=%async_computation.2 | async-start | bytes 14155776 | tf_op jit(solution)/shard_map/reduce_scatter | solution.py:32
  242.5 0.7 copy-start.1
Sparse Core Ops, SparseCore 0:
  9.8 152.5 all-gather.1
  242.6 129.8 reduce-scatter.1
where the time goes:
time: 384 us
  waiting for transfers between devices  285 us (74%)
  matrix products  52.8 us (14%)
  local copies, waits for them, and re-layouts  19.2 us (5%)
  between operations  13.4 us (3%)
  other arithmetic  12.9 us (3%)
    all_gather x1, waiting for transfers between devices, on_device(): lax.all_gather(recv_spec, 'shot', axis=2, tiled=True)  155 us
    reduce_scatter x1, waiting for transfers between devices, on_device(): lax.psum_scatter(terms.astype(jnp.bfloat16), 'surf', scatter_dimension=3,...  129 us
    another operation x1, local copies, waits for them, and re-layouts, complex_product(): return jnp.stack([real_term, imaginary_term])  16.8 us
    dot_general x1, matrix products, complex_product(): jnp.einsum(product_form, left_factor[0], right_factor[0], preferred_eleme...  13.5 us
    dot_general x1, matrix products, complex_product(): jnp.einsum(product_form, left_factor[1], right_factor[0], preferred_eleme...  13.4 us
    dot_general x1, matrix products, complex_product(): jnp.einsum(product_form, left_factor[0], right_factor[1], preferred_eleme...  13 us
    dot_general x1, matrix products, complex_product(): jnp.einsum(product_form, left_factor[1], right_factor[1], preferred_eleme...  12.9 us
    another operation x1, other arithmetic, complex_product(): return jnp.stack([real_term, imaginary_term])  10.5 us
  transfers between devices with their start and end apart: 2, of which 2 were waited for; matrix products, arithmetic and copies ran while one was open for 0% of the time, Pallas kernels for 0%

commit v1 on v0

v1 whole, which is shorter than its diff:
```python
import functools

import jax
import jax.numpy as jnp
from jax import lax
from jax.experimental import pallas as pl
from jax.experimental.pallas import tpu as pltpu
from jax.sharding import Mesh
from jax.sharding import PartitionSpec as P

FREQUENCY = ("yh", "yl", "z")
PLACES = ("yh", "yl", "z", "c")


def product_kernel(place, wave, q_own, q_left, q_right, q_far, p_own, p_other, out):
    rows = q_own.shape[2]
    groups = q_own.shape[0] // 2
    me, frequency = place[0], place[2]
    w_real, w_imag = wave[0, frequency], wave[1, frequency]

    def apply(p_ref):
        right_factor = jnp.concatenate(
            [p_ref[j].reshape(-1, p_ref.shape[-1]) for j in range(groups)], axis=1
        )
        left_factor = jnp.concatenate(
            [
                jnp.concatenate(
                    [q[half * groups + j].reshape(2 * rows, -1) for j in range(groups)], axis=1
                )
                for q in (q_own, q_left, q_right, q_far)
                for half in range(2)
            ],
            axis=0,
        )
        terms = lax.dot_general(
            left_factor,
            right_factor,
            (((1,), (1,)), ((), ())),
            preferred_element_type=jnp.float32,
        )
        shots = terms.shape[1] // 2
        for k, step in enumerate((0, 3, 1, 2)):
            to = lax.rem(me + step, 4)
            for half in range(2):
                at = (2 * k + half) * 2 * rows
                real, imag = terms[at : at + rows], terms[at + rows : at + 2 * rows]
                s_real = real[:, :shots] - imag[:, shots:]
                s_imag = real[:, shots:] + imag[:, :shots]
                out[0, half, to, 0, 0] = (w_real * s_real - w_imag * s_imag).astype(out.dtype)
                out[0, half, to, 0, 1] = (w_real * s_imag + w_imag * s_real).astype(out.dtype)

    @pl.when(pl.program_id(0) == 0)
    def _():
        apply(p_own)

    @pl.when(pl.program_id(0) == 1)
    def _():
        apply(p_other)


def product(place, wavelet, blocks, p_own, p_other):
    sources, _, rows, depth = blocks[0].shape
    shots = p_own.shape[2]
    q_spec = pl.BlockSpec((sources, 2, rows, depth), lambda d, s, place: (0, 0, 0, 0))
    p_block = (sources // 2, 2, shots, depth)
    flops = 2 * (8 * sources // 2 * rows) * (4 * 2 * shots) * (sources // 2 * depth)
    return pl.pallas_call(
        product_kernel,
        out_shape=jax.ShapeDtypeStruct((2, 2, 4, 2, 2, rows, shots), jnp.bfloat16),
        grid_spec=pltpu.PrefetchScalarGridSpec(
            num_scalar_prefetch=1,
            grid=(2, 2),
            in_specs=[pl.BlockSpec(memory_space=pltpu.SMEM)]
            + [q_spec] * 4
            + [
                pl.BlockSpec(p_block, lambda d, s, place: (jnp.where(d == 0, s, 1), 0, 0, 0)),
                pl.BlockSpec(p_block, lambda d, s, place: (jnp.where(d == 1, s, 0), 0, 0, 0)),
            ],
            out_specs=pl.BlockSpec(
                (1, 2, 4, 1, 2, rows, shots),
                lambda d, s, place: (s, 0, 0, lax.rem(place[1] + d, 2), 0, 0, 0),
            ),
        ),
        compiler_params=pltpu.CompilerParams(vmem_limit_bytes=48 * 2**20),
        cost_estimate=pl.CostEstimate(
            flops=flops,
            bytes_accessed=2 * (4 * blocks[0].size + 2 * p_own.size + 32 * 2 * rows * shots),
            transcendentals=0,
        ),
    )(place, wavelet, *blocks, p_own, p_other)


def shift(value, axis, size, step):
    return lax.ppermute(value, axis, [(i, (i + step) % size) for i in range(size)])


def by_frequency(value):
    return lax.all_to_all(value, FREQUENCY, 0, 0, tiled=True)


def on_device(shot_spec, recv_spec, wavelet):
    place = jnp.stack(
        [lax.axis_index("x"), lax.axis_index("c"), lax.axis_index(FREQUENCY)]
    ).astype(jnp.int32)
    half = recv_spec.shape[2] // 2
    recv = by_frequency(recv_spec.swapaxes(0, 1))
    first, second = recv[:, :, :half], recv[:, :, half:]
    first_left, first_right = shift(first, "x", 4, 1), shift(first, "x", 4, -1)
    first_far = shift(first_left, "x", 4, 1)
    second_left, second_right = shift(second, "x", 4, 1), shift(second, "x", 4, -1)
    second_far = shift(second_right, "x", 4, -1)
    shots = by_frequency(shot_spec.swapaxes(0, 1))
    other = shift(shots, "c", 2, 1)
    parts = []
    for blocks in (
        (first, first_left, first_right, first_far),
        (second, second_left, second_right, second_far),
    ):
        out = product(place, wavelet, blocks, shots, other)
        out = out.reshape((-1,) + out.shape[4:])
        out = lax.all_to_all(out, PLACES, 0, 0, tiled=True)
        out = out.reshape((out.shape[0] // 2, 2) + out.shape[1:])
        parts.append(out.transpose(2, 0, 1, 3, 4))
    out = jnp.concatenate(parts, axis=3)
    out = out.reshape(out.shape[:2] + (-1, out.shape[-1]))
    return out.swapaxes(2, 3)


def solution(mesh):
    devices = mesh.devices.reshape(2, 4, 2, 2, 4)
    wide = Mesh(devices, ("yh", "x", "c", "yl", "z"))
    spec = P(None, None, ("yh", "x", "c"), ("yl", "z"))
    return jax.shard_map(
        on_device, mesh=wide, in_specs=(spec, spec, P()), out_specs=spec, check_vma=False
    )
```

time: 384 us -> 158 us (0.41)
  waiting for transfers between devices: 285 us -> 85.3 us
  matrix products: 52.8 us -> 0 us
  starting transfers between devices: 0.04 us -> 45.3 us
  Pallas kernels: 0 us -> 15.5 us
  between operations: 13.4 us -> 0.09 us
  other arithmetic: 12.9 us -> 1.41 us
  local copies, waits for them, and re-layouts: 19.2 us -> 9.42 us
    all_gather x1 -> x0, waiting for transfers between devices: 155 us -> none  [on_device(): lax.all_gather(recv_spec, 'shot', axis=2, tiled=True)]
    reduce_scatter x1 -> x0, waiting for transfers between devices: 129 us -> none  [on_device(): lax.psum_scatter(terms.astype(jnp.bfloat16), 'surf', scatter_dimension=3,...]
    all_to_all x0 -> x4, waiting for transfers between devices: none -> 60.3 us  [the longest x2 40.7 us: by_frequency(): return lax.all_to_all(value, FREQUENCY, 0, 0, tiled=True)]
    dot_general x4 -> x0, matrix products: 52.8 us -> none  [the longest x1 13.5 us: complex_product(): jnp.einsum(product_form, left_factor[0], right_factor[0], preferred_eleme...]
    all_to_all x0 -> x4, starting transfers between devices: none -> 35.1 us  [the longest x2 22.1 us: on_device(): out = lax.all_to_all(out, PLACES, 0, 0, tiled=True)]
    ppermute x0 -> x7, waiting for transfers between devices: none -> 24.9 us  [shift(): lax.ppermute(value, axis, [(i, (i + step) % size) for i in range(size)])]
    another operation x2 -> x0, local copies, waits for them, and re-layouts: 18.5 us -> none  [the longest x1 16.8 us: complex_product(): return jnp.stack([real_term, imaginary_term])]
    pallas_call x0 -> x2, Pallas kernels: none -> 15.5 us  [product(): pl.pallas_call(product_kernel, out_shape=jax.ShapeDtypeStruct((2, 2, 4, 2...]
  transfers between devices with their start and end apart: 2 -> 11, of which waited for: 2 -> 6; matrix products, arithmetic and copies ran while one was open for 0% -> 4% of each run, Pallas kernels for 0% -> 10%
where the time goes in v1:
time: 158 us; the launch traced here: 157 us
  waiting for transfers between devices  85.3 us (54%)
  starting transfers between devices  45.3 us (29%)
  Pallas kernels  15.5 us (10%)
  local copies, waits for them, and re-layouts  9.42 us (6%)
    all_to_all x2, waiting for transfers between devices, by_frequency(): return lax.all_to_all(value, FREQUENCY, 0, 0, tiled=True)  40.7 us
    ppermute x7, waiting for transfers between devices, shift(): lax.ppermute(value, axis, [(i, (i + step) % size) for i in range(size)])  24.9 us
    all_to_all x2, starting transfers between devices, on_device(): out = lax.all_to_all(out, PLACES, 0, 0, tiled=True)  22.1 us
    all_to_all x2, waiting for transfers between devices, on_device(): out = lax.all_to_all(out, PLACES, 0, 0, tiled=True)  19.6 us
    pallas_call x2, Pallas kernels, product(): pl.pallas_call(product_kernel, out_shape=jax.ShapeDtypeStruct((2, 2, 4, 2...  15.5 us
    all_to_all x2, starting transfers between devices, by_frequency(): return lax.all_to_all(value, FREQUENCY, 0, 0, tiled=True)  13 us
    ppermute x7, starting transfers between devices, shift(): lax.ppermute(value, axis, [(i, (i + step) % size) for i in range(size)])  10.3 us
    unnamed x4, local copies, waits for them, and re-layouts  5.82 us
  transfers between devices with their start and end apart: 11, of which 6 were waited for; matrix products, arithmetic and copies ran while one was open for 4% of the time, Pallas kernels for 10%

profile of v1, /device:TPU:1, one launch (start us, length us, event | category | flops | bytes accessed | tf_op | source)
XLA Modules:
  0.0 157.0 jit_solution(14196629334975700978)
XLA Ops:
  0.0 3.1 %copy.12 = bf16[2,16,128,256]{3,2,0,1:T(8,128)(2,1)} copy(bf16[2,16,128,256]{3,2,1,0:T(8,128)(2,1)} %param.3) | data formatting | bytes 4194304 | tf_op args[0]
  3.1 8.6 %all-to-all-start.1 = ((bf16[16,2,128,256]{3,2,1,0:T(8,128)(2,1)}), bf16[16,2,128,256]{3,2,1,0:T(8,128)(2,1)S(1)}, u32[]{:S(2)}, u32[]{:S(2)}) async-start(bf16[16,2,128,256]{3,2,1,0:T(8,128)(2,1)} %bitcast.22), calls=%async_computation.1 | async-start | bytes 4194304 | tf_op jit(solution)/shard_map/all_to_all | solution.py:98
  11.7 2.7 %copy.13 = bf16[2,16,96,256]{3,2,0,1:T(8,128)(2,1)} copy(bf16[2,16,96,256]{3,2,1,0:T(8,128)(2,1)} %param.4) | data formatting | bytes 3145728 | tf_op args[1]
  14.4 25.2 %all-to-all-done.1.p_own = bf16[16,2,128,256]{3,2,1,0:T(8,128)(2,1)S(1)} async-done(((bf16[16,2,128,256]{3,2,1,0:T(8,128)(2,1)}), bf16[16,2,128,256]{3,2,1,0:T(8,128)(2,1)S(1)}, u32[]{:S(2)}, u32[]{:S(2)}) %all-to-all-start.1) | async-done | bytes 2097184 | tf_op jit(solution)/shard_map/all_to_all | solution.py:98
  39.6 4.4 %all-to-all-start = ((bf16[16,2,96,256]{3,2,1,0:T(8,128)(2,1)}), bf16[16,2,96,256]{3,2,1,0:T(8,128)(2,1)}, u32[]{:S(2)}, u32[]{:S(2)}) async-start(bf16[16,2,96,256]{3,2,1,0:T(8,128)(2,1)} %bitcast.23), calls=%async_computation | async-start | bytes 3145728 | tf_op jit(solution)/shard_map/all_to_all | solution.py:98
  44.0 0.0 copy-start
  44.0 3.5 %collective-permute-start.3 = (bf16[16,2,128,256]{3,2,1,0:T(8,128)(2,1)S(1)}, bf16[16,2,128,256]{3,2,1,0:T(8,128)(2,1)}, u32[]{:S(2)}, u32[]{:S(2)}) collective-permute-start(bf16[16,2,128,256]{3,2,1,0:T(8,128)(2,1)S(1)} %all-to-all-done.1.p_own), channel_id=1, source_target_pairs={{0,8},{8,0},{1,9},{9,1},{2,10},{10,2},{3,11},{11,3},{4,12},{12,4},... | collective-permute-start | bytes 6291464 | tf_op jit(solution)/shard_map/ppermute | solution.py:94
  47.6 15.5 %all-to-all-done = bf16[16,2,96,256]{3,2,1,0:T(8,128)(2,1)} async-done(((bf16[16,2,96,256]{3,2,1,0:T(8,128)(2,1)}), bf16[16,2,96,256]{3,2,1,0:T(8,128)(2,1)}, u32[]{:S(2)}, u32[]{:S(2)}) %all-to-all-start) | async-done | bytes 1572896 | tf_op jit(solution)/shard_map/all_to_all | solution.py:98
  63.1 2.4 %fusion = (bf16[16,2,48,256]{3,2,1,0:T(8,128)(2,1)}, bf16[16,2,48,256]{3,2,1,0:T(8,128)(2,1)S(1)}) fusion(bf16[16,2,96,256]{3,2,1,0:T(8,128)(2,1)} %all-to-all-done), kind=kLoop, calls=%fused_computation.6 | loop fusion | bytes 3145728 | tf_op jit(solution)/shard_map/slice | solution.py:107
  65.4 1.2 collective-permute-start
  66.6 1.5 collective-permute-start.5
  68.1 1.3 collective-permute-start.1
  69.4 11.4 %collective-permute-done.q_left = bf16[16,2,48,256]{3,2,1,0:T(8,128)(2,1)} collective-permute-done((bf16[16,2,48,256]{3,2,1,0:T(8,128)(2,1)}, bf16[16,2,48,256]{3,2,1,0:T(8,128)(2,1)}, u32[]{:S(2)}, u32[]{:S(2)}) %collective-permute-start) | collective-permute-done | bytes 786464 | tf_op jit(solution)/shard_map/ppermute | solution.py:94
  80.8 0.0 collective-permute-start.2
  80.8 0.1 pad_add_fusion.place
  80.9 1.2 collective-permute-start.4
  82.1 0.0 collective-permute-done.5.q_right
  82.1 1.6 collective-permute-start.6
  83.6 13.5 %collective-permute-done.1.q_right = bf16[16,2,48,256]{3,2,1,0:T(8,128)(2,1)} collective-permute-done((bf16[16,2,48,256]{3,2,1,0:T(8,128)(2,1)}, bf16[16,2,48,256]{3,2,1,0:T(8,128)(2,1)}, u32[]{:S(2)}, u32[]{:S(2)}) %collective-permute-start.1) | collective-permute-done | bytes 786464 | tf_op jit(solution)/shard_map/ppermute | solution.py:94
  97.1 0.0 collective-permute-done.2.q_far
  97.1 0.0 collective-permute-done.3.p_other
  97.2 7.9 %shard_map.37 = bf16[2,2,4,2,2,48,128]{6,5,4,3,2,1,0:T(8,128)(2,1)} custom-call(s32[3]{0:T(128)S(1)} %pad_add_fusion.place, f32[2,16]{1,0:T(2,128)S(1)} %copy-done, bf16[16,2,48,256]{3,2,1,0:T(8,128)(2,1)} %get-tuple-element.5.q_own, bf16[16,2,48,256]{3,2,1,0:T(8,128)(2,1)} %collective-permute-done.q_left, ...), custom_call_target="tpu_custom_call" | custom-call | flops 12884901888 | bytes 8126464 | tf_op jit(solution)/shard_map/pallas_call | solution.py:67
  105.0 18.3 %all-to-all-start.2 = ((bf16[32,2,48,128]{3,2,1,0:T(8,128)(2,1)}), bf16[32,2,48,128]{3,2,1,0:T(8,128)(2,1)}, u32[]{:S(2)}, u32[]{:S(2)}) async-start(bf16[32,2,48,128]{3,2,1,0:T(8,128)(2,1)} %bitcast.5), calls=%async_computation.2 | async-start | bytes 1572864 | tf_op jit(solution)/shard_map/all_to_all | solution.py:121
  123.3 0.0 collective-permute-done.4.q_left
  123.3 0.0 collective-permute-done.6.q_far
  123.3 7.7 %shard_map.38 = bf16[2,2,4,2,2,48,128]{6,5,4,3,2,1,0:T(8,128)(2,1)} custom-call(s32[3]{0:T(128)S(1)} %pad_add_fusion.place, f32[2,16]{1,0:T(2,128)S(1)} %copy-done, bf16[16,2,48,256]{3,2,1,0:T(8,128)(2,1)S(1)} %get-tuple-element.6.q_own, bf16[16,2,48,256]{3,2,1,0:T(8,128)(2,1)} %collective-permute-done.4.q_left, ...), custom_call_target="tpu_custom_call" | custom-call | flops 12884901888 | bytes 8126464 | tf_op jit(solution)/shard_map/pallas_call | solution.py:67
  131.0 6.6 %all-to-all-done.2 = bf16[32,2,48,128]{3,2,1,0:T(8,128)(2,1)} async-done(((bf16[32,2,48,128]{3,2,1,0:T(8,128)(2,1)}), bf16[32,2,48,128]{3,2,1,0:T(8,128)(2,1)}, u32[]{:S(2)}, u32[]{:S(2)}) %all-to-all-start.2) | async-done | bytes 786464 | tf_op jit(solution)/shard_map/all_to_all | solution.py:121
  137.6 3.8 %all-to-all-start.3 = ((bf16[32,2,48,128]{3,2,1,0:T(8,128)(2,1)}), bf16[32,2,48,128]{3,2,1,0:T(8,128)(2,1)S(1)}, u32[]{:S(2)}, u32[]{:S(2)}) async-start(bf16[32,2,48,128]{3,2,1,0:T(8,128)(2,1)} %bitcast.8), calls=%async_computation.3 | async-start | bytes 1572864 | tf_op jit(solution)/shard_map/all_to_all | solution.py:121
  141.4 1.2 copy.15
  142.6 13.0 %all-to-all-done.3 = bf16[32,2,48,128]{3,2,1,0:T(8,128)(2,1)S(1)} async-done(((bf16[32,2,48,128]{3,2,1,0:T(8,128)(2,1)}), bf16[32,2,48,128]{3,2,1,0:T(8,128)(2,1)S(1)}, u32[]{:S(2)}, u32[]{:S(2)}) %all-to-all-start.3) | async-done | bytes 786464 | tf_op jit(solution)/shard_map/all_to_all | solution.py:121
  155.7 0.1 copy.14
  155.7 1.3 pad_maximum_fusion
  (1 shorter events, 0.0 us)
Async XLA Ops:
  3.1 36.5 %all-to-all-start.1 = ((bf16[16,2,128,256]{3,2,1,0:T(8,128)(2,1)}), bf16[16,2,128,256]{3,2,1,0:T(8,128)(2,1)S(1)}, u32[]{:S(2)}, u32[]{:S(2)}) async-start(bf16[16,2,128,256]{3,2,1,0:T(8,128)(2,1)} %bitcast.22), calls=%async_computation.1 | async-start | bytes 4194304 | tf_op jit(solution)/shard_map/all_to_all | solution.py:98
  39.6 23.4 %all-to-all-start = ((bf16[16,2,96,256]{3,2,1,0:T(8,128)(2,1)}), bf16[16,2,96,256]{3,2,1,0:T(8,128)(2,1)}, u32[]{:S(2)}, u32[]{:S(2)}) async-start(bf16[16,2,96,256]{3,2,1,0:T(8,128)(2,1)} %bitcast.23), calls=%async_computation | async-start | bytes 3145728 | tf_op jit(solution)/shard_map/all_to_all | solution.py:98
  44.0 53.1 %copy-start = (f32[2,16]{1,0:T(2,128)S(1)}, f32[2,16]{1,0:T(2,128)}, u32[]{:S(2)}) copy-start(f32[2,16]{1,0:T(2,128)} %wave.3) | copy-start | bytes 388
  44.0 53.1 %collective-permute-start.3 = (bf16[16,2,128,256]{3,2,1,0:T(8,128)(2,1)S(1)}, bf16[16,2,128,256]{3,2,1,0:T(8,128)(2,1)}, u32[]{:S(2)}, u32[]{:S(2)}) collective-permute-start(bf16[16,2,128,256]{3,2,1,0:T(8,128)(2,1)S(1)} %all-to-all-done.1.p_own), channel_id=1, source_target_pairs={{0,8},{8,0},{1,9},{9,1},{2,10},{10,2},{3,11},{11,3},{4,12},{12,4},... | collective-permute-start | bytes 6291464 | tf_op jit(solution)/shard_map/ppermute | solution.py:94
  65.4 15.4 %collective-permute-start = (bf16[16,2,48,256]{3,2,1,0:T(8,128)(2,1)}, bf16[16,2,48,256]{3,2,1,0:T(8,128)(2,1)}, u32[]{:S(2)}, u32[]{:S(2)}) collective-permute-start(bf16[16,2,48,256]{3,2,1,0:T(8,128)(2,1)} %get-tuple-element.5.q_own), channel_id=1, source_target_pairs={{0,16},{16,32},{32,48},{48,0},{1,17},{17,33},{33,49},{49,1},{2,18}... | collective-permute-start | bytes 2359304 | tf_op jit(solution)/shard_map/ppermute | solution.py:94
  66.6 15.5 %collective-permute-start.5 = (bf16[16,2,48,256]{3,2,1,0:T(8,128)(2,1)S(1)}, bf16[16,2,48,256]{3,2,1,0:T(8,128)(2,1)}, u32[]{:S(2)}, u32[]{:S(2)}) collective-permute-start(bf16[16,2,48,256]{3,2,1,0:T(8,128)(2,1)S(1)} %get-tuple-element.6.q_own), channel_id=1, source_target_pairs={{0,48},{16,0},{32,16},{48,32},{1,49},{17,1},{33,17},{49,33},{2,50}... | collective-permute-start | bytes 2359304 | tf_op jit(solution)/shard_map/ppermute | solution.py:94
  68.1 29.1 %collective-permute-start.1 = (bf16[16,2,48,256]{3,2,1,0:T(8,128)(2,1)}, bf16[16,2,48,256]{3,2,1,0:T(8,128)(2,1)}, u32[]{:S(2)}, u32[]{:S(2)}) collective-permute-start(bf16[16,2,48,256]{3,2,1,0:T(8,128)(2,1)} %get-tuple-element.5.q_own), channel_id=1, source_target_pairs={{0,48},{16,0},{32,16},{48,32},{1,49},{17,1},{33,17},{49,33},{2,50}... | collective-permute-start | bytes 2359304 | tf_op jit(solution)/shard_map/ppermute | solution.py:94
  80.8 16.4 %collective-permute-start.2 = (bf16[16,2,48,256]{3,2,1,0:T(8,128)(2,1)}, bf16[16,2,48,256]{3,2,1,0:T(8,128)(2,1)}, u32[]{:S(2)}, u32[]{:S(2)}) collective-permute-start(bf16[16,2,48,256]{3,2,1,0:T(8,128)(2,1)} %collective-permute-done.q_left), channel_id=1, source_target_pairs={{0,16},{16,32},{32,48},{48,0},{1,17},{17,33},{33,49},{49,1},{2,18}... | collective-permute-start | bytes 2359304 | tf_op jit(solution)/shard_map/ppermute | solution.py:94
  80.9 42.4 %collective-permute-start.4 = (bf16[16,2,48,256]{3,2,1,0:T(8,128)(2,1)S(1)}, bf16[16,2,48,256]{3,2,1,0:T(8,128)(2,1)}, u32[]{:S(2)}, u32[]{:S(2)}) collective-permute-start(bf16[16,2,48,256]{3,2,1,0:T(8,128)(2,1)S(1)} %get-tuple-element.6.q_own), channel_id=1, source_target_pairs={{0,16},{16,32},{32,48},{48,0},{1,17},{17,33},{33,49},{49,1},{2,18}... | collective-permute-start | bytes 2359304 | tf_op jit(solution)/shard_map/ppermute | solution.py:94
  82.1 41.2 %collective-permute-start.6 = (bf16[16,2,48,256]{3,2,1,0:T(8,128)(2,1)}, bf16[16,2,48,256]{3,2,1,0:T(8,128)(2,1)}, u32[]{:S(2)}, u32[]{:S(2)}) collective-permute-start(bf16[16,2,48,256]{3,2,1,0:T(8,128)(2,1)} %collective-permute-done.5.q_right), channel_id=1, source_target_pairs={{0,48},{16,0},{32,16},{48,32},{1,49},{17,1},{33,17},{49,33},{2,50}... | collective-permute-start | bytes 2359304 | tf_op jit(solution)/shard_map/ppermute | solution.py:94
  105.0 32.6 %all-to-all-start.2 = ((bf16[32,2,48,128]{3,2,1,0:T(8,128)(2,1)}), bf16[32,2,48,128]{3,2,1,0:T(8,128)(2,1)}, u32[]{:S(2)}, u32[]{:S(2)}) async-start(bf16[32,2,48,128]{3,2,1,0:T(8,128)(2,1)} %bitcast.5), calls=%async_computation.2 | async-start | bytes 1572864 | tf_op jit(solution)/shard_map/all_to_all | solution.py:121
  137.6 18.1 %all-to-all-start.3 = ((bf16[32,2,48,128]{3,2,1,0:T(8,128)(2,1)}), bf16[32,2,48,128]{3,2,1,0:T(8,128)(2,1)S(1)}, u32[]{:S(2)}, u32[]{:S(2)}) async-start(bf16[32,2,48,128]{3,2,1,0:T(8,128)(2,1)} %bitcast.8), calls=%async_computation.3 | async-start | bytes 1572864 | tf_op jit(solution)/shard_map/all_to_all | solution.py:121

commit v2 on v0

v2 whole, which is shorter than its diff:
```python
import functools

import jax
import jax.numpy as jnp
from jax import lax
from jax.experimental import pallas as pl
from jax.experimental.pallas import tpu as pltpu
from jax.sharding import Mesh
from jax.sharding import PartitionSpec as P

FREQUENCY = ("yh", "yl", "z")
PLACES = ("yh", "yl", "z", "c")
ORDER = 10**11


def product_kernel(steps, place, wave, *refs):
    count = 2 * len(steps)
    pieces, (p_own, p_other), out = refs[:count], refs[count : count + 2], refs[-1]
    groups = p_own.shape[0] // 2
    shots = p_own.shape[2]
    x, core, frequency = place[0], place[1], place[2]
    w_real, w_imag = wave[0, frequency], wave[1, frequency]

    def rows_of(piece, half):
        return jnp.concatenate(
            [
                piece[half * groups + j].reshape(-1, piece.shape[3])
                for j in range(groups)
            ],
            axis=1,
        )

    for distance, p_ref in enumerate((p_own, p_other)):
        to_core = lax.rem(core + distance, 2)
        for p_half in range(2):
            right_factor = rows_of(p_ref, p_half)
            left_factor = jnp.concatenate(
                [rows_of(piece, half) for piece in pieces for half in range(2)], axis=0
            )
            terms = lax.dot_general(
                left_factor,
                right_factor,
                (((1,), (1,)), ((), ())),
                preferred_element_type=jnp.float32,
            )
            at = 0
            for k, piece in enumerate(pieces):
                rows = piece.shape[2]
                to = lax.rem(x + steps[k // 2], 4)
                low = 0 if k % 2 == 0 else pieces[k - 1].shape[2]
                for half in range(2):
                    real, imag = terms[at : at + rows], terms[at + rows : at + 2 * rows]
                    at += 2 * rows
                    s_real = real[:, :shots] - imag[:, shots:]
                    s_imag = real[:, shots:] + imag[:, :shots]
                    out[p_half, half, to, to_core, 0, low : low + rows] = (
                        w_real * s_real - w_imag * s_imag
                    ).astype(out.dtype)
                    out[p_half, half, to, to_core, 1, low : low + rows] = (
                        w_real * s_imag + w_imag * s_real
                    ).astype(out.dtype)


def product(place, wavelet, steps, pieces, p_own, p_other, earlier=None):
    sources, _, _, depth = pieces[0].shape
    rows = pieces[0].shape[2] + pieces[1].shape[2]
    shots = p_own.shape[2]
    vmem = pl.BlockSpec(memory_space=pltpu.VMEM)
    smem = pl.BlockSpec(memory_space=pltpu.SMEM)
    operands = [place, wavelet, *pieces, p_own, p_other]
    specs = [smem, smem] + [vmem] * (len(pieces) + 2)
    kernel = functools.partial(product_kernel, steps)
    aliases = {}
    if earlier is not None:
        aliases = {len(operands): 0}
        operands.append(earlier)
        specs.append(vmem)
    flops = 2 * (2 * rows * len(steps) * 2) * (4 * 2 * shots) * (sources // 2 * depth)
    return pl.pallas_call(
        kernel,
        out_shape=jax.ShapeDtypeStruct((2, 2, 4, 2, 2, rows, shots), jnp.bfloat16),
        in_specs=specs,
        out_specs=vmem,
        input_output_aliases=aliases,
        compiler_params=pltpu.CompilerParams(vmem_limit_bytes=32 * 2**20),
        cost_estimate=pl.CostEstimate(flops=flops, bytes_accessed=2**20, transcendentals=0),
    )(*operands)


def ordered_kernel(source, out):
    pass


def ordered(value):
    return pl.pallas_call(
        ordered_kernel,
        out_shape=jax.ShapeDtypeStruct(value.shape, value.dtype),
        in_specs=[pl.BlockSpec(memory_space=pl.ANY)],
        out_specs=pl.BlockSpec(memory_space=pl.ANY),
        input_output_aliases={0: 0},
        cost_estimate=pl.CostEstimate(flops=ORDER, bytes_accessed=0, transcendentals=0),
    )(value)


def shift(value, axis, size, step):
    return lax.ppermute(value, axis, [(i, (i + step) % size) for i in range(size)])


def by_frequency(value):
    return lax.all_to_all(value, FREQUENCY, 0, 0, tiled=True)


def on_device(shot_spec, recv_spec, wavelet):
    place = jnp.stack(
        [lax.axis_index("x"), lax.axis_index("c"), lax.axis_index(FREQUENCY)]
    ).astype(jnp.int32)
    half = recv_spec.shape[2] // 2
    recv = by_frequency(recv_spec.swapaxes(0, 1))
    recv, shot_spec = lax.optimization_barrier((recv, shot_spec))
    first, second = recv[:, :, :half], recv[:, :, half:]
    first_left, first_right = shift(first, "x", 4, 1), shift(first, "x", 4, -1)
    first_left = ordered(first_left)
    first_far = shift(first_left, "x", 4, 1)
    second_left, second_right = shift(second, "x", 4, 1), shift(second, "x", 4, -1)
    second_right = ordered(second_right)
    second_far = shift(second_right, "x", 4, -1)
    shots = by_frequency(shot_spec.swapaxes(0, 1))
    other = shift(shots, "c", 2, 1)
    near = (first, second, first_left, second_left, first_right, second_right)
    out = product(place, wavelet, (0, 3, 1), near, shots, other)
    out = product(place, wavelet, (2,), (first_far, second_far), shots, other, out)
    out = out.reshape((-1,) + out.shape[4:])
    out = lax.all_to_all(out, PLACES, 0, 0, tiled=True)
    out = out.reshape((out.shape[0] // 2, 2) + out.shape[1:])
    out = out.transpose(2, 0, 1, 3, 4)
    out = out.reshape(out.shape[:2] + (-1, out.shape[-1]))
    return out.swapaxes(2, 3)


def solution(mesh):
    devices = mesh.devices.reshape(2, 4, 2, 2, 4)
    wide = Mesh(devices, ("yh", "x", "c", "yl", "z"))
    spec = P(None, None, ("yh", "x", "c"), ("yl", "z"))
    return jax.shard_map(
        on_device, mesh=wide, in_specs=(spec, spec, P()), out_specs=spec, check_vma=False
    )
```

time: 384 us -> 127 us (0.33)
  waiting for transfers between devices: 285 us -> 34.4 us
  blocking collectives: 0 us -> 57.8 us
  matrix products: 52.8 us -> 0 us
  starting transfers between devices: 0.04 us -> 15.1 us
  between operations: 13.4 us -> 0.06 us
  other arithmetic: 12.9 us -> 0.08 us
  Pallas kernels: 0 us -> 11.6 us
  local copies, waits for them, and re-layouts: 19.2 us -> 7.67 us
    all_gather x1 -> x0, waiting for transfers between devices: 155 us -> none  [on_device(): lax.all_gather(recv_spec, 'shot', axis=2, tiled=True)]
    reduce_scatter x1 -> x0, waiting for transfers between devices: 129 us -> none  [on_device(): lax.psum_scatter(terms.astype(jnp.bfloat16), 'surf', scatter_dimension=3,...]
    all_to_all x0 -> x2, blocking collectives: none -> 57.8 us  [the longest x1 29.9 us: by_frequency(): return lax.all_to_all(value, FREQUENCY, 0, 0, tiled=True)]
    dot_general x4 -> x0, matrix products: 52.8 us -> none  [the longest x1 13.5 us: complex_product(): jnp.einsum(product_form, left_factor[0], right_factor[0], preferred_eleme...]
    another operation x2 -> x0, local copies, waits for them, and re-layouts: 18.5 us -> none  [the longest x1 16.8 us: complex_product(): return jnp.stack([real_term, imaginary_term])]
    ppermute x0 -> x7, waiting for transfers between devices: none -> 18 us  [shift(): lax.ppermute(value, axis, [(i, (i + step) % size) for i in range(size)])]
    all_to_all x0 -> x1, waiting for transfers between devices: none -> 16.4 us  [by_frequency(): return lax.all_to_all(value, FREQUENCY, 0, 0, tiled=True)]
    pallas_call x0 -> x4, Pallas kernels: none -> 11.6 us  [the longest x2 11.6 us: product(): pl.pallas_call(kernel, out_shape=jax.ShapeDtypeStruct((2, 2, 4, 2, 2, row...]
  transfers between devices with their start and end apart: 2 -> 8, of which waited for: 2 -> 4; matrix products, arithmetic and copies ran while one was open for 0% -> 1% of each run, Pallas kernels for 0% -> 6%
where the time goes in v2:
time: 127 us
  blocking collectives  57.8 us (46%)
  waiting for transfers between devices  34.4 us (27%)
  starting transfers between devices  15.1 us (12%)
  Pallas kernels  11.6 us (9%)
  local copies, waits for them, and re-layouts  7.67 us (6%)
    all_to_all x1, blocking collectives, by_frequency(): return lax.all_to_all(value, FREQUENCY, 0, 0, tiled=True)  29.9 us
    all_to_all x1, blocking collectives, on_device(): out = lax.all_to_all(out, PLACES, 0, 0, tiled=True)  27.9 us
    ppermute x7, waiting for transfers between devices, shift(): lax.ppermute(value, axis, [(i, (i + step) % size) for i in range(size)])  18 us
    all_to_all x1, waiting for transfers between devices, by_frequency(): return lax.all_to_all(value, FREQUENCY, 0, 0, tiled=True)  16.4 us
    pallas_call x2, Pallas kernels, product(): pl.pallas_call(kernel, out_shape=jax.ShapeDtypeStruct((2, 2, 4, 2, 2, row...  11.6 us
    ppermute x7, starting transfers between devices, shift(): lax.ppermute(value, axis, [(i, (i + step) % size) for i in range(size)])  11.3 us
    all_to_all x1, starting transfers between devices, by_frequency(): return lax.all_to_all(value, FREQUENCY, 0, 0, tiled=True)  3.77 us
    unnamed x9, local copies, waits for them, and re-layouts  3.54 us
  transfers between devices with their start and end apart: 8, of which 4 were waited for; matrix products, arithmetic and copies ran while one was open for 1% of the time, Pallas kernels for 6%

profile of v2, /device:TPU:1, one launch (start us, length us, event | category | flops | bytes accessed | tf_op | source)
XLA Modules:
  0.0 126.7 jit_solution(330394302476271571)
XLA Ops:
  0.0 1.5 %copy.13 = bf16[2,16,96,256]{3,2,0,1:T(8,128)(2,1)S(1)} copy(bf16[2,16,96,256]{3,2,1,0:T(8,128)(2,1)} %param.4) | data formatting | bytes 3145728 | tf_op args[1]
  1.5 29.9 %all_to_all.15 = bf16[16,2,96,256]{3,2,1,0:T(8,128)(2,1)S(1)} all-to-all(bf16[16,2,96,256]{3,2,1,0:T(8,128)(2,1)S(1)} %bitcast.19), channel_id=1, replica_groups=mesh['yh'=2,'x'=4,'c'=2,'yl'=2,'z'=4] {'yh','yl','z'}, dimensions={0} | all-to-all | bytes 3145728 | tf_op jit(solution)/shard_map/all_to_all | solution.py:110
  31.4 1.3 %fusion = (bf16[16,2,48,256]{3,2,1,0:T(8,128)(2,1)}, bf16[16,2,48,256]{3,2,1,0:T(8,128)(2,1)}) fusion(bf16[16,2,96,256]{3,2,1,0:T(8,128)(2,1)S(1)} %all_to_all.15), kind=kLoop, calls=%fused_computation.3 | loop fusion | bytes 3145728 | tf_op jit(solution)/shard_map/slice | solution.py:120
  32.8 1.2 collective-permute-start
  34.0 1.5 %collective-permute-start.2 = (bf16[16,2,48,256]{3,2,1,0:T(8,128)(2,1)}, bf16[16,2,48,256]{3,2,1,0:T(8,128)(2,1)}, u32[]{:S(2)}, u32[]{:S(2)}) collective-permute-start(bf16[16,2,48,256]{3,2,1,0:T(8,128)(2,1)} %get-tuple-element.9.refs_1_), channel_id=1, source_target_pairs={{0,48},{16,0},{32,16},{48,32},{1,49},{17,1},{33,17},{49,33},{2,50}... | collective-permute-start | bytes 2359304 | tf_op jit(solution)/shard_map/ppermute | solution.py:106
  35.4 0.0 collective-permute-start.5
  35.4 2.7 %collective-permute-start.6 = (bf16[16,2,48,256]{3,2,1,0:T(8,128)(2,1)}, bf16[16,2,48,256]{3,2,1,0:T(8,128)(2,1)}, u32[]{:S(2)}, u32[]{:S(2)}) collective-permute-start(bf16[16,2,48,256]{3,2,1,0:T(8,128)(2,1)} %get-tuple-element.10.refs_0_), channel_id=1, source_target_pairs={{0,48},{16,0},{32,16},{48,32},{1,49},{17,1},{33,17},{49,33},{2,50}... | collective-permute-start | bytes 2359304 | tf_op jit(solution)/shard_map/ppermute | solution.py:106
  38.1 0.0 copy-done.3
  38.1 1.5 %copy.12 = bf16[2,16,128,256]{3,2,0,1:T(8,128)(2,1)} copy(bf16[2,16,128,256]{3,2,1,0:T(8,128)(2,1)S(1)} %copy-done.3) | data formatting | bytes 4194304 | tf_op jit(solution)/shard_map/optimization_barrier | solution.py:119
  39.6 3.8 %all-to-all-start.1 = ((bf16[16,2,128,256]{3,2,1,0:T(8,128)(2,1)}), bf16[16,2,128,256]{3,2,1,0:T(8,128)(2,1)S(1)}, u32[]{:S(2)}, u32[]{:S(2)}) async-start(bf16[16,2,128,256]{3,2,1,0:T(8,128)(2,1)} %bitcast.17), calls=%async_computation.1 | async-start | bytes 4194304 | tf_op jit(solution)/shard_map/all_to_all | solution.py:110
  43.4 7.8 %collective-permute-done.source = bf16[16,2,48,256]{3,2,1,0:T(8,128)(2,1)S(1)} collective-permute-done((bf16[16,2,48,256]{3,2,1,0:T(8,128)(2,1)}, bf16[16,2,48,256]{3,2,1,0:T(8,128)(2,1)S(1)}, u32[]{:S(2)}, u32[]{:S(2)}) %collective-permute-start) | collective-permute-done | bytes 786464 | tf_op jit(solution)/shard_map/ppermute | solution.py:106
  51.2 0.0 copy-start.1
  51.2 0.9 copy-done.1
  52.1 0.0 copy-start
  52.1 0.1 collective-permute-start.1
  52.2 16.4 %all-to-all-done.1.refs_6_.refs_2_ = bf16[16,2,128,256]{3,2,1,0:T(8,128)(2,1)S(1)} async-done(((bf16[16,2,128,256]{3,2,1,0:T(8,128)(2,1)}), bf16[16,2,128,256]{3,2,1,0:T(8,128)(2,1)S(1)}, u32[]{:S(2)}, u32[]{:S(2)}) %all-to-all-start.1) | async-done | bytes 2097184 | tf_op jit(solution)/shard_map/all_to_all | solution.py:110
  68.5 5.8 %collective-permute-start.4 = (bf16[16,2,128,256]{3,2,1,0:T(8,128)(2,1)S(1)}, bf16[16,2,128,256]{3,2,1,0:T(8,128)(2,1)}, u32[]{:S(2)}, u32[]{:S(2)}) collective-permute-start(bf16[16,2,128,256]{3,2,1,0:T(8,128)(2,1)S(1)} %all-to-all-done.1.refs_6_.refs_2_), channel_id=1, source_target_pairs={{0,8},{8,0},{1,9},{9,1},{2,10},{10,2},{3,11},{11,3},{4,12},{12,4},... | collective-permute-start | bytes 6291464 | tf_op jit(solution)/shard_map/ppermute | solution.py:106
  74.3 0.0 collective-permute-done.2.source
  74.3 0.1 collective-permute-start.3
  74.4 0.1 pad_add_fusion.place
  74.5 0.0 collective-permute-done.5.refs_3_
  74.5 0.0 collective-permute-done.6.refs_4_
  74.5 3.8 %collective-permute-done.4.refs_7_.refs_3_ = bf16[16,2,128,256]{3,2,1,0:T(8,128)(2,1)} collective-permute-done((bf16[16,2,128,256]{3,2,1,0:T(8,128)(2,1)S(1)}, bf16[16,2,128,256]{3,2,1,0:T(8,128)(2,1)}, u32[]{:S(2)}, u32[]{:S(2)}) %collective-permute-start.4) | collective-permute-done | bytes 2097184 | tf_op jit(solution)/shard_map/ppermute | solution.py:106
  78.3 0.0 copy-done
  78.3 0.0 copy-start.2
  78.3 1.1 copy-done.2
  79.4 8.0 %shard_map.39.refs_4_ = bf16[2,2,4,2,2,96,128]{6,5,4,3,2,1,0:T(8,128)(2,1)S(1)} custom-call(s32[3]{0:T(128)S(1)} %pad_add_fusion.place, f32[2,16]{1,0:T(2,128)S(1)} %copy-done, bf16[16,2,48,256]{3,2,1,0:T(8,128)(2,1)} %get-tuple-element.10.refs_0_, bf16[16,2,48,256]{3,2,1,0:T(8,128)(2,1)} %get-tuple-element.9.refs_1_, ...), custom_call_target="tpu_custom_call" | custom-call | flops 4831838208 | bytes 1048576 | tf_op jit(solution)/shard_map/pallas_call | solution.py:79
  87.4 0.0 collective-permute-done.1.refs_0_
  87.4 6.4 %collective-permute-done.3.refs_1_ = bf16[16,2,48,256]{3,2,1,0:T(8,128)(2,1)} collective-permute-done((bf16[16,2,48,256]{3,2,1,0:T(8,128)(2,1)}, bf16[16,2,48,256]{3,2,1,0:T(8,128)(2,1)}, u32[]{:S(2)}, u32[]{:S(2)}) %collective-permute-start.3) | collective-permute-done | bytes 786464 | tf_op jit(solution)/shard_map/ppermute | solution.py:106
  93.8 3.7 %shard_map.40 = bf16[2,2,4,2,2,96,128]{6,5,4,3,2,1,0:T(8,128)(2,1)S(1)} custom-call(s32[3]{0:T(128)S(1)} %pad_add_fusion.place, f32[2,16]{1,0:T(2,128)S(1)} %copy-done, bf16[16,2,48,256]{3,2,1,0:T(8,128)(2,1)S(1)} %collective-permute-done.1.refs_0_, bf16[16,2,48,256]{3,2,1,0:T(8,128)(2,1)} %collective-permute-done.3.refs_1_, ...), custom_call_target="tpu_custom_call", output_to_operand_aliasing={{}: (6, {})} | custom-call | flops 1610612736 | bytes 1048576 | tf_op jit(solution)/shard_map/pallas_call | solution.py:79
  97.5 27.9 %all_to_all.16 = bf16[32,2,96,128]{3,2,1,0:T(8,128)(2,1)S(1)} all-to-all(bf16[32,2,96,128]{3,2,1,0:T(8,128)(2,1)S(1)} %bitcast.16), channel_id=1, replica_groups=mesh['yh'=2,'x'=4,'c'=2,'yl'=2,'z'=4] {'yh','yl','z','c'}, dimensions={0} | all-to-all | bytes 3145728 | tf_op jit(solution)/shard_map/all_to_all | solution.py:133
  125.4 1.3 %copy.9 = bf16[16,2,2,96,128]{4,3,1,0,2:T(8,128)(2,1)} copy(bf16[16,2,2,96,128]{4,3,2,1,0:T(8,128)(2,1)S(1)} %bitcast.18) | data formatting | bytes 3145728 | tf_op jit(solution)/shard_map/reshape | solution.py:134
  (3 shorter events, 0.0 us)
Async XLA Ops:
  31.4 6.7 %copy-start.3 = (bf16[2,16,128,256]{3,2,1,0:T(8,128)(2,1)S(1)}, bf16[2,16,128,256]{3,2,1,0:T(8,128)(2,1)}, u32[]{:S(2)}) copy-start(bf16[2,16,128,256]{3,2,1,0:T(8,128)(2,1)} %param.3) | copy-start | bytes 6291460
  32.8 18.4 %collective-permute-start = (bf16[16,2,48,256]{3,2,1,0:T(8,128)(2,1)}, bf16[16,2,48,256]{3,2,1,0:T(8,128)(2,1)S(1)}, u32[]{:S(2)}, u32[]{:S(2)}) collective-permute-start(bf16[16,2,48,256]{3,2,1,0:T(8,128)(2,1)} %get-tuple-element.10.refs_0_), channel_id=1, source_target_pairs={{0,16},{16,32},{32,48},{48,0},{1,17},{17,33},{33,49},{49,1},{2,18}... | collective-permute-start | bytes 2359304 | tf_op jit(solution)/shard_map/ppermute | solution.py:106
  34.0 40.4 %collective-permute-start.2 = (bf16[16,2,48,256]{3,2,1,0:T(8,128)(2,1)}, bf16[16,2,48,256]{3,2,1,0:T(8,128)(2,1)}, u32[]{:S(2)}, u32[]{:S(2)}) collective-permute-start(bf16[16,2,48,256]{3,2,1,0:T(8,128)(2,1)} %get-tuple-element.9.refs_1_), channel_id=1, source_target_pairs={{0,48},{16,0},{32,16},{48,32},{1,49},{17,1},{33,17},{49,33},{2,50}... | collective-permute-start | bytes 2359304 | tf_op jit(solution)/shard_map/ppermute | solution.py:106
  35.4 39.1 %collective-permute-start.5 = (bf16[16,2,48,256]{3,2,1,0:T(8,128)(2,1)}, bf16[16,2,48,256]{3,2,1,0:T(8,128)(2,1)}, u32[]{:S(2)}, u32[]{:S(2)}) collective-permute-start(bf16[16,2,48,256]{3,2,1,0:T(8,128)(2,1)} %get-tuple-element.9.refs_1_), channel_id=1, source_target_pairs={{0,16},{16,32},{32,48},{48,0},{1,17},{17,33},{33,49},{49,1},{2,18}... | collective-permute-start | bytes 2359304 | tf_op jit(solution)/shard_map/ppermute | solution.py:106
  35.4 39.1 %collective-permute-start.6 = (bf16[16,2,48,256]{3,2,1,0:T(8,128)(2,1)}, bf16[16,2,48,256]{3,2,1,0:T(8,128)(2,1)}, u32[]{:S(2)}, u32[]{:S(2)}) collective-permute-start(bf16[16,2,48,256]{3,2,1,0:T(8,128)(2,1)} %get-tuple-element.10.refs_0_), channel_id=1, source_target_pairs={{0,48},{16,0},{32,16},{48,32},{1,49},{17,1},{33,17},{49,33},{2,50}... | collective-permute-start | bytes 2359304 | tf_op jit(solution)/shard_map/ppermute | solution.py:106
  39.6 29.0 %all-to-all-start.1 = ((bf16[16,2,128,256]{3,2,1,0:T(8,128)(2,1)}), bf16[16,2,128,256]{3,2,1,0:T(8,128)(2,1)S(1)}, u32[]{:S(2)}, u32[]{:S(2)}) async-start(bf16[16,2,128,256]{3,2,1,0:T(8,128)(2,1)} %bitcast.17), calls=%async_computation.1 | async-start | bytes 4194304 | tf_op jit(solution)/shard_map/all_to_all | solution.py:110
  51.2 0.9 copy-start.1
  52.1 26.2 %copy-start = (f32[2,16]{1,0:T(2,128)S(1)}, f32[2,16]{1,0:T(2,128)}, u32[]{:S(2)}) copy-start(f32[2,16]{1,0:T(2,128)} %wave.3) | copy-start | bytes 388
  52.1 35.3 %collective-permute-start.1 = (bf16[16,2,48,256]{3,2,1,0:T(8,128)(2,1)}, bf16[16,2,48,256]{3,2,1,0:T(8,128)(2,1)S(1)}, u32[]{:S(2)}, u32[]{:S(2)}) collective-permute-start(bf16[16,2,48,256]{3,2,1,0:T(8,128)(2,1)} %shard_map.37.refs_2_), channel_id=1, source_target_pairs={{0,16},{16,32},{32,48},{48,0},{1,17},{17,33},{33,49},{49,1},{2,18}... | collective-permute-start | bytes 2359304 | tf_op jit(solution)/shard_map/ppermute | solution.py:106
  68.5 9.7 %collective-permute-start.4 = (bf16[16,2,128,256]{3,2,1,0:T(8,128)(2,1)S(1)}, bf16[16,2,128,256]{3,2,1,0:T(8,128)(2,1)}, u32[]{:S(2)}, u32[]{:S(2)}) collective-permute-start(bf16[16,2,128,256]{3,2,1,0:T(8,128)(2,1)S(1)} %all-to-all-done.1.refs_6_.refs_2_), channel_id=1, source_target_pairs={{0,8},{8,0},{1,9},{9,1},{2,10},{10,2},{3,11},{11,3},{4,12},{12,4},... | collective-permute-start | bytes 6291464 | tf_op jit(solution)/shard_map/ppermute | solution.py:106
  74.3 19.4 %collective-permute-start.3 = (bf16[16,2,48,256]{3,2,1,0:T(8,128)(2,1)}, bf16[16,2,48,256]{3,2,1,0:T(8,128)(2,1)}, u32[]{:S(2)}, u32[]{:S(2)}) collective-permute-start(bf16[16,2,48,256]{3,2,1,0:T(8,128)(2,1)} %shard_map.38.refs_5_), channel_id=1, source_target_pairs={{0,48},{16,0},{32,16},{48,32},{1,49},{17,1},{33,17},{49,33},{2,50}... | collective-permute-start | bytes 2359304 | tf_op jit(solution)/shard_map/ppermute | solution.py:106
  78.3 1.1 copy-start.2

commit v3 on v2

--- a/solution.py
+++ b/solution.py
@@ -61,7 +61,9 @@
                     ).astype(out.dtype)
 
 
-def product(place, wavelet, steps, pieces, p_own, p_other, earlier=None):
+def product(place, wavelet, blocks, p_own, p_other, earlier=None):
+    steps = tuple(blocks)
+    pieces = [piece for pair in blocks.values() for piece in pair]
     sources, _, _, depth = pieces[0].shape
     rows = pieces[0].shape[2] + pieces[1].shape[2]
     shots = p_own.shape[2]
@@ -118,17 +120,16 @@
     recv = by_frequency(recv_spec.swapaxes(0, 1))
     recv, shot_spec = lax.optimization_barrier((recv, shot_spec))
     first, second = recv[:, :, :half], recv[:, :, half:]
-    first_left, first_right = shift(first, "x", 4, 1), shift(first, "x", 4, -1)
-    first_left = ordered(first_left)
-    first_far = shift(first_left, "x", 4, 1)
-    second_left, second_right = shift(second, "x", 4, 1), shift(second, "x", 4, -1)
-    second_right = ordered(second_right)
-    second_far = shift(second_right, "x", 4, -1)
+    first_left, second_right = shift(first, "x", 4, 1), shift(second, "x", 4, -1)
+    first_left, second_right = ordered(first_left), ordered(second_right)
+    first_far, second_far = shift(first_left, "x", 4, 1), shift(second_right, "x", 4, -1)
+    first_right, second_left = ordered(shift(first, "x", 4, -1)), ordered(shift(second, "x", 4, 1))
     shots = by_frequency(shot_spec.swapaxes(0, 1))
     other = shift(shots, "c", 2, 1)
-    near = (first, second, first_left, second_left, first_right, second_right)
-    out = product(place, wavelet, (0, 3, 1), near, shots, other)
-    out = product(place, wavelet, (2,), (first_far, second_far), shots, other, out)
+    near = {0: (first, second), 3: (first_left, second_left), 1: (first_right, second_right)}
+    far = {2: (first_far, second_far)}
+    out = product(place, wavelet, near, shots, other)
+    out = product(place, wavelet, far, shots, other, out)
     out = out.reshape((-1,) + out.shape[4:])
     out = lax.all_to_all(out, PLACES, 0, 0, tiled=True)
     out = out.reshape((out.shape[0] // 2, 2) + out.shape[1:])

time: 127 us -> 120 us (0.945)
  waiting for transfers between devices: 34.4 us -> 25.7 us
  starting transfers between devices: 15.1 us -> 18.2 us
    all_to_all x1, waiting for transfers between devices: 16.4 us -> 1.2 us  [by_frequency(): return lax.all_to_all(value, FREQUENCY, 0, 0, tiled=True)]
    ppermute x7, waiting for transfers between devices: 18 us -> 24.5 us  [shift(): lax.ppermute(value, axis, [(i, (i + step) % size) for i in range(size)])]
    ppermute x7, starting transfers between devices: 11.3 us -> 13.7 us  [shift(): lax.ppermute(value, axis, [(i, (i + step) % size) for i in range(size)])]
  transfers between devices with their start and end apart: 8 -> 8, of which waited for: 4 -> 4; matrix products, arithmetic and copies ran while one was open for 1% -> 1% of each run, Pallas kernels for 6% -> 7%
where the time goes in v3:
time: 120 us
  blocking collectives  57.6 us (48%)
  waiting for transfers between devices  25.7 us (21%)
  starting transfers between devices  18.2 us (15%)
  Pallas kernels  11.9 us (10%)
  local copies, waits for them, and re-layouts  6.54 us (5%)
    all_to_all x1, blocking collectives, by_frequency(): return lax.all_to_all(value, FREQUENCY, 0, 0, tiled=True)  29.9 us
    all_to_all x1, blocking collectives, on_device(): out = lax.all_to_all(out, PLACES, 0, 0, tiled=True)  27.7 us
    ppermute x7, waiting for transfers between devices, shift(): lax.ppermute(value, axis, [(i, (i + step) % size) for i in range(size)])  24.5 us
    ppermute x7, starting transfers between devices, shift(): lax.ppermute(value, axis, [(i, (i + step) % size) for i in range(size)])  13.7 us
    pallas_call x2, Pallas kernels, product(): pl.pallas_call(kernel, out_shape=jax.ShapeDtypeStruct((2, 2, 4, 2, 2, row...  11.9 us
    all_to_all x1, starting transfers between devices, by_frequency(): return lax.all_to_all(value, FREQUENCY, 0, 0, tiled=True)  4.44 us
    unnamed x9, local copies, waits for them, and re-layouts  2.44 us
  transfers between devices with their start and end apart: 8, of which 4 were waited for; matrix products, arithmetic and copies ran while one was open for 1% of the time, Pallas kernels for 7%

profile of v3, /device:TPU:1, one launch (start us, length us, event | category | flops | bytes accessed | tf_op | source)
XLA Modules:
  0.0 120.0 jit_solution(2947269443508652752)
XLA Ops:
  0.0 1.5 %copy.15 = bf16[2,16,96,256]{3,2,0,1:T(8,128)(2,1)S(1)} copy(bf16[2,16,96,256]{3,2,1,0:T(8,128)(2,1)} %param.4) | data formatting | bytes 3145728 | tf_op args[1]
  1.5 29.9 %all_to_all.15 = bf16[16,2,96,256]{3,2,1,0:T(8,128)(2,1)S(1)} all-to-all(bf16[16,2,96,256]{3,2,1,0:T(8,128)(2,1)S(1)} %bitcast.18), channel_id=1, replica_groups=mesh['yh'=2,'x'=4,'c'=2,'yl'=2,'z'=4] {'yh','yl','z'}, dimensions={0} | all-to-all | bytes 3145728 | tf_op jit(solution)/shard_map/all_to_all | solution.py:112
  31.4 0.0 copy-start.3
  31.4 1.3 %fusion = (bf16[16,2,48,256]{3,2,1,0:T(8,128)(2,1)}, bf16[16,2,48,256]{3,2,1,0:T(8,128)(2,1)}) fusion(bf16[16,2,96,256]{3,2,1,0:T(8,128)(2,1)S(1)} %all_to_all.15), kind=kLoop, calls=%fused_computation.3 | loop fusion | bytes 3145728 | tf_op jit(solution)/shard_map/slice | solution.py:122
  32.8 1.2 %collective-permute-start = (bf16[16,2,48,256]{3,2,1,0:T(8,128)(2,1)}, bf16[16,2,48,256]{3,2,1,0:T(8,128)(2,1)S(1)}, u32[]{:S(2)}, u32[]{:S(2)}) collective-permute-start(bf16[16,2,48,256]{3,2,1,0:T(8,128)(2,1)} %get-tuple-element.10.refs_0_), channel_id=1, source_target_pairs={{0,16},{16,32},{32,48},{48,0},{1,17},{17,33},{33,49},{49,1},{2,18}... | collective-permute-start | bytes 2359304 | tf_op jit(solution)/shard_map/ppermute | solution.py:108
  34.0 0.1 pad_add_fusion.place
  34.0 1.5 %collective-permute-start.2 = (bf16[16,2,48,256]{3,2,1,0:T(8,128)(2,1)}, bf16[16,2,48,256]{3,2,1,0:T(8,128)(2,1)}, u32[]{:S(2)}, u32[]{:S(2)}) collective-permute-start(bf16[16,2,48,256]{3,2,1,0:T(8,128)(2,1)} %get-tuple-element.9.refs_1_), channel_id=1, source_target_pairs={{0,48},{16,0},{32,16},{48,32},{1,49},{17,1},{33,17},{49,33},{2,50}... | collective-permute-start | bytes 2359304 | tf_op jit(solution)/shard_map/ppermute | solution.py:108
  35.5 0.0 collective-permute-start.5
  35.5 2.7 %collective-permute-start.6 = (bf16[16,2,48,256]{3,2,1,0:T(8,128)(2,1)}, bf16[16,2,48,256]{3,2,1,0:T(8,128)(2,1)}, u32[]{:S(2)}, u32[]{:S(2)}) collective-permute-start(bf16[16,2,48,256]{3,2,1,0:T(8,128)(2,1)} %get-tuple-element.10.refs_0_), channel_id=1, source_target_pairs={{0,48},{16,0},{32,16},{48,32},{1,49},{17,1},{33,17},{49,33},{2,50}... | collective-permute-start | bytes 2359304 | tf_op jit(solution)/shard_map/ppermute | solution.py:108
  38.2 0.0 copy-done.3
  38.2 1.4 %copy.14 = bf16[2,16,128,256]{3,2,0,1:T(8,128)(2,1)} copy(bf16[2,16,128,256]{3,2,1,0:T(8,128)(2,1)S(1)} %copy-done.3) | data formatting | bytes 4194304 | tf_op jit(solution)/shard_map/optimization_barrier | solution.py:121
  39.6 4.4 %all-to-all-start.1 = ((bf16[16,2,128,256]{3,2,1,0:T(8,128)(2,1)}), bf16[16,2,128,256]{3,2,1,0:T(8,128)(2,1)}, u32[]{:S(2)}, u32[]{:S(2)}) async-start(bf16[16,2,128,256]{3,2,1,0:T(8,128)(2,1)} %bitcast.14), calls=%async_computation.1 | async-start | bytes 4194304 | tf_op jit(solution)/shard_map/all_to_all | solution.py:112
  44.1 7.1 %collective-permute-done.source = bf16[16,2,48,256]{3,2,1,0:T(8,128)(2,1)S(1)} collective-permute-done((bf16[16,2,48,256]{3,2,1,0:T(8,128)(2,1)}, bf16[16,2,48,256]{3,2,1,0:T(8,128)(2,1)S(1)}, u32[]{:S(2)}, u32[]{:S(2)}) %collective-permute-start) | collective-permute-done | bytes 786464 | tf_op jit(solution)/shard_map/ppermute | solution.py:108
  51.2 0.0 copy-start.1
  51.2 0.9 copy-done.1
  52.1 0.1 collective-permute-start.1
  52.2 0.0 collective-permute-done.2.source
  52.2 2.6 %collective-permute-start.3 = (bf16[16,2,48,256]{3,2,1,0:T(8,128)(2,1)}, bf16[16,2,48,256]{3,2,1,0:T(8,128)(2,1)}, u32[]{:S(2)}, u32[]{:S(2)}) collective-permute-start(bf16[16,2,48,256]{3,2,1,0:T(8,128)(2,1)} %shard_map.38.refs_5_), channel_id=1, source_target_pairs={{0,48},{16,0},{32,16},{48,32},{1,49},{17,1},{33,17},{49,33},{2,50}... | collective-permute-start | bytes 2359304 | tf_op jit(solution)/shard_map/ppermute | solution.py:108
  54.8 13.4 %collective-permute-done.5.source = bf16[16,2,48,256]{3,2,1,0:T(8,128)(2,1)} collective-permute-done((bf16[16,2,48,256]{3,2,1,0:T(8,128)(2,1)}, bf16[16,2,48,256]{3,2,1,0:T(8,128)(2,1)}, u32[]{:S(2)}, u32[]{:S(2)}) %collective-permute-start.5) | collective-permute-done | bytes 786464 | tf_op jit(solution)/shard_map/ppermute | solution.py:108
  68.1 0.0 copy-start
  68.2 1.2 %all-to-all-done.1.refs_6_.refs_2_ = bf16[16,2,128,256]{3,2,1,0:T(8,128)(2,1)} async-done(((bf16[16,2,128,256]{3,2,1,0:T(8,128)(2,1)}), bf16[16,2,128,256]{3,2,1,0:T(8,128)(2,1)}, u32[]{:S(2)}, u32[]{:S(2)}) %all-to-all-start.1) | async-done | bytes 2097184 | tf_op jit(solution)/shard_map/all_to_all | solution.py:112
  69.4 5.7 %collective-permute-start.4 = (bf16[16,2,128,256]{3,2,1,0:T(8,128)(2,1)}, bf16[16,2,128,256]{3,2,1,0:T(8,128)(2,1)S(1)}, u32[]{:S(2)}, u32[]{:S(2)}) collective-permute-start(bf16[16,2,128,256]{3,2,1,0:T(8,128)(2,1)} %all-to-all-done.1.refs_6_.refs_2_), channel_id=1, source_target_pairs={{0,8},{8,0},{1,9},{9,1},{2,10},{10,2},{3,11},{11,3},{4,12},{12,4},... | collective-permute-start | bytes 6291464 | tf_op jit(solution)/shard_map/ppermute | solution.py:108
  75.0 0.0 collective-permute-done.6.source
  75.1 4.0 %collective-permute-done.4.refs_7_.refs_3_ = bf16[16,2,128,256]{3,2,1,0:T(8,128)(2,1)S(1)} collective-permute-done((bf16[16,2,128,256]{3,2,1,0:T(8,128)(2,1)}, bf16[16,2,128,256]{3,2,1,0:T(8,128)(2,1)S(1)}, u32[]{:S(2)}, u32[]{:S(2)}) %collective-permute-start.4) | collective-permute-done | bytes 2097184 | tf_op jit(solution)/shard_map/ppermute | solution.py:108
  79.0 0.0 copy-done
  79.0 0.0 copy-done.2
  79.1 8.0 %shard_map.41.refs_4_ = bf16[2,2,4,2,2,96,128]{6,5,4,3,2,1,0:T(8,128)(2,1)S(1)} custom-call(s32[3]{0:T(128)S(1)} %pad_add_fusion.place, f32[2,16]{1,0:T(2,128)S(1)} %copy-done, bf16[16,2,48,256]{3,2,1,0:T(8,128)(2,1)} %get-tuple-element.10.refs_0_, bf16[16,2,48,256]{3,2,1,0:T(8,128)(2,1)} %get-tuple-element.9.refs_1_, ...), custom_call_target="tpu_custom_call" | custom-call | flops 4831838208 | bytes 1048576 | tf_op jit(solution)/shard_map/pallas_call | solution.py:81
  87.0 0.0 collective-permute-done.1.refs_0_
  87.0 0.0 collective-permute-done.3.refs_1_
  87.0 3.9 %shard_map.42 = bf16[2,2,4,2,2,96,128]{6,5,4,3,2,1,0:T(8,128)(2,1)S(1)} custom-call(s32[3]{0:T(128)S(1)} %pad_add_fusion.place, f32[2,16]{1,0:T(2,128)S(1)} %copy-done, bf16[16,2,48,256]{3,2,1,0:T(8,128)(2,1)} %collective-permute-done.1.refs_0_, bf16[16,2,48,256]{3,2,1,0:T(8,128)(2,1)} %collective-permute-done.3.refs_1_, ...), custom_call_target="tpu_custom_call", output_to_operand_aliasing={{}: (6, {})} | custom-call | flops 1610612736 | bytes 1048576 | tf_op jit(solution)/shard_map/pallas_call | solution.py:81
  91.0 27.7 %all_to_all.16 = bf16[32,2,96,128]{3,2,1,0:T(8,128)(2,1)S(1)} all-to-all(bf16[32,2,96,128]{3,2,1,0:T(8,128)(2,1)S(1)} %bitcast.16), channel_id=1, replica_groups=mesh['yh'=2,'x'=4,'c'=2,'yl'=2,'z'=4] {'yh','yl','z','c'}, dimensions={0} | all-to-all | bytes 3145728 | tf_op jit(solution)/shard_map/all_to_all | solution.py:134
  118.7 1.3 %copy.11 = bf16[16,2,2,96,128]{4,3,1,0,2:T(8,128)(2,1)} copy(bf16[16,2,2,96,128]{4,3,2,1,0:T(8,128)(2,1)S(1)} %bitcast.17) | data formatting | bytes 3145728 | tf_op jit(solution)/shard_map/reshape | solution.py:135
  (5 shorter events, 0.0 us)
Async XLA Ops:
  31.4 6.8 %copy-start.3 = (bf16[2,16,128,256]{3,2,1,0:T(8,128)(2,1)S(1)}, bf16[2,16,128,256]{3,2,1,0:T(8,128)(2,1)}, u32[]{:S(2)}) copy-start(bf16[2,16,128,256]{3,2,1,0:T(8,128)(2,1)} %param.3) | copy-start | bytes 6291460
  32.8 18.4 %collective-permute-start = (bf16[16,2,48,256]{3,2,1,0:T(8,128)(2,1)}, bf16[16,2,48,256]{3,2,1,0:T(8,128)(2,1)S(1)}, u32[]{:S(2)}, u32[]{:S(2)}) collective-permute-start(bf16[16,2,48,256]{3,2,1,0:T(8,128)(2,1)} %get-tuple-element.10.refs_0_), channel_id=1, source_target_pairs={{0,16},{16,32},{32,48},{48,0},{1,17},{17,33},{33,49},{49,1},{2,18}... | collective-permute-start | bytes 2359304 | tf_op jit(solution)/shard_map/ppermute | solution.py:108
  34.0 18.2 %collective-permute-start.2 = (bf16[16,2,48,256]{3,2,1,0:T(8,128)(2,1)}, bf16[16,2,48,256]{3,2,1,0:T(8,128)(2,1)}, u32[]{:S(2)}, u32[]{:S(2)}) collective-permute-start(bf16[16,2,48,256]{3,2,1,0:T(8,128)(2,1)} %get-tuple-element.9.refs_1_), channel_id=1, source_target_pairs={{0,48},{16,0},{32,16},{48,32},{1,49},{17,1},{33,17},{49,33},{2,50}... | collective-permute-start | bytes 2359304 | tf_op jit(solution)/shard_map/ppermute | solution.py:108
  35.5 32.6 %collective-permute-start.5 = (bf16[16,2,48,256]{3,2,1,0:T(8,128)(2,1)}, bf16[16,2,48,256]{3,2,1,0:T(8,128)(2,1)}, u32[]{:S(2)}, u32[]{:S(2)}) collective-permute-start(bf16[16,2,48,256]{3,2,1,0:T(8,128)(2,1)} %get-tuple-element.9.refs_1_), channel_id=1, source_target_pairs={{0,16},{16,32},{32,48},{48,0},{1,17},{17,33},{33,49},{49,1},{2,18}... | collective-permute-start | bytes 2359304 | tf_op jit(solution)/shard_map/ppermute | solution.py:108
  35.5 39.5 %collective-permute-start.6 = (bf16[16,2,48,256]{3,2,1,0:T(8,128)(2,1)}, bf16[16,2,48,256]{3,2,1,0:T(8,128)(2,1)}, u32[]{:S(2)}, u32[]{:S(2)}) collective-permute-start(bf16[16,2,48,256]{3,2,1,0:T(8,128)(2,1)} %get-tuple-element.10.refs_0_), channel_id=1, source_target_pairs={{0,48},{16,0},{32,16},{48,32},{1,49},{17,1},{33,17},{49,33},{2,50}... | collective-permute-start | bytes 2359304 | tf_op jit(solution)/shard_map/ppermute | solution.py:108
  39.6 29.7 %all-to-all-start.1 = ((bf16[16,2,128,256]{3,2,1,0:T(8,128)(2,1)}), bf16[16,2,128,256]{3,2,1,0:T(8,128)(2,1)}, u32[]{:S(2)}, u32[]{:S(2)}) async-start(bf16[16,2,128,256]{3,2,1,0:T(8,128)(2,1)} %bitcast.14), calls=%async_computation.1 | async-start | bytes 4194304 | tf_op jit(solution)/shard_map/all_to_all | solution.py:112
  51.2 0.9 copy-start.1
  52.1 34.9 %collective-permute-start.1 = (bf16[16,2,48,256]{3,2,1,0:T(8,128)(2,1)}, bf16[16,2,48,256]{3,2,1,0:T(8,128)(2,1)}, u32[]{:S(2)}, u32[]{:S(2)}) collective-permute-start(bf16[16,2,48,256]{3,2,1,0:T(8,128)(2,1)} %shard_map.37.refs_2_), channel_id=1, source_target_pairs={{0,16},{16,32},{32,48},{48,0},{1,17},{17,33},{33,49},{49,1},{2,18}... | collective-permute-start | bytes 2359304 | tf_op jit(solution)/shard_map/ppermute | solution.py:108
  52.2 34.8 %collective-permute-start.3 = (bf16[16,2,48,256]{3,2,1,0:T(8,128)(2,1)}, bf16[16,2,48,256]{3,2,1,0:T(8,128)(2,1)}, u32[]{:S(2)}, u32[]{:S(2)}) collective-permute-start(bf16[16,2,48,256]{3,2,1,0:T(8,128)(2,1)} %shard_map.38.refs_5_), channel_id=1, source_target_pairs={{0,48},{16,0},{32,16},{48,32},{1,49},{17,1},{33,17},{49,33},{2,50}... | collective-permute-start | bytes 2359304 | tf_op jit(solution)/shard_map/ppermute | solution.py:108
  68.1 10.9 %copy-start = (f32[2,16]{1,0:T(2,128)S(1)}, f32[2,16]{1,0:T(2,128)}, u32[]{:S(2)}) copy-start(f32[2,16]{1,0:T(2,128)} %wave.3) | copy-start | bytes 388
  68.2 10.9 %copy-start.2 = (bf16[16,2,48,256]{3,2,1,0:T(8,128)(2,1)S(1)}, bf16[16,2,48,256]{3,2,1,0:T(8,128)(2,1)}, u32[]{:S(2)}) copy-start(bf16[16,2,48,256]{3,2,1,0:T(8,128)(2,1)} %shard_map.37.refs_2_) | copy-start | bytes 2359300
  69.4 9.7 %collective-permute-start.4 = (bf16[16,2,128,256]{3,2,1,0:T(8,128)(2,1)}, bf16[16,2,128,256]{3,2,1,0:T(8,128)(2,1)S(1)}, u32[]{:S(2)}, u32[]{:S(2)}) collective-permute-start(bf16[16,2,128,256]{3,2,1,0:T(8,128)(2,1)} %all-to-all-done.1.refs_6_.refs_2_), channel_id=1, source_target_pairs={{0,8},{8,0},{1,9},{9,1},{2,10},{10,2},{3,11},{11,3},{4,12},{12,4},... | collective-permute-start | bytes 6291464 | tf_op jit(solution)/shard_map/ppermute | solution.py:108

commit v4 on v3

v4 whole, which is shorter than its diff:
```python
import functools

import jax
import jax.numpy as jnp
from jax import lax
from jax.experimental import pallas as pl
from jax.experimental.pallas import tpu as pltpu
from jax.sharding import Mesh
from jax.sharding import PartitionSpec as P

FREQUENCY = ("yh", "yl", "z")
PLACES = ("yh", "yl", "z", "c")
ORDER = 10**11


def rows_of(piece, half):
    groups = piece.shape[0] // 2
    return jnp.concatenate(
        [piece[half * groups + j].reshape(-1, piece.shape[3]) for j in range(groups)], axis=1
    )


def emit(terms, steps, pieces, p_half, to_core, place, wave, out):
    shots = terms.shape[1] // 2
    x, frequency = place[0], place[2]
    w_real, w_imag = wave[0, frequency], wave[1, frequency]
    at = 0
    for k, piece in enumerate(pieces):
        rows = piece.shape[2]
        to = lax.rem(x + steps[k // 2], 4)
        low = 0 if k % 2 == 0 else pieces[k - 1].shape[2]
        for half in range(2):
            real, imag = terms[at : at + rows], terms[at + rows : at + 2 * rows]
            at += 2 * rows
            s_real = real[:, :shots] - imag[:, shots:]
            s_imag = real[:, shots:] + imag[:, :shots]
            out[p_half, half, to, to_core, 0, low : low + rows] = (
                w_real * s_real - w_imag * s_imag
            ).astype(out.dtype)
            out[p_half, half, to, to_core, 1, low : low + rows] = (
                w_real * s_imag + w_imag * s_real
            ).astype(out.dtype)


def product_kernel(steps, place, wave, *refs):
    pieces, factors = refs[: 2 * len(steps)], refs[2 * len(steps) :]
    out = factors[-1] if len(factors) == 3 else factors[-2]
    for distance in range(2):
        to_core = lax.rem(place[1] + distance, 2)
        for p_half in range(2):
            if len(factors) == 4:
                right_factor = rows_of(factors[distance], p_half)
                factors[-1][distance, p_half] = right_factor
            else:
                right_factor = factors[0][distance, p_half]
            left_factor = jnp.concatenate(
                [rows_of(piece, half) for piece in pieces for half in range(2)], axis=0
            )
            terms = lax.dot_general(
                left_factor,
                right_factor,
                (((1,), (1,)), ((), ())),
                preferred_element_type=jnp.float32,
            )
            emit(terms, steps, pieces, p_half, to_core, place, wave, out)


def product(place, wavelet, blocks, factors, earlier=None):
    steps = tuple(blocks)
    pieces = [piece for pair in blocks.values() for piece in pair]
    depth = pieces[0].shape[0] // 2 * pieces[0].shape[3]
    rows = pieces[0].shape[2] + pieces[1].shape[2]
    shots = factors[0].shape[2] if earlier is None else factors[0].shape[2] // 2
    vmem = pl.BlockSpec(memory_space=pltpu.VMEM)
    smem = pl.BlockSpec(memory_space=pltpu.SMEM)
    operands = [place, wavelet, *pieces, *factors]
    shape = jax.ShapeDtypeStruct((2, 2, 4, 2, 2, rows, shots), jnp.bfloat16)
    aliases = {}
    if earlier is None:
        shape = (shape, jax.ShapeDtypeStruct((2, 2, 2 * shots, depth), jnp.bfloat16))
    else:
        aliases = {len(operands): 0}
        operands.append(earlier)
    flops = 2 * (4 * rows * len(steps)) * (8 * shots) * depth
    return pl.pallas_call(
        functools.partial(product_kernel, steps),
        out_shape=shape,
        in_specs=[smem, smem] + [vmem] * (len(operands) - 2),
        out_specs=(vmem, vmem) if earlier is None else vmem,
        input_output_aliases=aliases,
        compiler_params=pltpu.CompilerParams(vmem_limit_bytes=32 * 2**20),
        cost_estimate=pl.CostEstimate(flops=flops, bytes_accessed=2**20, transcendentals=0),
    )(*operands)


def moves_kernel(pairs, source, *refs):
    outs, done = refs[:-1], refs[-1]
    copies = [
        pltpu.make_async_copy(source.at[a], outs[k].at[b], done.at[i])
        for i, (a, k, b) in enumerate(pairs)
    ]
    for copy in copies:
        copy.start()
    for copy in copies:
        copy.wait()


def moves(value, pairs, shapes, source_space, out_space):
    outs = [jax.ShapeDtypeStruct(shape, value.dtype) for shape in shapes]
    return pl.pallas_call(
        functools.partial(moves_kernel, pairs),
        out_shape=outs,
        in_specs=[pl.BlockSpec(memory_space=source_space)],
        out_specs=[pl.BlockSpec(memory_space=out_space)] * len(outs),
        scratch_shapes=[pltpu.SemaphoreType.DMA((len(pairs),))],
        compiler_params=pltpu.CompilerParams(vmem_limit_bytes=8 * 2**20),
        cost_estimate=pl.CostEstimate(
            flops=0, bytes_accessed=2 * value.size * value.dtype.itemsize, transcendentals=0
        ),
    )(value)


def ordered_kernel(source, out):
    pass


def ordered(value):
    return pl.pallas_call(
        ordered_kernel,
        out_shape=jax.ShapeDtypeStruct(value.shape, value.dtype),
        in_specs=[pl.BlockSpec(memory_space=pl.ANY)],
        out_specs=pl.BlockSpec(memory_space=pl.ANY),
        input_output_aliases={0: 0},
        cost_estimate=pl.CostEstimate(flops=ORDER, bytes_accessed=0, transcendentals=0),
    )(value)


def shift(value, axis, size, step):
    return lax.ppermute(value, axis, [(i, (i + step) % size) for i in range(size)])


def by_frequency(value):
    return lax.all_to_all(value, FREQUENCY, 0, 0, tiled=True)


def on_device(shot_spec, recv_spec, wavelet):
    place = jnp.stack(
        [lax.axis_index("x"), lax.axis_index("c"), lax.axis_index(FREQUENCY)]
    ).astype(jnp.int32)
    rows, depth = recv_spec.shape[2:]
    half = rows // 2
    every = slice(None)
    (recv,) = moves(
        recv_spec,
        [(part, 0, (every, part)) for part in range(2)],
        [(16, 2, rows, depth)],
        pltpu.HBM,
        pltpu.VMEM,
    )
    recv = by_frequency(recv)
    recv, shot_spec = lax.optimization_barrier((recv, shot_spec))
    first, second = moves(
        recv,
        [((every, every, pl.ds(k * half, half)), k, every) for k in range(2)],
        [(16, 2, half, depth)] * 2,
        pltpu.VMEM,
        pl.ANY,
    )
    first_left, second_right = shift(first, "x", 4, 1), shift(second, "x", 4, -1)
    first_left, second_right = ordered(first_left), ordered(second_right)
    first_far, second_far = shift(first_left, "x", 4, 1), shift(second_right, "x", 4, -1)
    first_right, second_left = ordered(shift(first, "x", 4, -1)), ordered(shift(second, "x", 4, 1))
    shots = by_frequency(shot_spec.swapaxes(0, 1))
    other = shift(shots, "c", 2, 1)
    near = {0: (first, second), 3: (first_left, second_left), 1: (first_right, second_right)}
    far = {2: (first_far, second_far)}
    out, packed = product(place, wavelet, near, (shots, other))
    out = product(place, wavelet, far, (packed,), out)
    out = out.reshape((-1,) + out.shape[4:])
    out = lax.all_to_all(out, PLACES, 0, 0, tiled=True)
    out = out.reshape((out.shape[0] // 2, 2) + out.shape[1:])
    (out,) = moves(
        out,
        [((every, every, part), 0, part) for part in range(2)],
        [(2,) + out.shape[:2] + out.shape[3:]],
        pltpu.VMEM,
        pl.ANY,
    )
    out = out.reshape(out.shape[:2] + (-1, out.shape[-1]))
    return out.swapaxes(2, 3)


def solution(mesh):
    devices = mesh.devices.reshape(2, 4, 2, 2, 4)
    wide = Mesh(devices, ("yh", "x", "c", "yl", "z"))
    spec = P(None, None, ("yh", "x", "c"), ("yl", "z"))
    return jax.shard_map(
        on_device, mesh=wide, in_specs=(spec, spec, P()), out_specs=spec, check_vma=False
    )
```

time: 120 us -> 120 us (level)
  local copies, waits for them, and re-layouts: 6.54 us -> 3.76 us
  Pallas kernels: 11.9 us -> 13.7 us
    pallas_call x2 -> x5, Pallas kernels: 11.9 us -> 13.7 us  [the longest x2 11.2 us: product(): pl.pallas_call(functools.partial(product_kernel, steps), out_shape=shape,...]
    slice x1 -> x0, local copies, waits for them, and re-layouts: 1.33 us -> none  [on_device(): first, second = (recv[:, :, :half], recv[:, :, half:])]
    reshape x1 -> x0, local copies, waits for them, and re-layouts: 1.33 us -> none  [on_device(): out = out.reshape((out.shape[0] // 2, 2) + out.shape[1:])]
    unnamed x9 -> x10, local copies, waits for them, and re-layouts: 2.44 us -> 2.31 us
where the time goes in v4:
time: 120 us; the launch traced here: 119 us
  blocking collectives  57.7 us (48%)
  waiting for transfers between devices  25.7 us (21%)
  starting transfers between devices  18.2 us (15%)
  Pallas kernels  13.7 us (11%)
  local copies, waits for them, and re-layouts  3.76 us (3%)
    all_to_all x1, blocking collectives, by_frequency(): return lax.all_to_all(value, FREQUENCY, 0, 0, tiled=True)  30 us
    all_to_all x1, blocking collectives, on_device(): out = lax.all_to_all(out, PLACES, 0, 0, tiled=True)  27.7 us
    ppermute x7, waiting for transfers between devices, shift(): lax.ppermute(value, axis, [(i, (i + step) % size) for i in range(size)])  24.5 us
    ppermute x7, starting transfers between devices, shift(): lax.ppermute(value, axis, [(i, (i + step) % size) for i in range(size)])  13.8 us
    pallas_call x2, Pallas kernels, product(): pl.pallas_call(functools.partial(product_kernel, steps), out_shape=shape,...  11.2 us
    all_to_all x1, starting transfers between devices, by_frequency(): return lax.all_to_all(value, FREQUENCY, 0, 0, tiled=True)  4.45 us
    pallas_call x3, Pallas kernels, moves(): pl.pallas_call(functools.partial(moves_kernel, pairs), out_shape=outs, in...  2.45 us
  transfers between devices with their start and end apart: 8, of which 4 were waited for; matrix products, arithmetic and copies ran while one was open for 1% of the time, Pallas kernels for 7%

profile of v4, /device:TPU:1, one launch (start us, length us, event | category | flops | bytes accessed | tf_op | source)
XLA Modules:
  0.0 119.2 jit_solution(6129539458827145790)
XLA Ops:
  0.0 0.0 copy-start
  0.0 1.4 %copy-done = bf16[2,16,96,256]{3,2,1,0:T(8,128)(2,1)S(1)} copy-done((bf16[2,16,96,256]{3,2,1,0:T(8,128)(2,1)S(1)}, bf16[2,16,96,256]{3,2,1,0:T(8,128)(2,1)}, u32[]{:S(2)}) %copy-start) | copy-done | bytes 1572888
  1.4 0.1 shard_map.37
  1.5 0.0 copy-start.4
  1.6 30.0 %all_to_all.15.source = bf16[16,2,96,256]{3,2,1,0:T(8,128)(2,1)S(1)} all-to-all(bf16[16,2,96,256]{3,2,1,0:T(8,128)(2,1)S(1)} %shard_map.37), channel_id=1, replica_groups=mesh['yh'=2,'x'=4,'c'=2,'yl'=2,'z'=4] {'yh','yl','z'}, dimensions={0} | all-to-all | bytes 3145728 | tf_op jit(solution)/shard_map/all_to_all | solution.py:143
  31.6 1.2 shard_map.38
  32.8 1.3 %collective-permute-start = (bf16[16,2,48,256]{3,2,1,0:T(8,128)(2,1)}, bf16[16,2,48,256]{3,2,1,0:T(8,128)(2,1)S(1)}, u32[]{:S(2)}, u32[]{:S(2)}) collective-permute-start(bf16[16,2,48,256]{3,2,1,0:T(8,128)(2,1)} %get-tuple-element.12.refs_0_), channel_id=1, source_target_pairs={{0,16},{16,32},{32,48},{48,0},{1,17},{17,33},{33,49},{49,1},{2,18}... | collective-permute-start | bytes 2359304 | tf_op jit(solution)/shard_map/ppermute | solution.py:139
  34.0 0.1 pad_add_fusion.place
  34.1 1.5 %collective-permute-start.2 = (bf16[16,2,48,256]{3,2,1,0:T(8,128)(2,1)}, bf16[16,2,48,256]{3,2,1,0:T(8,128)(2,1)}, u32[]{:S(2)}, u32[]{:S(2)}) collective-permute-start(bf16[16,2,48,256]{3,2,1,0:T(8,128)(2,1)} %get-tuple-element.13.refs_1_), channel_id=1, source_target_pairs={{0,48},{16,0},{32,16},{48,32},{1,49},{17,1},{33,17},{49,33},{2,50}... | collective-permute-start | bytes 2359304 | tf_op jit(solution)/shard_map/ppermute | solution.py:139
  35.6 0.0 collective-permute-start.4
  35.6 2.7 %collective-permute-start.5 = (bf16[16,2,48,256]{3,2,1,0:T(8,128)(2,1)}, bf16[16,2,48,256]{3,2,1,0:T(8,128)(2,1)}, u32[]{:S(2)}, u32[]{:S(2)}) collective-permute-start(bf16[16,2,48,256]{3,2,1,0:T(8,128)(2,1)} %get-tuple-element.12.refs_0_), channel_id=1, source_target_pairs={{0,48},{16,0},{32,16},{48,32},{1,49},{17,1},{33,17},{49,33},{2,50}... | collective-permute-start | bytes 2359304 | tf_op jit(solution)/shard_map/ppermute | solution.py:139
  38.3 0.0 copy-done.4
  38.3 1.5 %copy.11 = bf16[2,16,128,256]{3,2,0,1:T(8,128)(2,1)} copy(bf16[2,16,128,256]{3,2,1,0:T(8,128)(2,1)S(1)} %copy-done.4) | data formatting | bytes 4194304 | tf_op jit(solution)/shard_map/optimization_barrier | solution.py:161
  39.7 4.4 %all-to-all-start.1 = ((bf16[16,2,128,256]{3,2,1,0:T(8,128)(2,1)}), bf16[16,2,128,256]{3,2,1,0:T(8,128)(2,1)}, u32[]{:S(2)}, u32[]{:S(2)}) async-start(bf16[16,2,128,256]{3,2,1,0:T(8,128)(2,1)} %bitcast.10), calls=%async_computation.1 | async-start | bytes 4194304 | tf_op jit(solution)/shard_map/all_to_all | solution.py:143
  44.2 7.1 %collective-permute-done.source = bf16[16,2,48,256]{3,2,1,0:T(8,128)(2,1)S(1)} collective-permute-done((bf16[16,2,48,256]{3,2,1,0:T(8,128)(2,1)}, bf16[16,2,48,256]{3,2,1,0:T(8,128)(2,1)S(1)}, u32[]{:S(2)}, u32[]{:S(2)}) %collective-permute-start) | collective-permute-done | bytes 786464 | tf_op jit(solution)/shard_map/ppermute | solution.py:139
  51.3 0.9 copy-done.2
  52.1 0.1 collective-permute-start.1
  52.3 0.0 collective-permute-done.2.source
  52.3 2.6 %collective-permute-start.3 = (bf16[16,2,48,256]{3,2,1,0:T(8,128)(2,1)}, bf16[16,2,48,256]{3,2,1,0:T(8,128)(2,1)}, u32[]{:S(2)}, u32[]{:S(2)}) collective-permute-start(bf16[16,2,48,256]{3,2,1,0:T(8,128)(2,1)} %shard_map.40.refs_5_), channel_id=1, source_target_pairs={{0,48},{16,0},{32,16},{48,32},{1,49},{17,1},{33,17},{49,33},{2,50}... | collective-permute-start | bytes 2359304 | tf_op jit(solution)/shard_map/ppermute | solution.py:139
  54.8 13.4 %collective-permute-done.4.source = bf16[16,2,48,256]{3,2,1,0:T(8,128)(2,1)} collective-permute-done((bf16[16,2,48,256]{3,2,1,0:T(8,128)(2,1)}, bf16[16,2,48,256]{3,2,1,0:T(8,128)(2,1)}, u32[]{:S(2)}, u32[]{:S(2)}) %collective-permute-start.4) | collective-permute-done | bytes 786464 | tf_op jit(solution)/shard_map/ppermute | solution.py:139
  68.2 1.2 %all-to-all-done.1.refs_6_ = bf16[16,2,128,256]{3,2,1,0:T(8,128)(2,1)} async-done(((bf16[16,2,128,256]{3,2,1,0:T(8,128)(2,1)}), bf16[16,2,128,256]{3,2,1,0:T(8,128)(2,1)}, u32[]{:S(2)}, u32[]{:S(2)}) %all-to-all-start.1) | async-done | bytes 2097184 | tf_op jit(solution)/shard_map/all_to_all | solution.py:143
  69.4 5.7 %collective-permute-start.6 = (bf16[16,2,128,256]{3,2,1,0:T(8,128)(2,1)}, bf16[16,2,128,256]{3,2,1,0:T(8,128)(2,1)S(1)}, u32[]{:S(2)}, u32[]{:S(2)}) collective-permute-start(bf16[16,2,128,256]{3,2,1,0:T(8,128)(2,1)} %all-to-all-done.1.refs_6_), channel_id=1, source_target_pairs={{0,8},{8,0},{1,9},{9,1},{2,10},{10,2},{3,11},{11,3},{4,12},{12,4},... | collective-permute-start | bytes 6291464 | tf_op jit(solution)/shard_map/ppermute | solution.py:139
  75.1 0.0 collective-permute-done.5.source
  75.1 4.0 %collective-permute-done.6.refs_7_ = bf16[16,2,128,256]{3,2,1,0:T(8,128)(2,1)S(1)} collective-permute-done((bf16[16,2,128,256]{3,2,1,0:T(8,128)(2,1)}, bf16[16,2,128,256]{3,2,1,0:T(8,128)(2,1)S(1)}, u32[]{:S(2)}, u32[]{:S(2)}) %collective-permute-start.6) | collective-permute-done | bytes 2097184 | tf_op jit(solution)/shard_map/ppermute | solution.py:139
  79.1 0.0 copy-done.1
  79.1 0.0 copy-done.3
  79.1 8.0 %shard_map.43 = (bf16[2,2,4,2,2,96,128]{6,5,4,3,2,1,0:T(8,128)(2,1)S(1)}, bf16[2,2,256,2048]{3,2,1,0:T(8,128)(2,1)S(1)}) custom-call(s32[3]{0:T(128)S(1)} %pad_add_fusion.place, f32[2,16]{1,0:T(2,128)S(1)} %copy-done.1, bf16[16,2,48,256]{3,2,1,0:T(8,128)(2,1)} %get-tuple-element.12.refs_0_, bf16[16,2,48,256]{3,2,1,0:T(8,128)(2,1)} %get-tuple-element.13.refs_1_, ...), custom_call_target="tpu_custom_call" | custom-call | flops 4831838208 | bytes 1048576 | tf_op jit(solution)/shard_map/pallas_call | solution.py:85
  87.1 0.0 collective-permute-done.1.refs_0_
  87.1 0.0 collective-permute-done.3.refs_1_
  87.2 3.2 %shard_map.44 = bf16[2,2,4,2,2,96,128]{6,5,4,3,2,1,0:T(8,128)(2,1)S(1)} custom-call(s32[3]{0:T(128)S(1)} %pad_add_fusion.place, f32[2,16]{1,0:T(2,128)S(1)} %copy-done.1, bf16[16,2,48,256]{3,2,1,0:T(8,128)(2,1)} %collective-permute-done.1.refs_0_, bf16[16,2,48,256]{3,2,1,0:T(8,128)(2,1)} %collective-permute-done.3.refs_1_, ...), custom_call_target="tpu_custom_call", output_to_operand_aliasing={{}: (5, {})} | custom-call | flops 1610612736 | bytes 1048576 | tf_op jit(solution)/shard_map/pallas_call | solution.py:85
  90.4 27.7 %all_to_all.16 = bf16[32,2,96,128]{3,2,1,0:T(8,128)(2,1)S(1)} all-to-all(bf16[32,2,96,128]{3,2,1,0:T(8,128)(2,1)S(1)} %bitcast.11), channel_id=1, replica_groups=mesh['yh'=2,'x'=4,'c'=2,'yl'=2,'z'=4] {'yh','yl','z','c'}, dimensions={0} | all-to-all | bytes 3145728 | tf_op jit(solution)/shard_map/all_to_all | solution.py:180
  118.1 1.2 shard_map.45
  (7 shorter events, 0.0 us)
Async XLA Ops:
  0.0 1.4 %copy-start = (bf16[2,16,96,256]{3,2,1,0:T(8,128)(2,1)S(1)}, bf16[2,16,96,256]{3,2,1,0:T(8,128)(2,1)}, u32[]{:S(2)}) copy-start(bf16[2,16,96,256]{3,2,1,0:T(8,128)(2,1)} %source.1) | copy-start | bytes 4718596
  1.5 36.7 %copy-start.4 = (bf16[2,16,128,256]{3,2,1,0:T(8,128)(2,1)S(1)}, bf16[2,16,128,256]{3,2,1,0:T(8,128)(2,1)}, u32[]{:S(2)}) copy-start(bf16[2,16,128,256]{3,2,1,0:T(8,128)(2,1)} %param.3) | copy-start | bytes 6291460
  32.8 18.5 %collective-permute-start = (bf16[16,2,48,256]{3,2,1,0:T(8,128)(2,1)}, bf16[16,2,48,256]{3,2,1,0:T(8,128)(2,1)S(1)}, u32[]{:S(2)}, u32[]{:S(2)}) collective-permute-start(bf16[16,2,48,256]{3,2,1,0:T(8,128)(2,1)} %get-tuple-element.12.refs_0_), channel_id=1, source_target_pairs={{0,16},{16,32},{32,48},{48,0},{1,17},{17,33},{33,49},{49,1},{2,18}... | collective-permute-start | bytes 2359304 | tf_op jit(solution)/shard_map/ppermute | solution.py:139
  34.1 18.1 %collective-permute-start.2 = (bf16[16,2,48,256]{3,2,1,0:T(8,128)(2,1)}, bf16[16,2,48,256]{3,2,1,0:T(8,128)(2,1)}, u32[]{:S(2)}, u32[]{:S(2)}) collective-permute-start(bf16[16,2,48,256]{3,2,1,0:T(8,128)(2,1)} %get-tuple-element.13.refs_1_), channel_id=1, source_target_pairs={{0,48},{16,0},{32,16},{48,32},{1,49},{17,1},{33,17},{49,33},{2,50}... | collective-permute-start | bytes 2359304 | tf_op jit(solution)/shard_map/ppermute | solution.py:139
  35.6 32.6 %collective-permute-start.4 = (bf16[16,2,48,256]{3,2,1,0:T(8,128)(2,1)}, bf16[16,2,48,256]{3,2,1,0:T(8,128)(2,1)}, u32[]{:S(2)}, u32[]{:S(2)}) collective-permute-start(bf16[16,2,48,256]{3,2,1,0:T(8,128)(2,1)} %get-tuple-element.13.refs_1_), channel_id=1, source_target_pairs={{0,16},{16,32},{32,48},{48,0},{1,17},{17,33},{33,49},{49,1},{2,18}... | collective-permute-start | bytes 2359304 | tf_op jit(solution)/shard_map/ppermute | solution.py:139
  35.6 39.6 %collective-permute-start.5 = (bf16[16,2,48,256]{3,2,1,0:T(8,128)(2,1)}, bf16[16,2,48,256]{3,2,1,0:T(8,128)(2,1)}, u32[]{:S(2)}, u32[]{:S(2)}) collective-permute-start(bf16[16,2,48,256]{3,2,1,0:T(8,128)(2,1)} %get-tuple-element.12.refs_0_), channel_id=1, source_target_pairs={{0,48},{16,0},{32,16},{48,32},{1,49},{17,1},{33,17},{49,33},{2,50}... | collective-permute-start | bytes 2359304 | tf_op jit(solution)/shard_map/ppermute | solution.py:139
  39.7 29.7 %all-to-all-start.1 = ((bf16[16,2,128,256]{3,2,1,0:T(8,128)(2,1)}), bf16[16,2,128,256]{3,2,1,0:T(8,128)(2,1)}, u32[]{:S(2)}, u32[]{:S(2)}) async-start(bf16[16,2,128,256]{3,2,1,0:T(8,128)(2,1)} %bitcast.10), calls=%async_computation.1 | async-start | bytes 4194304 | tf_op jit(solution)/shard_map/all_to_all | solution.py:143
  51.3 0.9 copy-start.2
  52.1 35.0 %collective-permute-start.1 = (bf16[16,2,48,256]{3,2,1,0:T(8,128)(2,1)}, bf16[16,2,48,256]{3,2,1,0:T(8,128)(2,1)}, u32[]{:S(2)}, u32[]{:S(2)}) collective-permute-start(bf16[16,2,48,256]{3,2,1,0:T(8,128)(2,1)} %shard_map.39.refs_2_), channel_id=1, source_target_pairs={{0,16},{16,32},{32,48},{48,0},{1,17},{17,33},{33,49},{49,1},{2,18}... | collective-permute-start | bytes 2359304 | tf_op jit(solution)/shard_map/ppermute | solution.py:139
  52.3 34.9 %collective-permute-start.3 = (bf16[16,2,48,256]{3,2,1,0:T(8,128)(2,1)}, bf16[16,2,48,256]{3,2,1,0:T(8,128)(2,1)}, u32[]{:S(2)}, u32[]{:S(2)}) collective-permute-start(bf16[16,2,48,256]{3,2,1,0:T(8,128)(2,1)} %shard_map.40.refs_5_), channel_id=1, source_target_pairs={{0,48},{16,0},{32,16},{48,32},{1,49},{17,1},{33,17},{49,33},{2,50}... | collective-permute-start | bytes 2359304 | tf_op jit(solution)/shard_map/ppermute | solution.py:139
  68.2 10.9 %copy-start.1 = (f32[2,16]{1,0:T(2,128)S(1)}, f32[2,16]{1,0:T(2,128)}, u32[]{:S(2)}) copy-start(f32[2,16]{1,0:T(2,128)} %wave.3) | copy-start | bytes 388
  68.2 10.9 %copy-start.3 = (bf16[16,2,48,256]{3,2,1,0:T(8,128)(2,1)S(1)}, bf16[16,2,48,256]{3,2,1,0:T(8,128)(2,1)}, u32[]{:S(2)}) copy-start(bf16[16,2,48,256]{3,2,1,0:T(8,128)(2,1)} %shard_map.39.refs_2_) | copy-start | bytes 2359300
  69.4 9.7 %collective-permute-start.6 = (bf16[16,2,128,256]{3,2,1,0:T(8,128)(2,1)}, bf16[16,2,128,256]{3,2,1,0:T(8,128)(2,1)S(1)}, u32[]{:S(2)}, u32[]{:S(2)}) collective-permute-start(bf16[16,2,128,256]{3,2,1,0:T(8,128)(2,1)} %all-to-all-done.1.refs_6_), channel_id=1, source_target_pairs={{0,8},{8,0},{1,9},{9,1},{2,10},{10,2},{3,11},{11,3},{4,12},{12,4},... | collective-permute-start | bytes 6291464 | tf_op jit(solution)/shard_map/ppermute | solution.py:139

commit v5 on v4

v5 whole, which is shorter than its diff:
```python
import functools

import jax
import jax.numpy as jnp
from jax import lax
from jax.experimental import pallas as pl
from jax.experimental.pallas import tpu as pltpu
from jax.sharding import Mesh
from jax.sharding import PartitionSpec as P

FREQUENCY = ("yh", "yl", "z")
PLACES = ("yh", "yl", "z", "c")
ORDER = 2 * 10**10


def rows_of(piece, half):
    groups = piece.shape[0] // 2
    return jnp.concatenate(
        [piece[half * groups + j].reshape(-1, piece.shape[3]) for j in range(groups)], axis=1
    )


def emit(terms, spots, pieces, p_half, to_core, place, wave, out):
    shots = terms.shape[1] // 2
    x, frequency = place[0], place[2]
    w_real, w_imag = wave[0, frequency], wave[1, frequency]
    at = 0
    for (step, low), piece in zip(spots, pieces):
        rows = piece.shape[2]
        to = lax.rem(x + step, 4)
        for half in range(2):
            real, imag = terms[at : at + rows], terms[at + rows : at + 2 * rows]
            at += 2 * rows
            s_real = real[:, :shots] - imag[:, shots:]
            s_imag = real[:, shots:] + imag[:, :shots]
            out[p_half, half, to, to_core, 0, low : low + rows] = (
                w_real * s_real - w_imag * s_imag
            ).astype(out.dtype)
            out[p_half, half, to, to_core, 1, low : low + rows] = (
                w_real * s_imag + w_imag * s_real
            ).astype(out.dtype)


def product_kernel(spots, distances, pack, earlier, place, wave, *refs):
    pieces, refs = refs[: len(spots)], refs[len(spots) :]
    factors = refs[: len(distances)]
    out, *packed = refs[len(distances) + earlier :]
    for distance, factor in zip(distances, factors):
        to_core = lax.rem(place[1] + distance, 2)
        for p_half in range(2):
            if len(factor.shape) == 4:
                right_factor = rows_of(factor, p_half)
            else:
                right_factor = factor[p_half]
            if pack:
                packed[distance - distances[0]][p_half] = right_factor
            left_factor = jnp.concatenate(
                [rows_of(piece, half) for piece in pieces for half in range(2)], axis=0
            )
            terms = lax.dot_general(
                left_factor,
                right_factor,
                (((1,), (1,)), ((), ())),
                preferred_element_type=jnp.float32,
            )
            emit(terms, spots, pieces, p_half, to_core, place, wave, out)


def product(place, wavelet, blocks, factors, rows, earlier=None, pack=False):
    spots, pieces = tuple(blocks), list(blocks.values())
    distances, factors = tuple(factors), list(factors.values())
    depth = pieces[0].shape[0] // 2 * pieces[0].shape[3]
    shots = factors[0].shape[2] if factors[0].ndim == 4 else factors[0].shape[1] // 2
    vmem = pl.BlockSpec(memory_space=pltpu.VMEM)
    smem = pl.BlockSpec(memory_space=pltpu.SMEM)
    operands = [place, wavelet, *pieces, *factors]
    shapes = [jax.ShapeDtypeStruct((2, 2, 4, 2, 2, rows, shots), jnp.bfloat16)]
    if pack:
        shapes += [jax.ShapeDtypeStruct((2, 2 * shots, depth), jnp.bfloat16)] * len(factors)
    aliases = {}
    if earlier is not None:
        aliases = {len(operands): 0}
        operands.append(earlier)
    count = sum(piece.shape[2] for piece in pieces)
    flops = 2 * (4 * count) * (4 * shots * len(factors)) * depth
    return pl.pallas_call(
        functools.partial(product_kernel, spots, distances, pack, len(aliases)),
        out_shape=shapes,
        in_specs=[smem, smem] + [vmem] * (len(operands) - 2),
        out_specs=[vmem] * len(shapes),
        input_output_aliases=aliases,
        compiler_params=pltpu.CompilerParams(vmem_limit_bytes=28 * 2**20),
        cost_estimate=pl.CostEstimate(flops=flops, bytes_accessed=2**20, transcendentals=0),
    )(*operands)


def moves_kernel(pairs, count, *refs):
    sources, outs, done = refs[:count], refs[count:-1], refs[-1]
    copies = [
        pltpu.make_async_copy(sources[n].at[a], outs[k].at[b], done.at[i])
        for i, (n, a, k, b) in enumerate(pairs)
    ]
    for copy in copies:
        copy.start()
    for copy in copies:
        copy.wait()


def moves(values, pairs, shapes, source_space, out_space):
    outs = [jax.ShapeDtypeStruct(shape, values[0].dtype) for shape in shapes]
    return pl.pallas_call(
        functools.partial(moves_kernel, pairs, len(values)),
        out_shape=outs,
        in_specs=[pl.BlockSpec(memory_space=source_space)] * len(values),
        out_specs=[pl.BlockSpec(memory_space=out_space)] * len(outs),
        scratch_shapes=[pltpu.SemaphoreType.DMA((len(pairs),))],
        compiler_params=pltpu.CompilerParams(vmem_limit_bytes=8 * 2**20),
        cost_estimate=pl.CostEstimate(
            flops=0, bytes_accessed=4 * sum(value.size for value in values), transcendentals=0
        ),
    )(*values)


def ordered_kernel(source, out):
    pass


def ordered(value):
    return pl.pallas_call(
        ordered_kernel,
        out_shape=jax.ShapeDtypeStruct(value.shape, value.dtype),
        in_specs=[pl.BlockSpec(memory_space=pl.ANY)],
        out_specs=pl.BlockSpec(memory_space=pl.ANY),
        input_output_aliases={0: 0},
        cost_estimate=pl.CostEstimate(flops=ORDER, bytes_accessed=0, transcendentals=0),
    )(value)


def shift(value, axis, size, step):
    return lax.ppermute(value, axis, [(i, (i + step) % size) for i in range(size)])


def by_frequency(value):
    return lax.all_to_all(value, FREQUENCY, 0, 0, tiled=True)


def on_device(shot_spec, recv_spec, wavelet):
    place = jnp.stack(
        [lax.axis_index("x"), lax.axis_index("c"), lax.axis_index(FREQUENCY)]
    ).astype(jnp.int32)
    rows, depth = recv_spec.shape[2:]
    every = slice(None)
    (recv,) = moves(
        [recv_spec],
        [(0, part, 0, (every, part)) for part in range(2)],
        [(16, 2, rows, depth)],
        pltpu.HBM,
        pltpu.VMEM,
    )
    recv = by_frequency(recv)
    recv, shot_spec = lax.optimization_barrier((recv, shot_spec))
    half = rows // 2
    first, second = moves(
        [recv],
        [(0, (every, every, pl.ds(k * half, half)), k, every) for k in range(2)],
        [(16, 2, half, depth)] * 2,
        pltpu.VMEM,
        pl.ANY,
    )
    first_left, second_right = shift(first, "x", 4, 1), shift(second, "x", 4, -1)
    first_left, second_right = ordered(first_left), ordered(second_right)
    far = {(2, 0): shift(first_left, "x", 4, 1), (2, half): shift(second_right, "x", 4, -1)}
    first_right = ordered(shift(first, "x", 4, -1))
    second_left = ordered(shift(second, "x", 4, 1))
    shots = by_frequency(shot_spec.swapaxes(0, 1))
    other = shift(shots, "c", 2, 1)
    near = {(0, 0): first, (0, half): second, (3, 0): first_left, (3, half): second_left}
    near |= {(1, 0): first_right, (1, half): second_right}
    out, own_p = product(place, wavelet, near, {0: shots}, rows, pack=True)
    out, other_p = product(place, wavelet, near, {1: other}, rows, out, pack=True)
    factors = {0: own_p, 1: other_p}
    (out,) = product(place, wavelet, far, factors, rows, out)
    out = back(out)
    (out,) = moves(
        [out],
        [(0, (every, every, part), 0, part) for part in range(2)],
        [(2,) + out.shape[:2] + out.shape[3:]],
        pltpu.VMEM,
        pl.ANY,
    )
    out = out.reshape(out.shape[:2] + (-1, out.shape[-1]))
    return out.swapaxes(2, 3)


def back(out):
    out = out.reshape((-1,) + out.shape[4:])
    out = lax.all_to_all(out, PLACES, 0, 0, tiled=True)
    return out.reshape((out.shape[0] // 2, 2) + out.shape[1:])


def solution(mesh):
    devices = mesh.devices.reshape(2, 4, 2, 2, 4)
    wide = Mesh(devices, ("yh", "x", "c", "yl", "z"))
    spec = P(None, None, ("yh", "x", "c"), ("yl", "z"))
    return jax.shard_map(
        on_device, mesh=wide, in_specs=(spec, spec, P()), out_specs=spec, check_vma=False
    )
```

time: 120 us -> 119 us (level)
  waiting for transfers between devices: 25.7 us -> 21.6 us
  Pallas kernels: 13.7 us -> 15.8 us
    ppermute x7, waiting for transfers between devices: 24.5 us -> 21.1 us  [shift(): lax.ppermute(value, axis, [(i, (i + step) % size) for i in range(size)])]
    pallas_call x5 -> x6, Pallas kernels: 13.7 us -> 15.8 us  [the longest x3 13.3 us: product(): pl.pallas_call(functools.partial(product_kernel, spots, distances, pack,...]
    unnamed x10 -> x12, local copies, waits for them, and re-layouts: 2.31 us -> 3.43 us
  transfers between devices with their start and end apart: 8 -> 8, of which waited for: 4 -> 3; matrix products, arithmetic and copies ran while one was open for 1% -> 1% of each run, Pallas kernels for 7% -> 9%
where the time goes in v5:
time: 119 us
  blocking collectives  58.8 us (49%)
  waiting for transfers between devices  21.6 us (18%)
  starting transfers between devices  17.7 us (15%)
  Pallas kernels  15.8 us (13%)
  local copies, waits for them, and re-layouts  4.92 us (4%)
    all_to_all x1, blocking collectives, by_frequency(): return lax.all_to_all(value, FREQUENCY, 0, 0, tiled=True)  30 us
    all_to_all x1, blocking collectives, back(): out = lax.all_to_all(out, PLACES, 0, 0, tiled=True)  28.8 us
    ppermute x7, waiting for transfers between devices, shift(): lax.ppermute(value, axis, [(i, (i + step) % size) for i in range(size)])  21.1 us
    ppermute x7, starting transfers between devices, shift(): lax.ppermute(value, axis, [(i, (i + step) % size) for i in range(size)])  13.9 us
    pallas_call x3, Pallas kernels, product(): pl.pallas_call(functools.partial(product_kernel, spots, distances, pack,...  13.3 us
    all_to_all x1, starting transfers between devices, by_frequency(): return lax.all_to_all(value, FREQUENCY, 0, 0, tiled=True)  3.77 us
    unnamed x12, local copies, waits for them, and re-layouts  3.43 us
    pallas_call x3, Pallas kernels, moves(): pl.pallas_call(functools.partial(moves_kernel, pairs, len(values)), out_s...  2.44 us
  transfers between devices with their start and end apart: 8, of which 3 were waited for; matrix products, arithmetic and copies ran while one was open for 1% of the time, Pallas kernels for 9%

profile of v5, /device:TPU:1, one launch (start us, length us, event | category | flops | bytes accessed | tf_op | source)
XLA Modules:
  0.0 119.0 jit_solution(10177215044888038692)
XLA Ops:
  0.0 1.4 %copy-done = bf16[2,16,96,256]{3,2,1,0:T(8,128)(2,1)S(1)} copy-done((bf16[2,16,96,256]{3,2,1,0:T(8,128)(2,1)S(1)}, bf16[2,16,96,256]{3,2,1,0:T(8,128)(2,1)}, u32[]{:S(2)}) %copy-start) | copy-done | bytes 1572888
  1.4 0.1 shard_map.37
  1.5 0.0 copy-start.5
  1.6 30.0 %all_to_all.15.refs_0_ = bf16[16,2,96,256]{3,2,1,0:T(8,128)(2,1)S(1)} all-to-all(bf16[16,2,96,256]{3,2,1,0:T(8,128)(2,1)S(1)} %shard_map.37), channel_id=1, replica_groups=mesh['yh'=2,'x'=4,'c'=2,'yl'=2,'z'=4] {'yh','yl','z'}, dimensions={0} | all-to-all | bytes 3145728 | tf_op jit(solution)/shard_map/all_to_all | solution.py:144
  31.6 1.2 shard_map.38
  32.7 1.3 %collective-permute-start = (bf16[16,2,48,256]{3,2,1,0:T(8,128)(2,1)}, bf16[16,2,48,256]{3,2,1,0:T(8,128)(2,1)S(1)}, u32[]{:S(2)}, u32[]{:S(2)}) collective-permute-start(bf16[16,2,48,256]{3,2,1,0:T(8,128)(2,1)} %get-tuple-element.14.refs_0_), channel_id=1, source_target_pairs={{0,16},{16,32},{32,48},{48,0},{1,17},{17,33},{33,49},{49,1},{2,18}... | collective-permute-start | bytes 2359304 | tf_op jit(solution)/shard_map/ppermute | solution.py:140
  34.0 0.1 pad_add_fusion.place
  34.1 1.5 %collective-permute-start.2 = (bf16[16,2,48,256]{3,2,1,0:T(8,128)(2,1)}, bf16[16,2,48,256]{3,2,1,0:T(8,128)(2,1)}, u32[]{:S(2)}, u32[]{:S(2)}) collective-permute-start(bf16[16,2,48,256]{3,2,1,0:T(8,128)(2,1)} %get-tuple-element.15.refs_1_), channel_id=1, source_target_pairs={{0,48},{16,0},{32,16},{48,32},{1,49},{17,1},{33,17},{49,33},{2,50}... | collective-permute-start | bytes 2359304 | tf_op jit(solution)/shard_map/ppermute | solution.py:140
  35.6 0.0 collective-permute-start.4
  35.6 2.7 %collective-permute-start.5 = (bf16[16,2,48,256]{3,2,1,0:T(8,128)(2,1)}, bf16[16,2,48,256]{3,2,1,0:T(8,128)(2,1)}, u32[]{:S(2)}, u32[]{:S(2)}) collective-permute-start(bf16[16,2,48,256]{3,2,1,0:T(8,128)(2,1)} %get-tuple-element.14.refs_0_), channel_id=1, source_target_pairs={{0,48},{16,0},{32,16},{48,32},{1,49},{17,1},{33,17},{49,33},{2,50}... | collective-permute-start | bytes 2359304 | tf_op jit(solution)/shard_map/ppermute | solution.py:140
  38.2 0.0 copy-done.5
  38.3 1.5 %copy.12 = bf16[2,16,128,256]{3,2,0,1:T(8,128)(2,1)} copy(bf16[2,16,128,256]{3,2,1,0:T(8,128)(2,1)S(1)} %copy-done.5) | data formatting | bytes 4194304 | tf_op jit(solution)/shard_map/optimization_barrier | solution.py:161
  39.7 3.8 %all-to-all-start.1 = ((bf16[16,2,128,256]{3,2,1,0:T(8,128)(2,1)}), bf16[16,2,128,256]{3,2,1,0:T(8,128)(2,1)S(1)}, u32[]{:S(2)}, u32[]{:S(2)}) async-start(bf16[16,2,128,256]{3,2,1,0:T(8,128)(2,1)} %bitcast.13), calls=%async_computation.1 | async-start | bytes 4194304 | tf_op jit(solution)/shard_map/all_to_all | solution.py:144
  43.5 7.7 %collective-permute-done.source = bf16[16,2,48,256]{3,2,1,0:T(8,128)(2,1)S(1)} collective-permute-done((bf16[16,2,48,256]{3,2,1,0:T(8,128)(2,1)}, bf16[16,2,48,256]{3,2,1,0:T(8,128)(2,1)S(1)}, u32[]{:S(2)}, u32[]{:S(2)}) %collective-permute-start) | collective-permute-done | bytes 786464 | tf_op jit(solution)/shard_map/ppermute | solution.py:140
  51.3 0.9 copy-done.2
  52.1 0.1 collective-permute-start.1
  52.2 0.0 collective-permute-done.2.source
  52.2 2.6 %collective-permute-start.3 = (bf16[16,2,48,256]{3,2,1,0:T(8,128)(2,1)}, bf16[16,2,48,256]{3,2,1,0:T(8,128)(2,1)}, u32[]{:S(2)}, u32[]{:S(2)}) collective-permute-start(bf16[16,2,48,256]{3,2,1,0:T(8,128)(2,1)} %shard_map.40.refs_5_), channel_id=1, source_target_pairs={{0,48},{16,0},{32,16},{48,32},{1,49},{17,1},{33,17},{49,33},{2,50}... | collective-permute-start | bytes 2359304 | tf_op jit(solution)/shard_map/ppermute | solution.py:140
  54.8 13.4 %collective-permute-done.4.source = bf16[16,2,48,256]{3,2,1,0:T(8,128)(2,1)} collective-permute-done((bf16[16,2,48,256]{3,2,1,0:T(8,128)(2,1)}, bf16[16,2,48,256]{3,2,1,0:T(8,128)(2,1)}, u32[]{:S(2)}, u32[]{:S(2)}) %collective-permute-start.4) | collective-permute-done | bytes 786464 | tf_op jit(solution)/shard_map/ppermute | solution.py:140
  68.2 0.5 all-to-all-done.1.refs_6_
  68.7 5.8 %collective-permute-start.6 = (bf16[16,2,128,256]{3,2,1,0:T(8,128)(2,1)S(1)}, bf16[16,2,128,256]{3,2,1,0:T(8,128)(2,1)}, u32[]{:S(2)}, u32[]{:S(2)}) collective-permute-start(bf16[16,2,128,256]{3,2,1,0:T(8,128)(2,1)S(1)} %all-to-all-done.1.refs_6_), channel_id=1, source_target_pairs={{0,8},{8,0},{1,9},{9,1},{2,10},{10,2},{3,11},{11,3},{4,12},{12,4},... | collective-permute-start | bytes 6291464 | tf_op jit(solution)/shard_map/ppermute | solution.py:140
  74.5 0.0 collective-permute-done.5.source
  74.5 0.0 copy-done.1
  74.5 1.1 copy-done.3
  75.6 4.9 %shard_map.43 = (bf16[2,2,4,2,2,96,128]{6,5,4,3,2,1,0:T(8,128)(2,1)S(1)}, bf16[2,256,2048]{2,1,0:T(8,128)(2,1)S(1)}) custom-call(s32[3]{0:T(128)S(1)} %pad_add_fusion.place, f32[2,16]{1,0:T(2,128)S(1)} %copy-done.1, bf16[16,2,48,256]{3,2,1,0:T(8,128)(2,1)} %get-tuple-element.14.refs_0_, bf16[16,2,48,256]{3,2,1,0:T(8,128)(2,1)} %get-tuple-element.15.refs_1_, ...), custom_call_target="tpu_custom_call" | custom-call | flops 2415919104 | bytes 1048576 | tf_op jit(solution)/shard_map/pallas_call | solution.py:86
  80.5 0.0 collective-permute-done.6.refs_6_
  80.5 5.5 %shard_map.44 = (bf16[2,2,4,2,2,96,128]{6,5,4,3,2,1,0:T(8,128)(2,1)S(1)}, bf16[2,256,2048]{2,1,0:T(8,128)(2,1)S(1)}) custom-call(s32[3]{0:T(128)S(1)} %pad_add_fusion.place, f32[2,16]{1,0:T(2,128)S(1)} %copy-done.1, bf16[16,2,48,256]{3,2,1,0:T(8,128)(2,1)} %get-tuple-element.14.refs_0_, ...), custom_call_target="tpu_custom_call", output_to_operand_aliasing={{0}: (9, {})} | custom-call | flops 2415919104 | bytes 1048576 | tf_op jit(solution)/shard_map/pallas_call | solution.py:86
  86.0 0.0 collective-permute-done.1.refs_0_
  86.1 0.0 collective-permute-done.3.refs_1_
  86.1 3.0 %shard_map.45 = bf16[2,2,4,2,2,96,128]{6,5,4,3,2,1,0:T(8,128)(2,1)S(1)} custom-call(s32[3]{0:T(128)S(1)} %pad_add_fusion.place, f32[2,16]{1,0:T(2,128)S(1)} %copy-done.1, bf16[16,2,48,256]{3,2,1,0:T(8,128)(2,1)S(1)} %collective-permute-done.1.refs_0_, bf16[16,2,48,256]{3,2,1,0:T(8,128)(2,1)} %collective-permute-done.3.refs_1_, ...), custom_call_target="tpu_custom_call", output_to_operand_aliasing={{}: (6, {})} | custom-call | flops 1610612736 | bytes 1048576 | tf_op jit(solution)/shard_map/pallas_call | solution.py:86
  89.1 28.8 %all_to_all.16 = bf16[32,2,96,128]{3,2,1,0:T(8,128)(2,1)S(1)} all-to-all(bf16[32,2,96,128]{3,2,1,0:T(8,128)(2,1)S(1)} %bitcast.11), channel_id=1, replica_groups=mesh['yh'=2,'x'=4,'c'=2,'yl'=2,'z'=4] {'yh','yl','z','c'}, dimensions={0} | all-to-all | bytes 3145728 | tf_op jit(solution)/shard_map/all_to_all | solution.py:197
  117.8 1.2 shard_map.46
  (10 shorter events, 0.0 us)
Async XLA Ops:
  0.0 1.4 %copy-start = (bf16[2,16,96,256]{3,2,1,0:T(8,128)(2,1)S(1)}, bf16[2,16,96,256]{3,2,1,0:T(8,128)(2,1)}, u32[]{:S(2)}) copy-start(bf16[2,16,96,256]{3,2,1,0:T(8,128)(2,1)} %refs_0_.1) | copy-start | bytes 4718596
  1.5 36.7 %copy-start.5 = (bf16[2,16,128,256]{3,2,1,0:T(8,128)(2,1)S(1)}, bf16[2,16,128,256]{3,2,1,0:T(8,128)(2,1)}, u32[]{:S(2)}) copy-start(bf16[2,16,128,256]{3,2,1,0:T(8,128)(2,1)} %param.3) | copy-start | bytes 6291460
  32.7 18.5 %collective-permute-start = (bf16[16,2,48,256]{3,2,1,0:T(8,128)(2,1)}, bf16[16,2,48,256]{3,2,1,0:T(8,128)(2,1)S(1)}, u32[]{:S(2)}, u32[]{:S(2)}) collective-permute-start(bf16[16,2,48,256]{3,2,1,0:T(8,128)(2,1)} %get-tuple-element.14.refs_0_), channel_id=1, source_target_pairs={{0,16},{16,32},{32,48},{48,0},{1,17},{17,33},{33,49},{49,1},{2,18}... | collective-permute-start | bytes 2359304 | tf_op jit(solution)/shard_map/ppermute | solution.py:140
  34.1 18.1 %collective-permute-start.2 = (bf16[16,2,48,256]{3,2,1,0:T(8,128)(2,1)}, bf16[16,2,48,256]{3,2,1,0:T(8,128)(2,1)}, u32[]{:S(2)}, u32[]{:S(2)}) collective-permute-start(bf16[16,2,48,256]{3,2,1,0:T(8,128)(2,1)} %get-tuple-element.15.refs_1_), channel_id=1, source_target_pairs={{0,48},{16,0},{32,16},{48,32},{1,49},{17,1},{33,17},{49,33},{2,50}... | collective-permute-start | bytes 2359304 | tf_op jit(solution)/shard_map/ppermute | solution.py:140
  35.6 32.6 %collective-permute-start.4 = (bf16[16,2,48,256]{3,2,1,0:T(8,128)(2,1)}, bf16[16,2,48,256]{3,2,1,0:T(8,128)(2,1)}, u32[]{:S(2)}, u32[]{:S(2)}) collective-permute-start(bf16[16,2,48,256]{3,2,1,0:T(8,128)(2,1)} %get-tuple-element.15.refs_1_), channel_id=1, source_target_pairs={{0,16},{16,32},{32,48},{48,0},{1,17},{17,33},{33,49},{49,1},{2,18}... | collective-permute-start | bytes 2359304 | tf_op jit(solution)/shard_map/ppermute | solution.py:140
  35.6 38.9 %collective-permute-start.5 = (bf16[16,2,48,256]{3,2,1,0:T(8,128)(2,1)}, bf16[16,2,48,256]{3,2,1,0:T(8,128)(2,1)}, u32[]{:S(2)}, u32[]{:S(2)}) collective-permute-start(bf16[16,2,48,256]{3,2,1,0:T(8,128)(2,1)} %get-tuple-element.14.refs_0_), channel_id=1, source_target_pairs={{0,48},{16,0},{32,16},{48,32},{1,49},{17,1},{33,17},{49,33},{2,50}... | collective-permute-start | bytes 2359304 | tf_op jit(solution)/shard_map/ppermute | solution.py:140
  39.7 29.0 %all-to-all-start.1 = ((bf16[16,2,128,256]{3,2,1,0:T(8,128)(2,1)}), bf16[16,2,128,256]{3,2,1,0:T(8,128)(2,1)S(1)}, u32[]{:S(2)}, u32[]{:S(2)}) async-start(bf16[16,2,128,256]{3,2,1,0:T(8,128)(2,1)} %bitcast.13), calls=%async_computation.1 | async-start | bytes 4194304 | tf_op jit(solution)/shard_map/all_to_all | solution.py:144
  51.3 0.9 copy-start.2
  52.1 33.9 %collective-permute-start.1 = (bf16[16,2,48,256]{3,2,1,0:T(8,128)(2,1)}, bf16[16,2,48,256]{3,2,1,0:T(8,128)(2,1)S(1)}, u32[]{:S(2)}, u32[]{:S(2)}) collective-permute-start(bf16[16,2,48,256]{3,2,1,0:T(8,128)(2,1)} %shard_map.39.refs_2_), channel_id=1, source_target_pairs={{0,16},{16,32},{32,48},{48,0},{1,17},{17,33},{33,49},{49,1},{2,18}... | collective-permute-start | bytes 2359304 | tf_op jit(solution)/shard_map/ppermute | solution.py:140
  52.2 33.8 %collective-permute-start.3 = (bf16[16,2,48,256]{3,2,1,0:T(8,128)(2,1)}, bf16[16,2,48,256]{3,2,1,0:T(8,128)(2,1)}, u32[]{:S(2)}, u32[]{:S(2)}) collective-permute-start(bf16[16,2,48,256]{3,2,1,0:T(8,128)(2,1)} %shard_map.40.refs_5_), channel_id=1, source_target_pairs={{0,48},{16,0},{32,16},{48,32},{1,49},{17,1},{33,17},{49,33},{2,50}... | collective-permute-start | bytes 2359304 | tf_op jit(solution)/shard_map/ppermute | solution.py:140
  68.2 6.3 %copy-start.1 = (f32[2,16]{1,0:T(2,128)S(1)}, f32[2,16]{1,0:T(2,128)}, u32[]{:S(2)}) copy-start(f32[2,16]{1,0:T(2,128)} %wave.5) | copy-start | bytes 388
  68.7 11.8 %collective-permute-start.6 = (bf16[16,2,128,256]{3,2,1,0:T(8,128)(2,1)S(1)}, bf16[16,2,128,256]{3,2,1,0:T(8,128)(2,1)}, u32[]{:S(2)}, u32[]{:S(2)}) collective-permute-start(bf16[16,2,128,256]{3,2,1,0:T(8,128)(2,1)S(1)} %all-to-all-done.1.refs_6_), channel_id=1, source_target_pairs={{0,8},{8,0},{1,9},{9,1},{2,10},{10,2},{3,11},{11,3},{4,12},{12,4},... | collective-permute-start | bytes 6291464 | tf_op jit(solution)/shard_map/ppermute | solution.py:140
  74.5 1.1 copy-start.3
  75.6 4.9 %copy-start.4 = (bf16[16,2,48,256]{3,2,1,0:T(8,128)(2,1)S(1)}, bf16[16,2,48,256]{3,2,1,0:T(8,128)(2,1)}, u32[]{:S(2)}) copy-start(bf16[16,2,48,256]{3,2,1,0:T(8,128)(2,1)} %shard_map.39.refs_2_) | copy-start | bytes 2359300

commit v6 on v5

--- a/solution.py
+++ b/solution.py
@@ -9,7 +9,7 @@
 from jax.sharding import PartitionSpec as P
 
 FREQUENCY = ("yh", "yl", "z")
-PLACES = ("yh", "yl", "z", "c")
+PLACES = ("yh", "yl", "c", "z")
 ORDER = 2 * 10**10
 
 
@@ -33,10 +33,10 @@
             at += 2 * rows
             s_real = real[:, :shots] - imag[:, shots:]
             s_imag = real[:, shots:] + imag[:, :shots]
-            out[p_half, half, to, to_core, 0, low : low + rows] = (
+            out[p_half, half, to_core, to, 0, low : low + rows] = (
                 w_real * s_real - w_imag * s_imag
             ).astype(out.dtype)
-            out[p_half, half, to, to_core, 1, low : low + rows] = (
+            out[p_half, half, to_core, to, 1, low : low + rows] = (
                 w_real * s_imag + w_imag * s_real
             ).astype(out.dtype)
 
@@ -74,7 +74,7 @@
     vmem = pl.BlockSpec(memory_space=pltpu.VMEM)
     smem = pl.BlockSpec(memory_space=pltpu.SMEM)
     operands = [place, wavelet, *pieces, *factors]
-    shapes = [jax.ShapeDtypeStruct((2, 2, 4, 2, 2, rows, shots), jnp.bfloat16)]
+    shapes = [jax.ShapeDtypeStruct((2, 2, 2, 4, 2, rows, shots), jnp.bfloat16)]
     if pack:
         shapes += [jax.ShapeDtypeStruct((2, 2 * shots, depth), jnp.bfloat16)] * len(factors)
     aliases = {}
@@ -183,19 +183,23 @@
     out = back(out)
     (out,) = moves(
         [out],
-        [(0, (every, every, part), 0, part) for part in range(2)],
-        [(2,) + out.shape[:2] + out.shape[3:]],
+        [
+            (0, (every, core, every, part), 0, (part, every, every, core))
+            for part in range(2)
+            for core in range(2)
+        ],
+        [(2, 4, 4, 2) + out.shape[4:]],
         pltpu.VMEM,
         pl.ANY,
     )
-    out = out.reshape(out.shape[:2] + (-1, out.shape[-1]))
+    out = out.reshape((2, 16, -1, out.shape[-1]))
     return out.swapaxes(2, 3)
 
 
 def back(out):
     out = out.reshape((-1,) + out.shape[4:])
     out = lax.all_to_all(out, PLACES, 0, 0, tiled=True)
-    return out.reshape((out.shape[0] // 2, 2) + out.shape[1:])
+    return out.reshape((4, 2, 4) + out.shape[1:])
 
 
 def solution(mesh):

time: 119 us -> 119 us (level)
  no operation moved by 1% of the time
where the time goes in v6:
time: 119 us; the launch traced here: 118 us
  blocking collectives  58.3 us (49%)
  waiting for transfers between devices  21.6 us (18%)
  starting transfers between devices  17.7 us (15%)
  Pallas kernels  15.8 us (13%)
  local copies, waits for them, and re-layouts  4.92 us (4%)
    all_to_all x1, blocking collectives, by_frequency(): return lax.all_to_all(value, FREQUENCY, 0, 0, tiled=True)  30 us
    all_to_all x1, blocking collectives, back(): out = lax.all_to_all(out, PLACES, 0, 0, tiled=True)  28.2 us
    ppermute x7, waiting for transfers between devices, shift(): lax.ppermute(value, axis, [(i, (i + step) % size) for i in range(size)])  21.1 us
    ppermute x7, starting transfers between devices, shift(): lax.ppermute(value, axis, [(i, (i + step) % size) for i in range(size)])  13.9 us
    pallas_call x3, Pallas kernels, product(): pl.pallas_call(functools.partial(product_kernel, spots, distances, pack,...  13.3 us
    all_to_all x1, starting transfers between devices, by_frequency(): return lax.all_to_all(value, FREQUENCY, 0, 0, tiled=True)  3.77 us
    unnamed x12, local copies, waits for them, and re-layouts  3.43 us
    pallas_call x3, Pallas kernels, moves(): pl.pallas_call(functools.partial(moves_kernel, pairs, len(values)), out_s...  2.46 us
  transfers between devices with their start and end apart: 8, of which 3 were waited for; matrix products, arithmetic and copies ran while one was open for 1% of the time, Pallas kernels for 9%

profile of v6, /device:TPU:1, one launch (start us, length us, event | category | flops | bytes accessed | tf_op | source)
XLA Modules:
  0.0 118.5 jit_solution(7907361420058796798)
XLA Ops:
  0.0 1.4 %copy-done = bf16[2,16,96,256]{3,2,1,0:T(8,128)(2,1)S(1)} copy-done((bf16[2,16,96,256]{3,2,1,0:T(8,128)(2,1)S(1)}, bf16[2,16,96,256]{3,2,1,0:T(8,128)(2,1)}, u32[]{:S(2)}) %copy-start) | copy-done | bytes 1572888
  1.4 0.1 shard_map.37
  1.5 0.0 copy-start.5
  1.6 30.0 %all_to_all.15.refs_0_ = bf16[16,2,96,256]{3,2,1,0:T(8,128)(2,1)S(1)} all-to-all(bf16[16,2,96,256]{3,2,1,0:T(8,128)(2,1)S(1)} %shard_map.37), channel_id=1, replica_groups=mesh['yh'=2,'x'=4,'c'=2,'yl'=2,'z'=4] {'yh','yl','z'}, dimensions={0} | all-to-all | bytes 3145728 | tf_op jit(solution)/shard_map/all_to_all | solution.py:144
  31.6 1.2 shard_map.38
  32.7 1.3 %collective-permute-start = (bf16[16,2,48,256]{3,2,1,0:T(8,128)(2,1)}, bf16[16,2,48,256]{3,2,1,0:T(8,128)(2,1)S(1)}, u32[]{:S(2)}, u32[]{:S(2)}) collective-permute-start(bf16[16,2,48,256]{3,2,1,0:T(8,128)(2,1)} %get-tuple-element.14.refs_0_), channel_id=1, source_target_pairs={{0,16},{16,32},{32,48},{48,0},{1,17},{17,33},{33,49},{49,1},{2,18}... | collective-permute-start | bytes 2359304 | tf_op jit(solution)/shard_map/ppermute | solution.py:140
  34.0 0.1 pad_add_fusion.place
  34.1 1.5 %collective-permute-start.2 = (bf16[16,2,48,256]{3,2,1,0:T(8,128)(2,1)}, bf16[16,2,48,256]{3,2,1,0:T(8,128)(2,1)}, u32[]{:S(2)}, u32[]{:S(2)}) collective-permute-start(bf16[16,2,48,256]{3,2,1,0:T(8,128)(2,1)} %get-tuple-element.15.refs_1_), channel_id=1, source_target_pairs={{0,48},{16,0},{32,16},{48,32},{1,49},{17,1},{33,17},{49,33},{2,50}... | collective-permute-start | bytes 2359304 | tf_op jit(solution)/shard_map/ppermute | solution.py:140
  35.6 0.0 collective-permute-start.4
  35.6 2.7 %collective-permute-start.5 = (bf16[16,2,48,256]{3,2,1,0:T(8,128)(2,1)}, bf16[16,2,48,256]{3,2,1,0:T(8,128)(2,1)}, u32[]{:S(2)}, u32[]{:S(2)}) collective-permute-start(bf16[16,2,48,256]{3,2,1,0:T(8,128)(2,1)} %get-tuple-element.14.refs_0_), channel_id=1, source_target_pairs={{0,48},{16,0},{32,16},{48,32},{1,49},{17,1},{33,17},{49,33},{2,50}... | collective-permute-start | bytes 2359304 | tf_op jit(solution)/shard_map/ppermute | solution.py:140
  38.2 0.0 copy-done.5
  38.3 1.5 %copy.12 = bf16[2,16,128,256]{3,2,0,1:T(8,128)(2,1)} copy(bf16[2,16,128,256]{3,2,1,0:T(8,128)(2,1)S(1)} %copy-done.5) | data formatting | bytes 4194304 | tf_op jit(solution)/shard_map/optimization_barrier | solution.py:161
  39.7 3.8 %all-to-all-start.1 = ((bf16[16,2,128,256]{3,2,1,0:T(8,128)(2,1)}), bf16[16,2,128,256]{3,2,1,0:T(8,128)(2,1)S(1)}, u32[]{:S(2)}, u32[]{:S(2)}) async-start(bf16[16,2,128,256]{3,2,1,0:T(8,128)(2,1)} %bitcast.13), calls=%async_computation.1 | async-start | bytes 4194304 | tf_op jit(solution)/shard_map/all_to_all | solution.py:144
  43.5 7.7 %collective-permute-done.source = bf16[16,2,48,256]{3,2,1,0:T(8,128)(2,1)S(1)} collective-permute-done((bf16[16,2,48,256]{3,2,1,0:T(8,128)(2,1)}, bf16[16,2,48,256]{3,2,1,0:T(8,128)(2,1)S(1)}, u32[]{:S(2)}, u32[]{:S(2)}) %collective-permute-start) | collective-permute-done | bytes 786464 | tf_op jit(solution)/shard_map/ppermute | solution.py:140
  51.3 0.9 copy-done.2
  52.1 0.1 collective-permute-start.1
  52.2 0.0 collective-permute-done.2.source
  52.2 2.6 %collective-permute-start.3 = (bf16[16,2,48,256]{3,2,1,0:T(8,128)(2,1)}, bf16[16,2,48,256]{3,2,1,0:T(8,128)(2,1)}, u32[]{:S(2)}, u32[]{:S(2)}) collective-permute-start(bf16[16,2,48,256]{3,2,1,0:T(8,128)(2,1)} %shard_map.40.refs_5_), channel_id=1, source_target_pairs={{0,48},{16,0},{32,16},{48,32},{1,49},{17,1},{33,17},{49,33},{2,50}... | collective-permute-start | bytes 2359304 | tf_op jit(solution)/shard_map/ppermute | solution.py:140
  54.8 13.4 %collective-permute-done.4.source = bf16[16,2,48,256]{3,2,1,0:T(8,128)(2,1)} collective-permute-done((bf16[16,2,48,256]{3,2,1,0:T(8,128)(2,1)}, bf16[16,2,48,256]{3,2,1,0:T(8,128)(2,1)}, u32[]{:S(2)}, u32[]{:S(2)}) %collective-permute-start.4) | collective-permute-done | bytes 786464 | tf_op jit(solution)/shard_map/ppermute | solution.py:140
  68.2 0.5 all-to-all-done.1.refs_6_
  68.7 5.8 %collective-permute-start.6 = (bf16[16,2,128,256]{3,2,1,0:T(8,128)(2,1)S(1)}, bf16[16,2,128,256]{3,2,1,0:T(8,128)(2,1)}, u32[]{:S(2)}, u32[]{:S(2)}) collective-permute-start(bf16[16,2,128,256]{3,2,1,0:T(8,128)(2,1)S(1)} %all-to-all-done.1.refs_6_), channel_id=1, source_target_pairs={{0,8},{8,0},{1,9},{9,1},{2,10},{10,2},{3,11},{11,3},{4,12},{12,4},... | collective-permute-start | bytes 6291464 | tf_op jit(solution)/shard_map/ppermute | solution.py:140
  74.5 0.0 collective-permute-done.5.source
  74.5 1.1 copy-done.3
  75.6 4.9 %shard_map.43 = (bf16[2,2,2,4,2,96,128]{6,5,4,3,2,1,0:T(8,128)(2,1)S(1)}, bf16[2,256,2048]{2,1,0:T(8,128)(2,1)S(1)}) custom-call(s32[3]{0:T(128)S(1)} %pad_add_fusion.place, f32[2,16]{1,0:T(2,128)S(1)} %copy-done.1, bf16[16,2,48,256]{3,2,1,0:T(8,128)(2,1)} %get-tuple-element.14.refs_0_, bf16[16,2,48,256]{3,2,1,0:T(8,128)(2,1)} %get-tuple-element.15.refs_1_, ...), custom_call_target="tpu_custom_call" | custom-call | flops 2415919104 | bytes 1048576 | tf_op jit(solution)/shard_map/pallas_call | solution.py:86
  80.5 0.0 collective-permute-done.6.refs_6_
  80.5 0.0 copy-done.4
  80.5 5.5 %shard_map.44 = (bf16[2,2,2,4,2,96,128]{6,5,4,3,2,1,0:T(8,128)(2,1)S(1)}, bf16[2,256,2048]{2,1,0:T(8,128)(2,1)S(1)}) custom-call(s32[3]{0:T(128)S(1)} %pad_add_fusion.place, f32[2,16]{1,0:T(2,128)S(1)} %copy-done.1, bf16[16,2,48,256]{3,2,1,0:T(8,128)(2,1)} %get-tuple-element.14.refs_0_, ...), custom_call_target="tpu_custom_call", output_to_operand_aliasing={{0}: (9, {})} | custom-call | flops 2415919104 | bytes 1048576 | tf_op jit(solution)/shard_map/pallas_call | solution.py:86
  86.0 0.0 collective-permute-done.1.refs_0_
  86.1 0.0 collective-permute-done.3.refs_1_
  86.1 3.0 %shard_map.45 = bf16[2,2,2,4,2,96,128]{6,5,4,3,2,1,0:T(8,128)(2,1)S(1)} custom-call(s32[3]{0:T(128)S(1)} %pad_add_fusion.place, f32[2,16]{1,0:T(2,128)S(1)} %copy-done.1, bf16[16,2,48,256]{3,2,1,0:T(8,128)(2,1)S(1)} %collective-permute-done.1.refs_0_, bf16[16,2,48,256]{3,2,1,0:T(8,128)(2,1)} %collective-permute-done.3.refs_1_, ...), custom_call_target="tpu_custom_call", output_to_operand_aliasing={{}: (6, {})} | custom-call | flops 1610612736 | bytes 1048576 | tf_op jit(solution)/shard_map/pallas_call | solution.py:86
  89.1 28.2 %all_to_all.16 = bf16[32,2,96,128]{3,2,1,0:T(8,128)(2,1)S(1)} all-to-all(bf16[32,2,96,128]{3,2,1,0:T(8,128)(2,1)S(1)} %bitcast.11), channel_id=1, replica_groups=mesh['yh'=2,'x'=4,'c'=2,'yl'=2,'z'=4] {'yh','yl','c','z'}, dimensions={0} | all-to-all | bytes 3145728 | tf_op jit(solution)/shard_map/all_to_all | solution.py:201
  117.3 1.2 shard_map.46
  (10 shorter events, 0.0 us)
Async XLA Ops:
  0.0 1.4 %copy-start = (bf16[2,16,96,256]{3,2,1,0:T(8,128)(2,1)S(1)}, bf16[2,16,96,256]{3,2,1,0:T(8,128)(2,1)}, u32[]{:S(2)}) copy-start(bf16[2,16,96,256]{3,2,1,0:T(8,128)(2,1)} %refs_0_.1) | copy-start | bytes 4718596
  1.5 36.7 %copy-start.5 = (bf16[2,16,128,256]{3,2,1,0:T(8,128)(2,1)S(1)}, bf16[2,16,128,256]{3,2,1,0:T(8,128)(2,1)}, u32[]{:S(2)}) copy-start(bf16[2,16,128,256]{3,2,1,0:T(8,128)(2,1)} %param.3) | copy-start | bytes 6291460
  32.7 18.5 %collective-permute-start = (bf16[16,2,48,256]{3,2,1,0:T(8,128)(2,1)}, bf16[16,2,48,256]{3,2,1,0:T(8,128)(2,1)S(1)}, u32[]{:S(2)}, u32[]{:S(2)}) collective-permute-start(bf16[16,2,48,256]{3,2,1,0:T(8,128)(2,1)} %get-tuple-element.14.refs_0_), channel_id=1, source_target_pairs={{0,16},{16,32},{32,48},{48,0},{1,17},{17,33},{33,49},{49,1},{2,18}... | collective-permute-start | bytes 2359304 | tf_op jit(solution)/shard_map/ppermute | solution.py:140
  34.1 18.1 %collective-permute-start.2 = (bf16[16,2,48,256]{3,2,1,0:T(8,128)(2,1)}, bf16[16,2,48,256]{3,2,1,0:T(8,128)(2,1)}, u32[]{:S(2)}, u32[]{:S(2)}) collective-permute-start(bf16[16,2,48,256]{3,2,1,0:T(8,128)(2,1)} %get-tuple-element.15.refs_1_), channel_id=1, source_target_pairs={{0,48},{16,0},{32,16},{48,32},{1,49},{17,1},{33,17},{49,33},{2,50}... | collective-permute-start | bytes 2359304 | tf_op jit(solution)/shard_map/ppermute | solution.py:140
  35.6 32.6 %collective-permute-start.4 = (bf16[16,2,48,256]{3,2,1,0:T(8,128)(2,1)}, bf16[16,2,48,256]{3,2,1,0:T(8,128)(2,1)}, u32[]{:S(2)}, u32[]{:S(2)}) collective-permute-start(bf16[16,2,48,256]{3,2,1,0:T(8,128)(2,1)} %get-tuple-element.15.refs_1_), channel_id=1, source_target_pairs={{0,16},{16,32},{32,48},{48,0},{1,17},{17,33},{33,49},{49,1},{2,18}... | collective-permute-start | bytes 2359304 | tf_op jit(solution)/shard_map/ppermute | solution.py:140
  35.6 38.9 %collective-permute-start.5 = (bf16[16,2,48,256]{3,2,1,0:T(8,128)(2,1)}, bf16[16,2,48,256]{3,2,1,0:T(8,128)(2,1)}, u32[]{:S(2)}, u32[]{:S(2)}) collective-permute-start(bf16[16,2,48,256]{3,2,1,0:T(8,128)(2,1)} %get-tuple-element.14.refs_0_), channel_id=1, source_target_pairs={{0,48},{16,0},{32,16},{48,32},{1,49},{17,1},{33,17},{49,33},{2,50}... | collective-permute-start | bytes 2359304 | tf_op jit(solution)/shard_map/ppermute | solution.py:140
  39.7 29.0 %all-to-all-start.1 = ((bf16[16,2,128,256]{3,2,1,0:T(8,128)(2,1)}), bf16[16,2,128,256]{3,2,1,0:T(8,128)(2,1)S(1)}, u32[]{:S(2)}, u32[]{:S(2)}) async-start(bf16[16,2,128,256]{3,2,1,0:T(8,128)(2,1)} %bitcast.13), calls=%async_computation.1 | async-start | bytes 4194304 | tf_op jit(solution)/shard_map/all_to_all | solution.py:144
  51.3 0.9 copy-start.2
  52.1 33.9 %collective-permute-start.1 = (bf16[16,2,48,256]{3,2,1,0:T(8,128)(2,1)}, bf16[16,2,48,256]{3,2,1,0:T(8,128)(2,1)S(1)}, u32[]{:S(2)}, u32[]{:S(2)}) collective-permute-start(bf16[16,2,48,256]{3,2,1,0:T(8,128)(2,1)} %shard_map.39.refs_2_), channel_id=1, source_target_pairs={{0,16},{16,32},{32,48},{48,0},{1,17},{17,33},{33,49},{49,1},{2,18}... | collective-permute-start | bytes 2359304 | tf_op jit(solution)/shard_map/ppermute | solution.py:140
  52.2 33.8 %collective-permute-start.3 = (bf16[16,2,48,256]{3,2,1,0:T(8,128)(2,1)}, bf16[16,2,48,256]{3,2,1,0:T(8,128)(2,1)}, u32[]{:S(2)}, u32[]{:S(2)}) collective-permute-start(bf16[16,2,48,256]{3,2,1,0:T(8,128)(2,1)} %shard_map.40.refs_5_), channel_id=1, source_target_pairs={{0,48},{16,0},{32,16},{48,32},{1,49},{17,1},{33,17},{49,33},{2,50}... | collective-permute-start | bytes 2359304 | tf_op jit(solution)/shard_map/ppermute | solution.py:140
  68.2 6.3 %copy-start.1 = (f32[2,16]{1,0:T(2,128)S(1)}, f32[2,16]{1,0:T(2,128)}, u32[]{:S(2)}) copy-start(f32[2,16]{1,0:T(2,128)} %wave.5) | copy-start | bytes 388
  68.7 11.8 %collective-permute-start.6 = (bf16[16,2,128,256]{3,2,1,0:T(8,128)(2,1)S(1)}, bf16[16,2,128,256]{3,2,1,0:T(8,128)(2,1)}, u32[]{:S(2)}, u32[]{:S(2)}) collective-permute-start(bf16[16,2,128,256]{3,2,1,0:T(8,128)(2,1)S(1)} %all-to-all-done.1.refs_6_), channel_id=1, source_target_pairs={{0,8},{8,0},{1,9},{9,1},{2,10},{10,2},{3,11},{11,3},{4,12},{12,4},... | collective-permute-start | bytes 6291464 | tf_op jit(solution)/shard_map/ppermute | solution.py:140
  74.5 1.1 copy-start.3
  75.6 4.9 %copy-start.4 = (bf16[16,2,48,256]{3,2,1,0:T(8,128)(2,1)S(1)}, bf16[16,2,48,256]{3,2,1,0:T(8,128)(2,1)}, u32[]{:S(2)}) copy-start(bf16[16,2,48,256]{3,2,1,0:T(8,128)(2,1)} %shard_map.39.refs_2_) | copy-start | bytes 2359300

commit v7 on v6

--- a/solution.py
+++ b/solution.py
@@ -8,15 +8,15 @@
 from jax.sharding import Mesh
 from jax.sharding import PartitionSpec as P
 
-FREQUENCY = ("yh", "yl", "z")
-PLACES = ("yh", "yl", "c", "z")
+FREQUENCY = ("z", "yl", "yh")
+PLACES = ("z", "yl", "c", "yh")
 ORDER = 2 * 10**10
 
 
 def rows_of(piece, half):
     groups = piece.shape[0] // 2
     return jnp.concatenate(
-        [piece[half * groups + j].reshape(-1, piece.shape[3]) for j in range(groups)], axis=1
+        [piece[2 * j + half].reshape(-1, piece.shape[3]) for j in range(groups)], axis=1
     )
 
 
@@ -33,10 +33,10 @@
             at += 2 * rows
             s_real = real[:, :shots] - imag[:, shots:]
             s_imag = real[:, shots:] + imag[:, :shots]
-            out[p_half, half, to_core, to, 0, low : low + rows] = (
+            out[to, half, to_core, p_half, 0, low : low + rows] = (
                 w_real * s_real - w_imag * s_imag
             ).astype(out.dtype)
-            out[p_half, half, to_core, to, 1, low : low + rows] = (
+            out[to, half, to_core, p_half, 1, low : low + rows] = (
                 w_real * s_imag + w_imag * s_real
             ).astype(out.dtype)
 
@@ -74,7 +74,7 @@
     vmem = pl.BlockSpec(memory_space=pltpu.VMEM)
     smem = pl.BlockSpec(memory_space=pltpu.SMEM)
     operands = [place, wavelet, *pieces, *factors]
-    shapes = [jax.ShapeDtypeStruct((2, 2, 2, 4, 2, rows, shots), jnp.bfloat16)]
+    shapes = [jax.ShapeDtypeStruct((4, 2, 2, 2, 2, rows, shots), jnp.bfloat16)]
     if pack:
         shapes += [jax.ShapeDtypeStruct((2, 2 * shots, depth), jnp.bfloat16)] * len(factors)
     aliases = {}
@@ -188,7 +188,7 @@
             for part in range(2)
             for core in range(2)
         ],
-        [(2, 4, 4, 2) + out.shape[4:]],
+        [(2, 8, 2, 2) + out.shape[4:]],
         pltpu.VMEM,
         pl.ANY,
     )
@@ -199,7 +199,7 @@
 def back(out):
     out = out.reshape((-1,) + out.shape[4:])
     out = lax.all_to_all(out, PLACES, 0, 0, tiled=True)
-    return out.reshape((4, 2, 4) + out.shape[1:])
+    return out.reshape((8, 2, 2) + out.shape[1:])
 
 
 def solution(mesh):

time: 119 us -> 118 us (level)
  blocking collectives: 58.3 us -> 56.6 us
  waiting for transfers between devices: 21.6 us -> 20.4 us
  starting transfers between devices: 17.7 us -> 18.9 us
    ppermute x7, waiting for transfers between devices: 21.1 us -> 19.8 us  [shift(): lax.ppermute(value, axis, [(i, (i + step) % size) for i in range(size)])]
where the time goes in v7:
time: 118 us; the launch traced here: 117 us
  blocking collectives  56.6 us (48%)
  waiting for transfers between devices  20.4 us (17%)
  starting transfers between devices  18.9 us (16%)
  Pallas kernels  15.8 us (13%)
  local copies, waits for them, and re-layouts  4.92 us (4%)
    all_to_all x1, blocking collectives, by_frequency(): return lax.all_to_all(value, FREQUENCY, 0, 0, tiled=True)  28.8 us
    all_to_all x1, blocking collectives, back(): out = lax.all_to_all(out, PLACES, 0, 0, tiled=True)  27.7 us
    ppermute x7, waiting for transfers between devices, shift(): lax.ppermute(value, axis, [(i, (i + step) % size) for i in range(size)])  19.8 us
    ppermute x7, starting transfers between devices, shift(): lax.ppermute(value, axis, [(i, (i + step) % size) for i in range(size)])  14.5 us
    pallas_call x3, Pallas kernels, product(): pl.pallas_call(functools.partial(product_kernel, spots, distances, pack,...  13.3 us
    all_to_all x1, starting transfers between devices, by_frequency(): return lax.all_to_all(value, FREQUENCY, 0, 0, tiled=True)  4.33 us
    unnamed x12, local copies, waits for them, and re-layouts  3.43 us
    pallas_call x3, Pallas kernels, moves(): pl.pallas_call(functools.partial(moves_kernel, pairs, len(values)), out_s...  2.46 us
  transfers between devices with their start and end apart: 8, of which 3 were waited for; matrix products, arithmetic and copies ran while one was open for 1% of the time, Pallas kernels for 9%

profile of v7, /device:TPU:1, one launch (start us, length us, event | category | flops | bytes accessed | tf_op | source)
XLA Modules:
  0.0 116.7 jit_solution(14713744527473779961)
XLA Ops:
  0.0 1.4 %copy-done = bf16[2,16,96,256]{3,2,1,0:T(8,128)(2,1)S(1)} copy-done((bf16[2,16,96,256]{3,2,1,0:T(8,128)(2,1)S(1)}, bf16[2,16,96,256]{3,2,1,0:T(8,128)(2,1)}, u32[]{:S(2)}) %copy-start) | copy-done | bytes 1572888
  1.4 0.1 shard_map.37
  1.5 0.0 copy-start.5
  1.6 28.8 %all_to_all.15.refs_0_ = bf16[16,2,96,256]{3,2,1,0:T(8,128)(2,1)S(1)} all-to-all(bf16[16,2,96,256]{3,2,1,0:T(8,128)(2,1)S(1)} %shard_map.37), channel_id=1, replica_groups=mesh['yh'=2,'x'=4,'c'=2,'yl'=2,'z'=4] {'z','yl','yh'}, dimensions={0} | all-to-all | bytes 3145728 | tf_op jit(solution)/shard_map/all_to_all | solution.py:144
  30.4 1.2 shard_map.38
  31.6 1.3 %collective-permute-start = (bf16[16,2,48,256]{3,2,1,0:T(8,128)(2,1)}, bf16[16,2,48,256]{3,2,1,0:T(8,128)(2,1)S(1)}, u32[]{:S(2)}, u32[]{:S(2)}) collective-permute-start(bf16[16,2,48,256]{3,2,1,0:T(8,128)(2,1)} %get-tuple-element.14.refs_0_), channel_id=1, source_target_pairs={{0,16},{16,32},{32,48},{48,0},{1,17},{17,33},{33,49},{49,1},{2,18}... | collective-permute-start | bytes 2359304 | tf_op jit(solution)/shard_map/ppermute | solution.py:140
  32.8 0.1 pad_add_fusion.place
  32.9 1.5 %collective-permute-start.2 = (bf16[16,2,48,256]{3,2,1,0:T(8,128)(2,1)}, bf16[16,2,48,256]{3,2,1,0:T(8,128)(2,1)}, u32[]{:S(2)}, u32[]{:S(2)}) collective-permute-start(bf16[16,2,48,256]{3,2,1,0:T(8,128)(2,1)} %get-tuple-element.15.refs_1_), channel_id=1, source_target_pairs={{0,48},{16,0},{32,16},{48,32},{1,49},{17,1},{33,17},{49,33},{2,50}... | collective-permute-start | bytes 2359304 | tf_op jit(solution)/shard_map/ppermute | solution.py:140
  34.4 0.0 collective-permute-start.4
  34.4 2.7 %collective-permute-start.5 = (bf16[16,2,48,256]{3,2,1,0:T(8,128)(2,1)}, bf16[16,2,48,256]{3,2,1,0:T(8,128)(2,1)}, u32[]{:S(2)}, u32[]{:S(2)}) collective-permute-start(bf16[16,2,48,256]{3,2,1,0:T(8,128)(2,1)} %get-tuple-element.14.refs_0_), channel_id=1, source_target_pairs={{0,48},{16,0},{32,16},{48,32},{1,49},{17,1},{33,17},{49,33},{2,50}... | collective-permute-start | bytes 2359304 | tf_op jit(solution)/shard_map/ppermute | solution.py:140
  37.1 0.0 copy-done.5
  37.1 1.5 %copy.12 = bf16[2,16,128,256]{3,2,0,1:T(8,128)(2,1)} copy(bf16[2,16,128,256]{3,2,1,0:T(8,128)(2,1)S(1)} %copy-done.5) | data formatting | bytes 4194304 | tf_op jit(solution)/shard_map/optimization_barrier | solution.py:161
  38.6 4.3 %all-to-all-start.1 = ((bf16[16,2,128,256]{3,2,1,0:T(8,128)(2,1)}), bf16[16,2,128,256]{3,2,1,0:T(8,128)(2,1)S(1)}, u32[]{:S(2)}, u32[]{:S(2)}) async-start(bf16[16,2,128,256]{3,2,1,0:T(8,128)(2,1)} %bitcast.13), calls=%async_computation.1 | async-start | bytes 4194304 | tf_op jit(solution)/shard_map/all_to_all | solution.py:144
  42.9 6.4 %collective-permute-done.source = bf16[16,2,48,256]{3,2,1,0:T(8,128)(2,1)S(1)} collective-permute-done((bf16[16,2,48,256]{3,2,1,0:T(8,128)(2,1)}, bf16[16,2,48,256]{3,2,1,0:T(8,128)(2,1)S(1)}, u32[]{:S(2)}, u32[]{:S(2)}) %collective-permute-start) | collective-permute-done | bytes 786464 | tf_op jit(solution)/shard_map/ppermute | solution.py:140
  49.3 0.9 copy-done.2
  50.2 0.1 collective-permute-start.1
  50.3 0.0 collective-permute-done.2.source
  50.3 2.6 %collective-permute-start.3 = (bf16[16,2,48,256]{3,2,1,0:T(8,128)(2,1)}, bf16[16,2,48,256]{3,2,1,0:T(8,128)(2,1)}, u32[]{:S(2)}, u32[]{:S(2)}) collective-permute-start(bf16[16,2,48,256]{3,2,1,0:T(8,128)(2,1)} %shard_map.40.refs_5_), channel_id=1, source_target_pairs={{0,48},{16,0},{32,16},{48,32},{1,49},{17,1},{33,17},{49,33},{2,50}... | collective-permute-start | bytes 2359304 | tf_op jit(solution)/shard_map/ppermute | solution.py:140
  52.9 13.4 %collective-permute-done.4.source = bf16[16,2,48,256]{3,2,1,0:T(8,128)(2,1)} collective-permute-done((bf16[16,2,48,256]{3,2,1,0:T(8,128)(2,1)}, bf16[16,2,48,256]{3,2,1,0:T(8,128)(2,1)}, u32[]{:S(2)}, u32[]{:S(2)}) %collective-permute-start.4) | collective-permute-done | bytes 786464 | tf_op jit(solution)/shard_map/ppermute | solution.py:140
  66.3 0.5 all-to-all-done.1.refs_6_
  66.8 6.4 %collective-permute-start.6 = (bf16[16,2,128,256]{3,2,1,0:T(8,128)(2,1)S(1)}, bf16[16,2,128,256]{3,2,1,0:T(8,128)(2,1)}, u32[]{:S(2)}, u32[]{:S(2)}) collective-permute-start(bf16[16,2,128,256]{3,2,1,0:T(8,128)(2,1)S(1)} %all-to-all-done.1.refs_6_), channel_id=1, source_target_pairs={{0,8},{8,0},{1,9},{9,1},{2,10},{10,2},{3,11},{11,3},{4,12},{12,4},... | collective-permute-start | bytes 6291464 | tf_op jit(solution)/shard_map/ppermute | solution.py:140
  73.3 0.0 collective-permute-done.5.source
  73.3 0.0 copy-done.1
  73.3 1.1 copy-done.3
  74.4 4.9 %shard_map.43 = (bf16[4,2,2,2,2,96,128]{6,5,4,3,2,1,0:T(8,128)(2,1)S(1)}, bf16[2,256,2048]{2,1,0:T(8,128)(2,1)S(1)}) custom-call(s32[3]{0:T(128)S(1)} %pad_add_fusion.place, f32[2,16]{1,0:T(2,128)S(1)} %copy-done.1, bf16[16,2,48,256]{3,2,1,0:T(8,128)(2,1)} %get-tuple-element.14.refs_0_, bf16[16,2,48,256]{3,2,1,0:T(8,128)(2,1)} %get-tuple-element.15.refs_1_, ...), custom_call_target="tpu_custom_call" | custom-call | flops 2415919104 | bytes 1048576 | tf_op jit(solution)/shard_map/pallas_call | solution.py:86
  79.3 0.0 collective-permute-done.6.refs_6_
  79.3 5.5 %shard_map.44 = (bf16[4,2,2,2,2,96,128]{6,5,4,3,2,1,0:T(8,128)(2,1)S(1)}, bf16[2,256,2048]{2,1,0:T(8,128)(2,1)S(1)}) custom-call(s32[3]{0:T(128)S(1)} %pad_add_fusion.place, f32[2,16]{1,0:T(2,128)S(1)} %copy-done.1, bf16[16,2,48,256]{3,2,1,0:T(8,128)(2,1)} %get-tuple-element.14.refs_0_, ...), custom_call_target="tpu_custom_call", output_to_operand_aliasing={{0}: (9, {})} | custom-call | flops 2415919104 | bytes 1048576 | tf_op jit(solution)/shard_map/pallas_call | solution.py:86
  84.8 0.0 collective-permute-done.1.refs_0_
  84.8 0.0 collective-permute-done.3.refs_1_
  84.8 3.0 %shard_map.45 = bf16[4,2,2,2,2,96,128]{6,5,4,3,2,1,0:T(8,128)(2,1)S(1)} custom-call(s32[3]{0:T(128)S(1)} %pad_add_fusion.place, f32[2,16]{1,0:T(2,128)S(1)} %copy-done.1, bf16[16,2,48,256]{3,2,1,0:T(8,128)(2,1)S(1)} %collective-permute-done.1.refs_0_, bf16[16,2,48,256]{3,2,1,0:T(8,128)(2,1)} %collective-permute-done.3.refs_1_, ...), custom_call_target="tpu_custom_call", output_to_operand_aliasing={{}: (6, {})} | custom-call | flops 1610612736 | bytes 1048576 | tf_op jit(solution)/shard_map/pallas_call | solution.py:86
  87.8 27.7 %all_to_all.16 = bf16[32,2,96,128]{3,2,1,0:T(8,128)(2,1)S(1)} all-to-all(bf16[32,2,96,128]{3,2,1,0:T(8,128)(2,1)S(1)} %bitcast.11), channel_id=1, replica_groups=mesh['yh'=2,'x'=4,'c'=2,'yl'=2,'z'=4] {'z','yl','c','yh'}, dimensions={0} | all-to-all | bytes 3145728 | tf_op jit(solution)/shard_map/all_to_all | solution.py:201
  115.5 1.2 shard_map.46
  (10 shorter events, 0.0 us)
Async XLA Ops:
  0.0 1.4 %copy-start = (bf16[2,16,96,256]{3,2,1,0:T(8,128)(2,1)S(1)}, bf16[2,16,96,256]{3,2,1,0:T(8,128)(2,1)}, u32[]{:S(2)}) copy-start(bf16[2,16,96,256]{3,2,1,0:T(8,128)(2,1)} %refs_0_.1) | copy-start | bytes 4718596
  1.5 35.5 %copy-start.5 = (bf16[2,16,128,256]{3,2,1,0:T(8,128)(2,1)S(1)}, bf16[2,16,128,256]{3,2,1,0:T(8,128)(2,1)}, u32[]{:S(2)}) copy-start(bf16[2,16,128,256]{3,2,1,0:T(8,128)(2,1)} %param.3) | copy-start | bytes 6291460
  31.6 17.8 %collective-permute-start = (bf16[16,2,48,256]{3,2,1,0:T(8,128)(2,1)}, bf16[16,2,48,256]{3,2,1,0:T(8,128)(2,1)S(1)}, u32[]{:S(2)}, u32[]{:S(2)}) collective-permute-start(bf16[16,2,48,256]{3,2,1,0:T(8,128)(2,1)} %get-tuple-element.14.refs_0_), channel_id=1, source_target_pairs={{0,16},{16,32},{32,48},{48,0},{1,17},{17,33},{33,49},{49,1},{2,18}... | collective-permute-start | bytes 2359304 | tf_op jit(solution)/shard_map/ppermute | solution.py:140
  32.9 17.4 %collective-permute-start.2 = (bf16[16,2,48,256]{3,2,1,0:T(8,128)(2,1)}, bf16[16,2,48,256]{3,2,1,0:T(8,128)(2,1)}, u32[]{:S(2)}, u32[]{:S(2)}) collective-permute-start(bf16[16,2,48,256]{3,2,1,0:T(8,128)(2,1)} %get-tuple-element.15.refs_1_), channel_id=1, source_target_pairs={{0,48},{16,0},{32,16},{48,32},{1,49},{17,1},{33,17},{49,33},{2,50}... | collective-permute-start | bytes 2359304 | tf_op jit(solution)/shard_map/ppermute | solution.py:140
  34.4 31.9 %collective-permute-start.4 = (bf16[16,2,48,256]{3,2,1,0:T(8,128)(2,1)}, bf16[16,2,48,256]{3,2,1,0:T(8,128)(2,1)}, u32[]{:S(2)}, u32[]{:S(2)}) collective-permute-start(bf16[16,2,48,256]{3,2,1,0:T(8,128)(2,1)} %get-tuple-element.15.refs_1_), channel_id=1, source_target_pairs={{0,16},{16,32},{32,48},{48,0},{1,17},{17,33},{33,49},{49,1},{2,18}... | collective-permute-start | bytes 2359304 | tf_op jit(solution)/shard_map/ppermute | solution.py:140
  34.4 38.9 %collective-permute-start.5 = (bf16[16,2,48,256]{3,2,1,0:T(8,128)(2,1)}, bf16[16,2,48,256]{3,2,1,0:T(8,128)(2,1)}, u32[]{:S(2)}, u32[]{:S(2)}) collective-permute-start(bf16[16,2,48,256]{3,2,1,0:T(8,128)(2,1)} %get-tuple-element.14.refs_0_), channel_id=1, source_target_pairs={{0,48},{16,0},{32,16},{48,32},{1,49},{17,1},{33,17},{49,33},{2,50}... | collective-permute-start | bytes 2359304 | tf_op jit(solution)/shard_map/ppermute | solution.py:140
  38.6 28.3 %all-to-all-start.1 = ((bf16[16,2,128,256]{3,2,1,0:T(8,128)(2,1)}), bf16[16,2,128,256]{3,2,1,0:T(8,128)(2,1)S(1)}, u32[]{:S(2)}, u32[]{:S(2)}) async-start(bf16[16,2,128,256]{3,2,1,0:T(8,128)(2,1)} %bitcast.13), calls=%async_computation.1 | async-start | bytes 4194304 | tf_op jit(solution)/shard_map/all_to_all | solution.py:144
  49.3 0.9 copy-start.2
  50.2 34.6 %collective-permute-start.1 = (bf16[16,2,48,256]{3,2,1,0:T(8,128)(2,1)}, bf16[16,2,48,256]{3,2,1,0:T(8,128)(2,1)S(1)}, u32[]{:S(2)}, u32[]{:S(2)}) collective-permute-start(bf16[16,2,48,256]{3,2,1,0:T(8,128)(2,1)} %shard_map.39.refs_2_), channel_id=1, source_target_pairs={{0,16},{16,32},{32,48},{48,0},{1,17},{17,33},{33,49},{49,1},{2,18}... | collective-permute-start | bytes 2359304 | tf_op jit(solution)/shard_map/ppermute | solution.py:140
  50.3 34.5 %collective-permute-start.3 = (bf16[16,2,48,256]{3,2,1,0:T(8,128)(2,1)}, bf16[16,2,48,256]{3,2,1,0:T(8,128)(2,1)}, u32[]{:S(2)}, u32[]{:S(2)}) collective-permute-start(bf16[16,2,48,256]{3,2,1,0:T(8,128)(2,1)} %shard_map.40.refs_5_), channel_id=1, source_target_pairs={{0,48},{16,0},{32,16},{48,32},{1,49},{17,1},{33,17},{49,33},{2,50}... | collective-permute-start | bytes 2359304 | tf_op jit(solution)/shard_map/ppermute | solution.py:140
  66.3 7.0 %copy-start.1 = (f32[2,16]{1,0:T(2,128)S(1)}, f32[2,16]{1,0:T(2,128)}, u32[]{:S(2)}) copy-start(f32[2,16]{1,0:T(2,128)} %wave.5) | copy-start | bytes 388
  66.8 12.4 %collective-permute-start.6 = (bf16[16,2,128,256]{3,2,1,0:T(8,128)(2,1)S(1)}, bf16[16,2,128,256]{3,2,1,0:T(8,128)(2,1)}, u32[]{:S(2)}, u32[]{:S(2)}) collective-permute-start(bf16[16,2,128,256]{3,2,1,0:T(8,128)(2,1)S(1)} %all-to-all-done.1.refs_6_), channel_id=1, source_target_pairs={{0,8},{8,0},{1,9},{9,1},{2,10},{10,2},{3,11},{11,3},{4,12},{12,4},... | collective-permute-start | bytes 6291464 | tf_op jit(solution)/shard_map/ppermute | solution.py:140
  73.3 1.1 copy-start.3
  74.4 4.9 %copy-start.4 = (bf16[16,2,48,256]{3,2,1,0:T(8,128)(2,1)S(1)}, bf16[16,2,48,256]{3,2,1,0:T(8,128)(2,1)}, u32[]{:S(2)}) copy-start(bf16[16,2,48,256]{3,2,1,0:T(8,128)(2,1)} %shard_map.39.refs_2_) | copy-start | bytes 2359300

commit v8 on v7

--- a/solution.py
+++ b/solution.py
@@ -9,7 +9,7 @@
 from jax.sharding import PartitionSpec as P
 
 FREQUENCY = ("z", "yl", "yh")
-PLACES = ("z", "yl", "c", "yh")
+PLACES = ("z", "yh", "c", "yl")
 ORDER = 2 * 10**10
 
 
@@ -33,10 +33,10 @@
             at += 2 * rows
             s_real = real[:, :shots] - imag[:, shots:]
             s_imag = real[:, shots:] + imag[:, :shots]
-            out[to, half, to_core, p_half, 0, low : low + rows] = (
+            out[to, p_half, to_core, half, 0, low : low + rows] = (
                 w_real * s_real - w_imag * s_imag
             ).astype(out.dtype)
-            out[to, half, to_core, p_half, 1, low : low + rows] = (
+            out[to, p_half, to_core, half, 1, low : low + rows] = (
                 w_real * s_imag + w_imag * s_real
             ).astype(out.dtype)
 
@@ -184,11 +184,12 @@
     (out,) = moves(
         [out],
         [
-            (0, (every, core, every, part), 0, (part, every, every, core))
+            (0, (every, yh, core, every, part), 0, (part, every, every, yh, core))
             for part in range(2)
             for core in range(2)
+            for yh in range(2)
         ],
-        [(2, 8, 2, 2) + out.shape[4:]],
+        [(2, 4, 2, 2, 2) + out.shape[5:]],
         pltpu.VMEM,
         pl.ANY,
     )
@@ -199,7 +200,7 @@
 def back(out):
     out = out.reshape((-1,) + out.shape[4:])
     out = lax.all_to_all(out, PLACES, 0, 0, tiled=True)
-    return out.reshape((8, 2, 2) + out.shape[1:])
+    return out.reshape((4, 2, 2, 2) + out.shape[1:])
 
 
 def solution(mesh):

time: 118 us -> 118 us (level)
  no operation moved by 1% of the time
where the time goes in v8:
time: 118 us; the launch traced here: 117 us
  blocking collectives  57 us (48%)
  waiting for transfers between devices  20.4 us (17%)
  starting transfers between devices  18.9 us (16%)
  Pallas kernels  15.8 us (13%)
  local copies, waits for them, and re-layouts  4.92 us (4%)
    all_to_all x1, blocking collectives, by_frequency(): return lax.all_to_all(value, FREQUENCY, 0, 0, tiled=True)  28.8 us
    all_to_all x1, blocking collectives, back(): out = lax.all_to_all(out, PLACES, 0, 0, tiled=True)  28.2 us
    ppermute x7, waiting for transfers between devices, shift(): lax.ppermute(value, axis, [(i, (i + step) % size) for i in range(size)])  19.8 us
    ppermute x7, starting transfers between devices, shift(): lax.ppermute(value, axis, [(i, (i + step) % size) for i in range(size)])  14.5 us
    pallas_call x3, Pallas kernels, product(): pl.pallas_call(functools.partial(product_kernel, spots, distances, pack,...  13.3 us
    all_to_all x1, starting transfers between devices, by_frequency(): return lax.all_to_all(value, FREQUENCY, 0, 0, tiled=True)  4.33 us
    unnamed x12, local copies, waits for them, and re-layouts  3.43 us
    pallas_call x3, Pallas kernels, moves(): pl.pallas_call(functools.partial(moves_kernel, pairs, len(values)), out_s...  2.49 us
  transfers between devices with their start and end apart: 8, of which 3 were waited for; matrix products, arithmetic and copies ran while one was open for 1% of the time, Pallas kernels for 9%

profile of v8, /device:TPU:1, one launch (start us, length us, event | category | flops | bytes accessed | tf_op | source)
XLA Modules:
  0.0 117.2 jit_solution(15404168909623391444)
XLA Ops:
  0.0 1.4 %copy-done = bf16[2,16,96,256]{3,2,1,0:T(8,128)(2,1)S(1)} copy-done((bf16[2,16,96,256]{3,2,1,0:T(8,128)(2,1)S(1)}, bf16[2,16,96,256]{3,2,1,0:T(8,128)(2,1)}, u32[]{:S(2)}) %copy-start) | copy-done | bytes 1572888
  1.4 0.1 shard_map.37
  1.5 0.0 copy-start.5
  1.6 28.8 %all_to_all.15.refs_0_ = bf16[16,2,96,256]{3,2,1,0:T(8,128)(2,1)S(1)} all-to-all(bf16[16,2,96,256]{3,2,1,0:T(8,128)(2,1)S(1)} %shard_map.37), channel_id=1, replica_groups=mesh['yh'=2,'x'=4,'c'=2,'yl'=2,'z'=4] {'z','yl','yh'}, dimensions={0} | all-to-all | bytes 3145728 | tf_op jit(solution)/shard_map/all_to_all | solution.py:144
  30.4 1.2 shard_map.38
  31.6 1.3 %collective-permute-start = (bf16[16,2,48,256]{3,2,1,0:T(8,128)(2,1)}, bf16[16,2,48,256]{3,2,1,0:T(8,128)(2,1)S(1)}, u32[]{:S(2)}, u32[]{:S(2)}) collective-permute-start(bf16[16,2,48,256]{3,2,1,0:T(8,128)(2,1)} %get-tuple-element.14.refs_0_), channel_id=1, source_target_pairs={{0,16},{16,32},{32,48},{48,0},{1,17},{17,33},{33,49},{49,1},{2,18}... | collective-permute-start | bytes 2359304 | tf_op jit(solution)/shard_map/ppermute | solution.py:140
  32.8 0.1 pad_add_fusion.place
  32.9 1.5 %collective-permute-start.2 = (bf16[16,2,48,256]{3,2,1,0:T(8,128)(2,1)}, bf16[16,2,48,256]{3,2,1,0:T(8,128)(2,1)}, u32[]{:S(2)}, u32[]{:S(2)}) collective-permute-start(bf16[16,2,48,256]{3,2,1,0:T(8,128)(2,1)} %get-tuple-element.15.refs_1_), channel_id=1, source_target_pairs={{0,48},{16,0},{32,16},{48,32},{1,49},{17,1},{33,17},{49,33},{2,50}... | collective-permute-start | bytes 2359304 | tf_op jit(solution)/shard_map/ppermute | solution.py:140
  34.4 0.0 collective-permute-start.4
  34.4 2.7 %collective-permute-start.5 = (bf16[16,2,48,256]{3,2,1,0:T(8,128)(2,1)}, bf16[16,2,48,256]{3,2,1,0:T(8,128)(2,1)}, u32[]{:S(2)}, u32[]{:S(2)}) collective-permute-start(bf16[16,2,48,256]{3,2,1,0:T(8,128)(2,1)} %get-tuple-element.14.refs_0_), channel_id=1, source_target_pairs={{0,48},{16,0},{32,16},{48,32},{1,49},{17,1},{33,17},{49,33},{2,50}... | collective-permute-start | bytes 2359304 | tf_op jit(solution)/shard_map/ppermute | solution.py:140
  37.1 0.0 copy-done.5
  37.1 1.5 %copy.12 = bf16[2,16,128,256]{3,2,0,1:T(8,128)(2,1)} copy(bf16[2,16,128,256]{3,2,1,0:T(8,128)(2,1)S(1)} %copy-done.5) | data formatting | bytes 4194304 | tf_op jit(solution)/shard_map/optimization_barrier | solution.py:161
  38.6 4.3 %all-to-all-start.1 = ((bf16[16,2,128,256]{3,2,1,0:T(8,128)(2,1)}), bf16[16,2,128,256]{3,2,1,0:T(8,128)(2,1)S(1)}, u32[]{:S(2)}, u32[]{:S(2)}) async-start(bf16[16,2,128,256]{3,2,1,0:T(8,128)(2,1)} %bitcast.13), calls=%async_computation.1 | async-start | bytes 4194304 | tf_op jit(solution)/shard_map/all_to_all | solution.py:144
  42.9 6.4 %collective-permute-done.source = bf16[16,2,48,256]{3,2,1,0:T(8,128)(2,1)S(1)} collective-permute-done((bf16[16,2,48,256]{3,2,1,0:T(8,128)(2,1)}, bf16[16,2,48,256]{3,2,1,0:T(8,128)(2,1)S(1)}, u32[]{:S(2)}, u32[]{:S(2)}) %collective-permute-start) | collective-permute-done | bytes 786464 | tf_op jit(solution)/shard_map/ppermute | solution.py:140
  49.3 0.9 copy-done.2
  50.2 0.1 collective-permute-start.1
  50.3 0.0 collective-permute-done.2.source
  50.3 2.6 %collective-permute-start.3 = (bf16[16,2,48,256]{3,2,1,0:T(8,128)(2,1)}, bf16[16,2,48,256]{3,2,1,0:T(8,128)(2,1)}, u32[]{:S(2)}, u32[]{:S(2)}) collective-permute-start(bf16[16,2,48,256]{3,2,1,0:T(8,128)(2,1)} %shard_map.40.refs_5_), channel_id=1, source_target_pairs={{0,48},{16,0},{32,16},{48,32},{1,49},{17,1},{33,17},{49,33},{2,50}... | collective-permute-start | bytes 2359304 | tf_op jit(solution)/shard_map/ppermute | solution.py:140
  52.9 13.4 %collective-permute-done.4.source = bf16[16,2,48,256]{3,2,1,0:T(8,128)(2,1)} collective-permute-done((bf16[16,2,48,256]{3,2,1,0:T(8,128)(2,1)}, bf16[16,2,48,256]{3,2,1,0:T(8,128)(2,1)}, u32[]{:S(2)}, u32[]{:S(2)}) %collective-permute-start.4) | collective-permute-done | bytes 786464 | tf_op jit(solution)/shard_map/ppermute | solution.py:140
  66.3 0.5 all-to-all-done.1.refs_6_
  66.8 6.4 %collective-permute-start.6 = (bf16[16,2,128,256]{3,2,1,0:T(8,128)(2,1)S(1)}, bf16[16,2,128,256]{3,2,1,0:T(8,128)(2,1)}, u32[]{:S(2)}, u32[]{:S(2)}) collective-permute-start(bf16[16,2,128,256]{3,2,1,0:T(8,128)(2,1)S(1)} %all-to-all-done.1.refs_6_), channel_id=1, source_target_pairs={{0,8},{8,0},{1,9},{9,1},{2,10},{10,2},{3,11},{11,3},{4,12},{12,4},... | collective-permute-start | bytes 6291464 | tf_op jit(solution)/shard_map/ppermute | solution.py:140
  73.3 0.0 collective-permute-done.5.source
  73.3 0.0 copy-done.1
  73.3 1.1 copy-done.3
  74.4 4.9 %shard_map.43 = (bf16[4,2,2,2,2,96,128]{6,5,4,3,2,1,0:T(8,128)(2,1)S(1)}, bf16[2,256,2048]{2,1,0:T(8,128)(2,1)S(1)}) custom-call(s32[3]{0:T(128)S(1)} %pad_add_fusion.place, f32[2,16]{1,0:T(2,128)S(1)} %copy-done.1, bf16[16,2,48,256]{3,2,1,0:T(8,128)(2,1)} %get-tuple-element.14.refs_0_, bf16[16,2,48,256]{3,2,1,0:T(8,128)(2,1)} %get-tuple-element.15.refs_1_, ...), custom_call_target="tpu_custom_call" | custom-call | flops 2415919104 | bytes 1048576 | tf_op jit(solution)/shard_map/pallas_call | solution.py:86
  79.3 0.0 collective-permute-done.6.refs_6_
  79.3 5.5 %shard_map.44 = (bf16[4,2,2,2,2,96,128]{6,5,4,3,2,1,0:T(8,128)(2,1)S(1)}, bf16[2,256,2048]{2,1,0:T(8,128)(2,1)S(1)}) custom-call(s32[3]{0:T(128)S(1)} %pad_add_fusion.place, f32[2,16]{1,0:T(2,128)S(1)} %copy-done.1, bf16[16,2,48,256]{3,2,1,0:T(8,128)(2,1)} %get-tuple-element.14.refs_0_, ...), custom_call_target="tpu_custom_call", output_to_operand_aliasing={{0}: (9, {})} | custom-call | flops 2415919104 | bytes 1048576 | tf_op jit(solution)/shard_map/pallas_call | solution.py:86
  84.8 0.0 collective-permute-done.1.refs_0_
  84.8 0.0 collective-permute-done.3.refs_1_
  84.8 3.0 %shard_map.45 = bf16[4,2,2,2,2,96,128]{6,5,4,3,2,1,0:T(8,128)(2,1)S(1)} custom-call(s32[3]{0:T(128)S(1)} %pad_add_fusion.place, f32[2,16]{1,0:T(2,128)S(1)} %copy-done.1, bf16[16,2,48,256]{3,2,1,0:T(8,128)(2,1)S(1)} %collective-permute-done.1.refs_0_, bf16[16,2,48,256]{3,2,1,0:T(8,128)(2,1)} %collective-permute-done.3.refs_1_, ...), custom_call_target="tpu_custom_call", output_to_operand_aliasing={{}: (6, {})} | custom-call | flops 1610612736 | bytes 1048576 | tf_op jit(solution)/shard_map/pallas_call | solution.py:86
  87.8 28.2 %all_to_all.16 = bf16[32,2,96,128]{3,2,1,0:T(8,128)(2,1)S(1)} all-to-all(bf16[32,2,96,128]{3,2,1,0:T(8,128)(2,1)S(1)} %bitcast.11), channel_id=1, replica_groups=mesh['yh'=2,'x'=4,'c'=2,'yl'=2,'z'=4] {'z','yh','c','yl'}, dimensions={0} | all-to-all | bytes 3145728 | tf_op jit(solution)/shard_map/all_to_all | solution.py:202
  116.0 1.2 %shard_map.46 = bf16[2,4,2,2,2,96,128]{6,5,4,3,2,1,0:T(8,128)(2,1)} custom-call(bf16[4,2,2,2,2,96,128]{6,5,4,3,2,1,0:T(8,128)(2,1)S(1)} %bitcast.12), custom_call_target="tpu_custom_call" | custom-call | bytes 3145728 | tf_op jit(solution)/shard_map/pallas_call | solution.py:111
  (10 shorter events, 0.0 us)
Async XLA Ops:
  0.0 1.4 %copy-start = (bf16[2,16,96,256]{3,2,1,0:T(8,128)(2,1)S(1)}, bf16[2,16,96,256]{3,2,1,0:T(8,128)(2,1)}, u32[]{:S(2)}) copy-start(bf16[2,16,96,256]{3,2,1,0:T(8,128)(2,1)} %refs_0_.1) | copy-start | bytes 4718596
  1.5 35.5 %copy-start.5 = (bf16[2,16,128,256]{3,2,1,0:T(8,128)(2,1)S(1)}, bf16[2,16,128,256]{3,2,1,0:T(8,128)(2,1)}, u32[]{:S(2)}) copy-start(bf16[2,16,128,256]{3,2,1,0:T(8,128)(2,1)} %param.3) | copy-start | bytes 6291460
  31.6 17.8 %collective-permute-start = (bf16[16,2,48,256]{3,2,1,0:T(8,128)(2,1)}, bf16[16,2,48,256]{3,2,1,0:T(8,128)(2,1)S(1)}, u32[]{:S(2)}, u32[]{:S(2)}) collective-permute-start(bf16[16,2,48,256]{3,2,1,0:T(8,128)(2,1)} %get-tuple-element.14.refs_0_), channel_id=1, source_target_pairs={{0,16},{16,32},{32,48},{48,0},{1,17},{17,33},{33,49},{49,1},{2,18}... | collective-permute-start | bytes 2359304 | tf_op jit(solution)/shard_map/ppermute | solution.py:140
  32.9 17.4 %collective-permute-start.2 = (bf16[16,2,48,256]{3,2,1,0:T(8,128)(2,1)}, bf16[16,2,48,256]{3,2,1,0:T(8,128)(2,1)}, u32[]{:S(2)}, u32[]{:S(2)}) collective-permute-start(bf16[16,2,48,256]{3,2,1,0:T(8,128)(2,1)} %get-tuple-element.15.refs_1_), channel_id=1, source_target_pairs={{0,48},{16,0},{32,16},{48,32},{1,49},{17,1},{33,17},{49,33},{2,50}... | collective-permute-start | bytes 2359304 | tf_op jit(solution)/shard_map/ppermute | solution.py:140
  34.4 31.9 %collective-permute-start.4 = (bf16[16,2,48,256]{3,2,1,0:T(8,128)(2,1)}, bf16[16,2,48,256]{3,2,1,0:T(8,128)(2,1)}, u32[]{:S(2)}, u32[]{:S(2)}) collective-permute-start(bf16[16,2,48,256]{3,2,1,0:T(8,128)(2,1)} %get-tuple-element.15.refs_1_), channel_id=1, source_target_pairs={{0,16},{16,32},{32,48},{48,0},{1,17},{17,33},{33,49},{49,1},{2,18}... | collective-permute-start | bytes 2359304 | tf_op jit(solution)/shard_map/ppermute | solution.py:140
  34.4 38.9 %collective-permute-start.5 = (bf16[16,2,48,256]{3,2,1,0:T(8,128)(2,1)}, bf16[16,2,48,256]{3,2,1,0:T(8,128)(2,1)}, u32[]{:S(2)}, u32[]{:S(2)}) collective-permute-start(bf16[16,2,48,256]{3,2,1,0:T(8,128)(2,1)} %get-tuple-element.14.refs_0_), channel_id=1, source_target_pairs={{0,48},{16,0},{32,16},{48,32},{1,49},{17,1},{33,17},{49,33},{2,50}... | collective-permute-start | bytes 2359304 | tf_op jit(solution)/shard_map/ppermute | solution.py:140
  38.6 28.3 %all-to-all-start.1 = ((bf16[16,2,128,256]{3,2,1,0:T(8,128)(2,1)}), bf16[16,2,128,256]{3,2,1,0:T(8,128)(2,1)S(1)}, u32[]{:S(2)}, u32[]{:S(2)}) async-start(bf16[16,2,128,256]{3,2,1,0:T(8,128)(2,1)} %bitcast.13), calls=%async_computation.1 | async-start | bytes 4194304 | tf_op jit(solution)/shard_map/all_to_all | solution.py:144
  49.3 0.9 copy-start.2
  50.2 34.6 %collective-permute-start.1 = (bf16[16,2,48,256]{3,2,1,0:T(8,128)(2,1)}, bf16[16,2,48,256]{3,2,1,0:T(8,128)(2,1)S(1)}, u32[]{:S(2)}, u32[]{:S(2)}) collective-permute-start(bf16[16,2,48,256]{3,2,1,0:T(8,128)(2,1)} %shard_map.39.refs_2_), channel_id=1, source_target_pairs={{0,16},{16,32},{32,48},{48,0},{1,17},{17,33},{33,49},{49,1},{2,18}... | collective-permute-start | bytes 2359304 | tf_op jit(solution)/shard_map/ppermute | solution.py:140
  50.3 34.5 %collective-permute-start.3 = (bf16[16,2,48,256]{3,2,1,0:T(8,128)(2,1)}, bf16[16,2,48,256]{3,2,1,0:T(8,128)(2,1)}, u32[]{:S(2)}, u32[]{:S(2)}) collective-permute-start(bf16[16,2,48,256]{3,2,1,0:T(8,128)(2,1)} %shard_map.40.refs_5_), channel_id=1, source_target_pairs={{0,48},{16,0},{32,16},{48,32},{1,49},{17,1},{33,17},{49,33},{2,50}... | collective-permute-start | bytes 2359304 | tf_op jit(solution)/shard_map/ppermute | solution.py:140
  66.3 7.0 %copy-start.1 = (f32[2,16]{1,0:T(2,128)S(1)}, f32[2,16]{1,0:T(2,128)}, u32[]{:S(2)}) copy-start(f32[2,16]{1,0:T(2,128)} %wave.5) | copy-start | bytes 388
  66.8 12.4 %collective-permute-start.6 = (bf16[16,2,128,256]{3,2,1,0:T(8,128)(2,1)S(1)}, bf16[16,2,128,256]{3,2,1,0:T(8,128)(2,1)}, u32[]{:S(2)}, u32[]{:S(2)}) collective-permute-start(bf16[16,2,128,256]{3,2,1,0:T(8,128)(2,1)S(1)} %all-to-all-done.1.refs_6_), channel_id=1, source_target_pairs={{0,8},{8,0},{1,9},{9,1},{2,10},{10,2},{3,11},{11,3},{4,12},{12,4},... | collective-permute-start | bytes 6291464 | tf_op jit(solution)/shard_map/ppermute | solution.py:140
  73.3 1.1 copy-start.3
  74.4 4.9 %copy-start.4 = (bf16[16,2,48,256]{3,2,1,0:T(8,128)(2,1)S(1)}, bf16[16,2,48,256]{3,2,1,0:T(8,128)(2,1)}, u32[]{:S(2)}) copy-start(bf16[16,2,48,256]{3,2,1,0:T(8,128)(2,1)} %shard_map.39.refs_2_) | copy-start | bytes 2359300

commit v9 on v7

--- a/solution.py
+++ b/solution.py
@@ -45,6 +45,30 @@
     pieces, refs = refs[: len(spots)], refs[len(spots) :]
     factors = refs[: len(distances)]
     out, *packed = refs[len(distances) + earlier :]
+    if not pack:
+        left_factor = jnp.concatenate(
+            [rows_of(piece, half) for piece in pieces for half in range(2)], axis=0
+        )
+        rights = []
+        for distance, factor in zip(distances, factors):
+            for p_half in range(2):
+                right_factor = rows_of(factor, p_half) if len(factor.shape) == 4 else factor[p_half]
+                if pack:
+                    packed[distance - distances[0]][p_half] = right_factor
+                rights.append(right_factor)
+        terms = lax.dot_general(
+            left_factor,
+            jnp.concatenate(rights, axis=0),
+            (((1,), (1,)), ((), ())),
+            preferred_element_type=jnp.float32,
+        )
+        width = rights[0].shape[0]
+        for i, distance in enumerate(distances):
+            to_core = lax.rem(place[1] + distance, 2)
+            for p_half in range(2):
+                at = (2 * i + p_half) * width
+                emit(terms[:, at : at + width], spots, pieces, p_half, to_core, place, wave, out)
+        return
     for distance, factor in zip(distances, factors):
         to_core = lax.rem(place[1] + distance, 2)
         for p_half in range(2):

time: 118 us -> 118 us (level)
  no operation moved by 1% of the time
where the time goes in v9:
time: 118 us; the launch traced here: 117 us
  blocking collectives  56.6 us (48%)
  waiting for transfers between devices  20.4 us (17%)
  starting transfers between devices  18.9 us (16%)
  Pallas kernels  15.8 us (13%)
  local copies, waits for them, and re-layouts  4.92 us (4%)
    all_to_all x1, blocking collectives, by_frequency(): return lax.all_to_all(value, FREQUENCY, 0, 0, tiled=True)  28.8 us
    all_to_all x1, blocking collectives, back(): out = lax.all_to_all(out, PLACES, 0, 0, tiled=True)  27.7 us
    ppermute x7, waiting for transfers between devices, shift(): lax.ppermute(value, axis, [(i, (i + step) % size) for i in range(size)])  19.8 us
    ppermute x7, starting transfers between devices, shift(): lax.ppermute(value, axis, [(i, (i + step) % size) for i in range(size)])  14.5 us
    pallas_call x3, Pallas kernels, product(): pl.pallas_call(functools.partial(product_kernel, spots, distances, pack,...  13.3 us
    all_to_all x1, starting transfers between devices, by_frequency(): return lax.all_to_all(value, FREQUENCY, 0, 0, tiled=True)  4.33 us
    unnamed x12, local copies, waits for them, and re-layouts  3.43 us
    pallas_call x3, Pallas kernels, moves(): pl.pallas_call(functools.partial(moves_kernel, pairs, len(values)), out_s...  2.46 us
  transfers between devices with their start and end apart: 8, of which 3 were waited for; matrix products, arithmetic and copies ran while one was open for 1% of the time, Pallas kernels for 9%

profile of v9, /device:TPU:1, one launch (start us, length us, event | category | flops | bytes accessed | tf_op | source)
XLA Modules:
  0.0 116.7 jit_solution(13478074599658643013)
XLA Ops:
  0.0 1.4 %copy-done = bf16[2,16,96,256]{3,2,1,0:T(8,128)(2,1)S(1)} copy-done((bf16[2,16,96,256]{3,2,1,0:T(8,128)(2,1)S(1)}, bf16[2,16,96,256]{3,2,1,0:T(8,128)(2,1)}, u32[]{:S(2)}) %copy-start) | copy-done | bytes 1572888
  1.4 0.1 shard_map.37
  1.5 0.0 copy-start.5
  1.6 28.8 %all_to_all.15.refs_0_ = bf16[16,2,96,256]{3,2,1,0:T(8,128)(2,1)S(1)} all-to-all(bf16[16,2,96,256]{3,2,1,0:T(8,128)(2,1)S(1)} %shard_map.37), channel_id=1, replica_groups=mesh['yh'=2,'x'=4,'c'=2,'yl'=2,'z'=4] {'z','yl','yh'}, dimensions={0} | all-to-all | bytes 3145728 | tf_op jit(solution)/shard_map/all_to_all | solution.py:168
  30.4 1.2 shard_map.38
  31.6 1.3 %collective-permute-start = (bf16[16,2,48,256]{3,2,1,0:T(8,128)(2,1)}, bf16[16,2,48,256]{3,2,1,0:T(8,128)(2,1)S(1)}, u32[]{:S(2)}, u32[]{:S(2)}) collective-permute-start(bf16[16,2,48,256]{3,2,1,0:T(8,128)(2,1)} %get-tuple-element.14.refs_0_), channel_id=1, source_target_pairs={{0,16},{16,32},{32,48},{48,0},{1,17},{17,33},{33,49},{49,1},{2,18}... | collective-permute-start | bytes 2359304 | tf_op jit(solution)/shard_map/ppermute | solution.py:164
  32.8 0.1 pad_add_fusion.place
  32.9 1.5 %collective-permute-start.2 = (bf16[16,2,48,256]{3,2,1,0:T(8,128)(2,1)}, bf16[16,2,48,256]{3,2,1,0:T(8,128)(2,1)}, u32[]{:S(2)}, u32[]{:S(2)}) collective-permute-start(bf16[16,2,48,256]{3,2,1,0:T(8,128)(2,1)} %get-tuple-element.15.refs_1_), channel_id=1, source_target_pairs={{0,48},{16,0},{32,16},{48,32},{1,49},{17,1},{33,17},{49,33},{2,50}... | collective-permute-start | bytes 2359304 | tf_op jit(solution)/shard_map/ppermute | solution.py:164
  34.4 0.0 collective-permute-start.4
  34.4 2.7 %collective-permute-start.5 = (bf16[16,2,48,256]{3,2,1,0:T(8,128)(2,1)}, bf16[16,2,48,256]{3,2,1,0:T(8,128)(2,1)}, u32[]{:S(2)}, u32[]{:S(2)}) collective-permute-start(bf16[16,2,48,256]{3,2,1,0:T(8,128)(2,1)} %get-tuple-element.14.refs_0_), channel_id=1, source_target_pairs={{0,48},{16,0},{32,16},{48,32},{1,49},{17,1},{33,17},{49,33},{2,50}... | collective-permute-start | bytes 2359304 | tf_op jit(solution)/shard_map/ppermute | solution.py:164
  37.1 0.0 copy-done.5
  37.1 1.5 %copy.12 = bf16[2,16,128,256]{3,2,0,1:T(8,128)(2,1)} copy(bf16[2,16,128,256]{3,2,1,0:T(8,128)(2,1)S(1)} %copy-done.5) | data formatting | bytes 4194304 | tf_op jit(solution)/shard_map/optimization_barrier | solution.py:185
  38.6 4.3 %all-to-all-start.1 = ((bf16[16,2,128,256]{3,2,1,0:T(8,128)(2,1)}), bf16[16,2,128,256]{3,2,1,0:T(8,128)(2,1)S(1)}, u32[]{:S(2)}, u32[]{:S(2)}) async-start(bf16[16,2,128,256]{3,2,1,0:T(8,128)(2,1)} %bitcast.13), calls=%async_computation.1 | async-start | bytes 4194304 | tf_op jit(solution)/shard_map/all_to_all | solution.py:168
  42.9 6.4 %collective-permute-done.source = bf16[16,2,48,256]{3,2,1,0:T(8,128)(2,1)S(1)} collective-permute-done((bf16[16,2,48,256]{3,2,1,0:T(8,128)(2,1)}, bf16[16,2,48,256]{3,2,1,0:T(8,128)(2,1)S(1)}, u32[]{:S(2)}, u32[]{:S(2)}) %collective-permute-start) | collective-permute-done | bytes 786464 | tf_op jit(solution)/shard_map/ppermute | solution.py:164
  49.3 0.9 copy-done.2
  50.2 0.1 collective-permute-start.1
  50.3 0.0 collective-permute-done.2.source
  50.3 2.6 %collective-permute-start.3 = (bf16[16,2,48,256]{3,2,1,0:T(8,128)(2,1)}, bf16[16,2,48,256]{3,2,1,0:T(8,128)(2,1)}, u32[]{:S(2)}, u32[]{:S(2)}) collective-permute-start(bf16[16,2,48,256]{3,2,1,0:T(8,128)(2,1)} %shard_map.40.refs_5_), channel_id=1, source_target_pairs={{0,48},{16,0},{32,16},{48,32},{1,49},{17,1},{33,17},{49,33},{2,50}... | collective-permute-start | bytes 2359304 | tf_op jit(solution)/shard_map/ppermute | solution.py:164
  52.9 13.4 %collective-permute-done.4.source = bf16[16,2,48,256]{3,2,1,0:T(8,128)(2,1)} collective-permute-done((bf16[16,2,48,256]{3,2,1,0:T(8,128)(2,1)}, bf16[16,2,48,256]{3,2,1,0:T(8,128)(2,1)}, u32[]{:S(2)}, u32[]{:S(2)}) %collective-permute-start.4) | collective-permute-done | bytes 786464 | tf_op jit(solution)/shard_map/ppermute | solution.py:164
  66.3 0.5 all-to-all-done.1.refs_6_
  66.8 6.4 %collective-permute-start.6 = (bf16[16,2,128,256]{3,2,1,0:T(8,128)(2,1)S(1)}, bf16[16,2,128,256]{3,2,1,0:T(8,128)(2,1)}, u32[]{:S(2)}, u32[]{:S(2)}) collective-permute-start(bf16[16,2,128,256]{3,2,1,0:T(8,128)(2,1)S(1)} %all-to-all-done.1.refs_6_), channel_id=1, source_target_pairs={{0,8},{8,0},{1,9},{9,1},{2,10},{10,2},{3,11},{11,3},{4,12},{12,4},... | collective-permute-start | bytes 6291464 | tf_op jit(solution)/shard_map/ppermute | solution.py:164
  73.3 0.0 collective-permute-done.5.source
  73.3 0.0 copy-done.1
  73.3 1.1 copy-done.3
  74.4 4.9 %shard_map.43 = (bf16[4,2,2,2,2,96,128]{6,5,4,3,2,1,0:T(8,128)(2,1)S(1)}, bf16[2,256,2048]{2,1,0:T(8,128)(2,1)S(1)}) custom-call(s32[3]{0:T(128)S(1)} %pad_add_fusion.place, f32[2,16]{1,0:T(2,128)S(1)} %copy-done.1, bf16[16,2,48,256]{3,2,1,0:T(8,128)(2,1)} %get-tuple-element.14.refs_0_, bf16[16,2,48,256]{3,2,1,0:T(8,128)(2,1)} %get-tuple-element.15.refs_1_, ...), custom_call_target="tpu_custom_call" | custom-call | flops 2415919104 | bytes 1048576 | tf_op jit(solution)/shard_map/pallas_call | solution.py:110
  79.3 0.0 collective-permute-done.6.refs_6_
  79.3 5.5 %shard_map.44 = (bf16[4,2,2,2,2,96,128]{6,5,4,3,2,1,0:T(8,128)(2,1)S(1)}, bf16[2,256,2048]{2,1,0:T(8,128)(2,1)S(1)}) custom-call(s32[3]{0:T(128)S(1)} %pad_add_fusion.place, f32[2,16]{1,0:T(2,128)S(1)} %copy-done.1, bf16[16,2,48,256]{3,2,1,0:T(8,128)(2,1)} %get-tuple-element.14.refs_0_, ...), custom_call_target="tpu_custom_call", output_to_operand_aliasing={{0}: (9, {})} | custom-call | flops 2415919104 | bytes 1048576 | tf_op jit(solution)/shard_map/pallas_call | solution.py:110
  84.8 0.0 collective-permute-done.1.refs_0_
  84.8 0.0 collective-permute-done.3.refs_1_
  84.8 3.0 %shard_map.45 = bf16[4,2,2,2,2,96,128]{6,5,4,3,2,1,0:T(8,128)(2,1)S(1)} custom-call(s32[3]{0:T(128)S(1)} %pad_add_fusion.place, f32[2,16]{1,0:T(2,128)S(1)} %copy-done.1, bf16[16,2,48,256]{3,2,1,0:T(8,128)(2,1)S(1)} %collective-permute-done.1.refs_0_, bf16[16,2,48,256]{3,2,1,0:T(8,128)(2,1)} %collective-permute-done.3.refs_1_, ...), custom_call_target="tpu_custom_call", output_to_operand_aliasing={{}: (6, {})} | custom-call | flops 1610612736 | bytes 1048576 | tf_op jit(solution)/shard_map/pallas_call | solution.py:110
  87.8 27.7 %all_to_all.16 = bf16[32,2,96,128]{3,2,1,0:T(8,128)(2,1)S(1)} all-to-all(bf16[32,2,96,128]{3,2,1,0:T(8,128)(2,1)S(1)} %bitcast.11), channel_id=1, replica_groups=mesh['yh'=2,'x'=4,'c'=2,'yl'=2,'z'=4] {'z','yl','c','yh'}, dimensions={0} | all-to-all | bytes 3145728 | tf_op jit(solution)/shard_map/all_to_all | solution.py:225
  115.5 1.2 shard_map.46
  (10 shorter events, 0.0 us)
Async XLA Ops:
  0.0 1.4 %copy-start = (bf16[2,16,96,256]{3,2,1,0:T(8,128)(2,1)S(1)}, bf16[2,16,96,256]{3,2,1,0:T(8,128)(2,1)}, u32[]{:S(2)}) copy-start(bf16[2,16,96,256]{3,2,1,0:T(8,128)(2,1)} %refs_0_.1) | copy-start | bytes 4718596
  1.5 35.5 %copy-start.5 = (bf16[2,16,128,256]{3,2,1,0:T(8,128)(2,1)S(1)}, bf16[2,16,128,256]{3,2,1,0:T(8,128)(2,1)}, u32[]{:S(2)}) copy-start(bf16[2,16,128,256]{3,2,1,0:T(8,128)(2,1)} %param.3) | copy-start | bytes 6291460
  31.6 17.8 %collective-permute-start = (bf16[16,2,48,256]{3,2,1,0:T(8,128)(2,1)}, bf16[16,2,48,256]{3,2,1,0:T(8,128)(2,1)S(1)}, u32[]{:S(2)}, u32[]{:S(2)}) collective-permute-start(bf16[16,2,48,256]{3,2,1,0:T(8,128)(2,1)} %get-tuple-element.14.refs_0_), channel_id=1, source_target_pairs={{0,16},{16,32},{32,48},{48,0},{1,17},{17,33},{33,49},{49,1},{2,18}... | collective-permute-start | bytes 2359304 | tf_op jit(solution)/shard_map/ppermute | solution.py:164
  32.9 17.4 %collective-permute-start.2 = (bf16[16,2,48,256]{3,2,1,0:T(8,128)(2,1)}, bf16[16,2,48,256]{3,2,1,0:T(8,128)(2,1)}, u32[]{:S(2)}, u32[]{:S(2)}) collective-permute-start(bf16[16,2,48,256]{3,2,1,0:T(8,128)(2,1)} %get-tuple-element.15.refs_1_), channel_id=1, source_target_pairs={{0,48},{16,0},{32,16},{48,32},{1,49},{17,1},{33,17},{49,33},{2,50}... | collective-permute-start | bytes 2359304 | tf_op jit(solution)/shard_map/ppermute | solution.py:164
  34.4 31.9 %collective-permute-start.4 = (bf16[16,2,48,256]{3,2,1,0:T(8,128)(2,1)}, bf16[16,2,48,256]{3,2,1,0:T(8,128)(2,1)}, u32[]{:S(2)}, u32[]{:S(2)}) collective-permute-start(bf16[16,2,48,256]{3,2,1,0:T(8,128)(2,1)} %get-tuple-element.15.refs_1_), channel_id=1, source_target_pairs={{0,16},{16,32},{32,48},{48,0},{1,17},{17,33},{33,49},{49,1},{2,18}... | collective-permute-start | bytes 2359304 | tf_op jit(solution)/shard_map/ppermute | solution.py:164
  34.4 38.9 %collective-permute-start.5 = (bf16[16,2,48,256]{3,2,1,0:T(8,128)(2,1)}, bf16[16,2,48,256]{3,2,1,0:T(8,128)(2,1)}, u32[]{:S(2)}, u32[]{:S(2)}) collective-permute-start(bf16[16,2,48,256]{3,2,1,0:T(8,128)(2,1)} %get-tuple-element.14.refs_0_), channel_id=1, source_target_pairs={{0,48},{16,0},{32,16},{48,32},{1,49},{17,1},{33,17},{49,33},{2,50}... | collective-permute-start | bytes 2359304 | tf_op jit(solution)/shard_map/ppermute | solution.py:164
  38.6 28.3 %all-to-all-start.1 = ((bf16[16,2,128,256]{3,2,1,0:T(8,128)(2,1)}), bf16[16,2,128,256]{3,2,1,0:T(8,128)(2,1)S(1)}, u32[]{:S(2)}, u32[]{:S(2)}) async-start(bf16[16,2,128,256]{3,2,1,0:T(8,128)(2,1)} %bitcast.13), calls=%async_computation.1 | async-start | bytes 4194304 | tf_op jit(solution)/shard_map/all_to_all | solution.py:168
  49.3 0.9 copy-start.2
  50.2 34.6 %collective-permute-start.1 = (bf16[16,2,48,256]{3,2,1,0:T(8,128)(2,1)}, bf16[16,2,48,256]{3,2,1,0:T(8,128)(2,1)S(1)}, u32[]{:S(2)}, u32[]{:S(2)}) collective-permute-start(bf16[16,2,48,256]{3,2,1,0:T(8,128)(2,1)} %shard_map.39.refs_2_), channel_id=1, source_target_pairs={{0,16},{16,32},{32,48},{48,0},{1,17},{17,33},{33,49},{49,1},{2,18}... | collective-permute-start | bytes 2359304 | tf_op jit(solution)/shard_map/ppermute | solution.py:164
  50.3 34.5 %collective-permute-start.3 = (bf16[16,2,48,256]{3,2,1,0:T(8,128)(2,1)}, bf16[16,2,48,256]{3,2,1,0:T(8,128)(2,1)}, u32[]{:S(2)}, u32[]{:S(2)}) collective-permute-start(bf16[16,2,48,256]{3,2,1,0:T(8,128)(2,1)} %shard_map.40.refs_5_), channel_id=1, source_target_pairs={{0,48},{16,0},{32,16},{48,32},{1,49},{17,1},{33,17},{49,33},{2,50}... | collective-permute-start | bytes 2359304 | tf_op jit(solution)/shard_map/ppermute | solution.py:164
  66.3 7.0 %copy-start.1 = (f32[2,16]{1,0:T(2,128)S(1)}, f32[2,16]{1,0:T(2,128)}, u32[]{:S(2)}) copy-start(f32[2,16]{1,0:T(2,128)} %wave.5) | copy-start | bytes 388
  66.8 12.4 %collective-permute-start.6 = (bf16[16,2,128,256]{3,2,1,0:T(8,128)(2,1)S(1)}, bf16[16,2,128,256]{3,2,1,0:T(8,128)(2,1)}, u32[]{:S(2)}, u32[]{:S(2)}) collective-permute-start(bf16[16,2,128,256]{3,2,1,0:T(8,128)(2,1)S(1)} %all-to-all-done.1.refs_6_), channel_id=1, source_target_pairs={{0,8},{8,0},{1,9},{9,1},{2,10},{10,2},{3,11},{11,3},{4,12},{12,4},... | collective-permute-start | bytes 6291464 | tf_op jit(solution)/shard_map/ppermute | solution.py:164
  73.3 1.1 copy-start.3
  74.4 4.9 %copy-start.4 = (bf16[16,2,48,256]{3,2,1,0:T(8,128)(2,1)S(1)}, bf16[16,2,48,256]{3,2,1,0:T(8,128)(2,1)}, u32[]{:S(2)}) copy-start(bf16[16,2,48,256]{3,2,1,0:T(8,128)(2,1)} %shard_map.39.refs_2_) | copy-start | bytes 2359300

commit v10 on v9

--- a/solution.py
+++ b/solution.py
@@ -9,7 +9,7 @@
 from jax.sharding import PartitionSpec as P
 
 FREQUENCY = ("z", "yl", "yh")
-PLACES = ("z", "yl", "c", "yh")
+PLACES = ("z", "yh", "c", "yl")
 ORDER = 2 * 10**10
 
 
@@ -33,10 +33,10 @@
             at += 2 * rows
             s_real = real[:, :shots] - imag[:, shots:]
             s_imag = real[:, shots:] + imag[:, :shots]
-            out[to, half, to_core, p_half, 0, low : low + rows] = (
+            out[to, p_half, to_core, half, 0, low : low + rows] = (
                 w_real * s_real - w_imag * s_imag
             ).astype(out.dtype)
-            out[to, half, to_core, p_half, 1, low : low + rows] = (
+            out[to, p_half, to_core, half, 1, low : low + rows] = (
                 w_real * s_imag + w_imag * s_real
             ).astype(out.dtype)
 
@@ -208,11 +208,12 @@
     (out,) = moves(
         [out],
         [
-            (0, (every, core, every, part), 0, (part, every, every, core))
+            (0, (every, yh, core, every, part), 0, (part, every, every, yh, core))
             for part in range(2)
             for core in range(2)
+            for yh in range(2)
         ],
-        [(2, 8, 2, 2) + out.shape[4:]],
+        [(2, 4, 2, 2, 2) + out.shape[5:]],
         pltpu.VMEM,
         pl.ANY,
     )
@@ -223,7 +224,7 @@
 def back(out):
     out = out.reshape((-1,) + out.shape[4:])
     out = lax.all_to_all(out, PLACES, 0, 0, tiled=True)
-    return out.reshape((8, 2, 2) + out.shape[1:])
+    return out.reshape((4, 2, 2, 2) + out.shape[1:])
 
 
 def solution(mesh):

time: 118 us -> 118 us (level)
  no operation moved by 1% of the time
where the time goes in v10:
time: 118 us; the launch traced here: 117 us
  blocking collectives  57 us (48%)
  waiting for transfers between devices  20.4 us (17%)
  starting transfers between devices  18.9 us (16%)
  Pallas kernels  15.8 us (13%)
  local copies, waits for them, and re-layouts  4.92 us (4%)
    all_to_all x1, blocking collectives, by_frequency(): return lax.all_to_all(value, FREQUENCY, 0, 0, tiled=True)  28.8 us
    all_to_all x1, blocking collectives, back(): out = lax.all_to_all(out, PLACES, 0, 0, tiled=True)  28.2 us
    ppermute x7, waiting for transfers between devices, shift(): lax.ppermute(value, axis, [(i, (i + step) % size) for i in range(size)])  19.8 us
    ppermute x7, starting transfers between devices, shift(): lax.ppermute(value, axis, [(i, (i + step) % size) for i in range(size)])  14.5 us
    pallas_call x3, Pallas kernels, product(): pl.pallas_call(functools.partial(product_kernel, spots, distances, pack,...  13.3 us
    all_to_all x1, starting transfers between devices, by_frequency(): return lax.all_to_all(value, FREQUENCY, 0, 0, tiled=True)  4.33 us
    unnamed x12, local copies, waits for them, and re-layouts  3.43 us
    pallas_call x3, Pallas kernels, moves(): pl.pallas_call(functools.partial(moves_kernel, pairs, len(values)), out_s...  2.49 us
  transfers between devices with their start and end apart: 8, of which 3 were waited for; matrix products, arithmetic and copies ran while one was open for 1% of the time, Pallas kernels for 9%

profile of v10, /device:TPU:1, one launch (start us, length us, event | category | flops | bytes accessed | tf_op | source)
XLA Modules:
  0.0 117.2 jit_solution(16583452846867615462)
XLA Ops:
  0.0 1.4 %copy-done = bf16[2,16,96,256]{3,2,1,0:T(8,128)(2,1)S(1)} copy-done((bf16[2,16,96,256]{3,2,1,0:T(8,128)(2,1)S(1)}, bf16[2,16,96,256]{3,2,1,0:T(8,128)(2,1)}, u32[]{:S(2)}) %copy-start) | copy-done | bytes 1572888
  1.4 0.1 shard_map.37
  1.5 0.0 copy-start.5
  1.6 28.8 %all_to_all.15.refs_0_ = bf16[16,2,96,256]{3,2,1,0:T(8,128)(2,1)S(1)} all-to-all(bf16[16,2,96,256]{3,2,1,0:T(8,128)(2,1)S(1)} %shard_map.37), channel_id=1, replica_groups=mesh['yh'=2,'x'=4,'c'=2,'yl'=2,'z'=4] {'z','yl','yh'}, dimensions={0} | all-to-all | bytes 3145728 | tf_op jit(solution)/shard_map/all_to_all | solution.py:168
  30.4 1.2 shard_map.38
  31.6 1.3 %collective-permute-start = (bf16[16,2,48,256]{3,2,1,0:T(8,128)(2,1)}, bf16[16,2,48,256]{3,2,1,0:T(8,128)(2,1)S(1)}, u32[]{:S(2)}, u32[]{:S(2)}) collective-permute-start(bf16[16,2,48,256]{3,2,1,0:T(8,128)(2,1)} %get-tuple-element.14.refs_0_), channel_id=1, source_target_pairs={{0,16},{16,32},{32,48},{48,0},{1,17},{17,33},{33,49},{49,1},{2,18}... | collective-permute-start | bytes 2359304 | tf_op jit(solution)/shard_map/ppermute | solution.py:164
  32.8 0.1 pad_add_fusion.place
  32.9 1.5 %collective-permute-start.2 = (bf16[16,2,48,256]{3,2,1,0:T(8,128)(2,1)}, bf16[16,2,48,256]{3,2,1,0:T(8,128)(2,1)}, u32[]{:S(2)}, u32[]{:S(2)}) collective-permute-start(bf16[16,2,48,256]{3,2,1,0:T(8,128)(2,1)} %get-tuple-element.15.refs_1_), channel_id=1, source_target_pairs={{0,48},{16,0},{32,16},{48,32},{1,49},{17,1},{33,17},{49,33},{2,50}... | collective-permute-start | bytes 2359304 | tf_op jit(solution)/shard_map/ppermute | solution.py:164
  34.4 0.0 collective-permute-start.4
  34.4 2.7 %collective-permute-start.5 = (bf16[16,2,48,256]{3,2,1,0:T(8,128)(2,1)}, bf16[16,2,48,256]{3,2,1,0:T(8,128)(2,1)}, u32[]{:S(2)}, u32[]{:S(2)}) collective-permute-start(bf16[16,2,48,256]{3,2,1,0:T(8,128)(2,1)} %get-tuple-element.14.refs_0_), channel_id=1, source_target_pairs={{0,48},{16,0},{32,16},{48,32},{1,49},{17,1},{33,17},{49,33},{2,50}... | collective-permute-start | bytes 2359304 | tf_op jit(solution)/shard_map/ppermute | solution.py:164
  37.1 0.0 copy-done.5
  37.1 1.5 %copy.12 = bf16[2,16,128,256]{3,2,0,1:T(8,128)(2,1)} copy(bf16[2,16,128,256]{3,2,1,0:T(8,128)(2,1)S(1)} %copy-done.5) | data formatting | bytes 4194304 | tf_op jit(solution)/shard_map/optimization_barrier | solution.py:185
  38.6 4.3 %all-to-all-start.1 = ((bf16[16,2,128,256]{3,2,1,0:T(8,128)(2,1)}), bf16[16,2,128,256]{3,2,1,0:T(8,128)(2,1)S(1)}, u32[]{:S(2)}, u32[]{:S(2)}) async-start(bf16[16,2,128,256]{3,2,1,0:T(8,128)(2,1)} %bitcast.13), calls=%async_computation.1 | async-start | bytes 4194304 | tf_op jit(solution)/shard_map/all_to_all | solution.py:168
  42.9 6.4 %collective-permute-done.source = bf16[16,2,48,256]{3,2,1,0:T(8,128)(2,1)S(1)} collective-permute-done((bf16[16,2,48,256]{3,2,1,0:T(8,128)(2,1)}, bf16[16,2,48,256]{3,2,1,0:T(8,128)(2,1)S(1)}, u32[]{:S(2)}, u32[]{:S(2)}) %collective-permute-start) | collective-permute-done | bytes 786464 | tf_op jit(solution)/shard_map/ppermute | solution.py:164
  49.3 0.9 copy-done.2
  50.2 0.1 collective-permute-start.1
  50.3 0.0 collective-permute-done.2.source
  50.3 2.6 %collective-permute-start.3 = (bf16[16,2,48,256]{3,2,1,0:T(8,128)(2,1)}, bf16[16,2,48,256]{3,2,1,0:T(8,128)(2,1)}, u32[]{:S(2)}, u32[]{:S(2)}) collective-permute-start(bf16[16,2,48,256]{3,2,1,0:T(8,128)(2,1)} %shard_map.40.refs_5_), channel_id=1, source_target_pairs={{0,48},{16,0},{32,16},{48,32},{1,49},{17,1},{33,17},{49,33},{2,50}... | collective-permute-start | bytes 2359304 | tf_op jit(solution)/shard_map/ppermute | solution.py:164
  52.9 13.4 %collective-permute-done.4.source = bf16[16,2,48,256]{3,2,1,0:T(8,128)(2,1)} collective-permute-done((bf16[16,2,48,256]{3,2,1,0:T(8,128)(2,1)}, bf16[16,2,48,256]{3,2,1,0:T(8,128)(2,1)}, u32[]{:S(2)}, u32[]{:S(2)}) %collective-permute-start.4) | collective-permute-done | bytes 786464 | tf_op jit(solution)/shard_map/ppermute | solution.py:164
  66.3 0.5 all-to-all-done.1.refs_6_
  66.8 6.4 %collective-permute-start.6 = (bf16[16,2,128,256]{3,2,1,0:T(8,128)(2,1)S(1)}, bf16[16,2,128,256]{3,2,1,0:T(8,128)(2,1)}, u32[]{:S(2)}, u32[]{:S(2)}) collective-permute-start(bf16[16,2,128,256]{3,2,1,0:T(8,128)(2,1)S(1)} %all-to-all-done.1.refs_6_), channel_id=1, source_target_pairs={{0,8},{8,0},{1,9},{9,1},{2,10},{10,2},{3,11},{11,3},{4,12},{12,4},... | collective-permute-start | bytes 6291464 | tf_op jit(solution)/shard_map/ppermute | solution.py:164
  73.3 0.0 collective-permute-done.5.source
  73.3 0.0 copy-done.1
  73.3 1.1 copy-done.3
  74.4 4.9 %shard_map.43 = (bf16[4,2,2,2,2,96,128]{6,5,4,3,2,1,0:T(8,128)(2,1)S(1)}, bf16[2,256,2048]{2,1,0:T(8,128)(2,1)S(1)}) custom-call(s32[3]{0:T(128)S(1)} %pad_add_fusion.place, f32[2,16]{1,0:T(2,128)S(1)} %copy-done.1, bf16[16,2,48,256]{3,2,1,0:T(8,128)(2,1)} %get-tuple-element.14.refs_0_, bf16[16,2,48,256]{3,2,1,0:T(8,128)(2,1)} %get-tuple-element.15.refs_1_, ...), custom_call_target="tpu_custom_call" | custom-call | flops 2415919104 | bytes 1048576 | tf_op jit(solution)/shard_map/pallas_call | solution.py:110
  79.3 0.0 collective-permute-done.6.refs_6_
  79.3 5.5 %shard_map.44 = (bf16[4,2,2,2,2,96,128]{6,5,4,3,2,1,0:T(8,128)(2,1)S(1)}, bf16[2,256,2048]{2,1,0:T(8,128)(2,1)S(1)}) custom-call(s32[3]{0:T(128)S(1)} %pad_add_fusion.place, f32[2,16]{1,0:T(2,128)S(1)} %copy-done.1, bf16[16,2,48,256]{3,2,1,0:T(8,128)(2,1)} %get-tuple-element.14.refs_0_, ...), custom_call_target="tpu_custom_call", output_to_operand_aliasing={{0}: (9, {})} | custom-call | flops 2415919104 | bytes 1048576 | tf_op jit(solution)/shard_map/pallas_call | solution.py:110
  84.8 0.0 collective-permute-done.1.refs_0_
  84.8 0.0 collective-permute-done.3.refs_1_
  84.8 3.0 %shard_map.45 = bf16[4,2,2,2,2,96,128]{6,5,4,3,2,1,0:T(8,128)(2,1)S(1)} custom-call(s32[3]{0:T(128)S(1)} %pad_add_fusion.place, f32[2,16]{1,0:T(2,128)S(1)} %copy-done.1, bf16[16,2,48,256]{3,2,1,0:T(8,128)(2,1)S(1)} %collective-permute-done.1.refs_0_, bf16[16,2,48,256]{3,2,1,0:T(8,128)(2,1)} %collective-permute-done.3.refs_1_, ...), custom_call_target="tpu_custom_call", output_to_operand_aliasing={{}: (6, {})} | custom-call | flops 1610612736 | bytes 1048576 | tf_op jit(solution)/shard_map/pallas_call | solution.py:110
  87.8 28.2 %all_to_all.16 = bf16[32,2,96,128]{3,2,1,0:T(8,128)(2,1)S(1)} all-to-all(bf16[32,2,96,128]{3,2,1,0:T(8,128)(2,1)S(1)} %bitcast.11), channel_id=1, replica_groups=mesh['yh'=2,'x'=4,'c'=2,'yl'=2,'z'=4] {'z','yh','c','yl'}, dimensions={0} | all-to-all | bytes 3145728 | tf_op jit(solution)/shard_map/all_to_all | solution.py:226
  116.0 1.2 %shard_map.46 = bf16[2,4,2,2,2,96,128]{6,5,4,3,2,1,0:T(8,128)(2,1)} custom-call(bf16[4,2,2,2,2,96,128]{6,5,4,3,2,1,0:T(8,128)(2,1)S(1)} %bitcast.12), custom_call_target="tpu_custom_call" | custom-call | bytes 3145728 | tf_op jit(solution)/shard_map/pallas_call | solution.py:135
  (10 shorter events, 0.0 us)
Async XLA Ops:
  0.0 1.4 %copy-start = (bf16[2,16,96,256]{3,2,1,0:T(8,128)(2,1)S(1)}, bf16[2,16,96,256]{3,2,1,0:T(8,128)(2,1)}, u32[]{:S(2)}) copy-start(bf16[2,16,96,256]{3,2,1,0:T(8,128)(2,1)} %refs_0_.1) | copy-start | bytes 4718596
  1.5 35.5 %copy-start.5 = (bf16[2,16,128,256]{3,2,1,0:T(8,128)(2,1)S(1)}, bf16[2,16,128,256]{3,2,1,0:T(8,128)(2,1)}, u32[]{:S(2)}) copy-start(bf16[2,16,128,256]{3,2,1,0:T(8,128)(2,1)} %param.3) | copy-start | bytes 6291460
  31.6 17.8 %collective-permute-start = (bf16[16,2,48,256]{3,2,1,0:T(8,128)(2,1)}, bf16[16,2,48,256]{3,2,1,0:T(8,128)(2,1)S(1)}, u32[]{:S(2)}, u32[]{:S(2)}) collective-permute-start(bf16[16,2,48,256]{3,2,1,0:T(8,128)(2,1)} %get-tuple-element.14.refs_0_), channel_id=1, source_target_pairs={{0,16},{16,32},{32,48},{48,0},{1,17},{17,33},{33,49},{49,1},{2,18}... | collective-permute-start | bytes 2359304 | tf_op jit(solution)/shard_map/ppermute | solution.py:164
  32.9 17.4 %collective-permute-start.2 = (bf16[16,2,48,256]{3,2,1,0:T(8,128)(2,1)}, bf16[16,2,48,256]{3,2,1,0:T(8,128)(2,1)}, u32[]{:S(2)}, u32[]{:S(2)}) collective-permute-start(bf16[16,2,48,256]{3,2,1,0:T(8,128)(2,1)} %get-tuple-element.15.refs_1_), channel_id=1, source_target_pairs={{0,48},{16,0},{32,16},{48,32},{1,49},{17,1},{33,17},{49,33},{2,50}... | collective-permute-start | bytes 2359304 | tf_op jit(solution)/shard_map/ppermute | solution.py:164
  34.4 31.9 %collective-permute-start.4 = (bf16[16,2,48,256]{3,2,1,0:T(8,128)(2,1)}, bf16[16,2,48,256]{3,2,1,0:T(8,128)(2,1)}, u32[]{:S(2)}, u32[]{:S(2)}) collective-permute-start(bf16[16,2,48,256]{3,2,1,0:T(8,128)(2,1)} %get-tuple-element.15.refs_1_), channel_id=1, source_target_pairs={{0,16},{16,32},{32,48},{48,0},{1,17},{17,33},{33,49},{49,1},{2,18}... | collective-permute-start | bytes 2359304 | tf_op jit(solution)/shard_map/ppermute | solution.py:164
  34.4 38.9 %collective-permute-start.5 = (bf16[16,2,48,256]{3,2,1,0:T(8,128)(2,1)}, bf16[16,2,48,256]{3,2,1,0:T(8,128)(2,1)}, u32[]{:S(2)}, u32[]{:S(2)}) collective-permute-start(bf16[16,2,48,256]{3,2,1,0:T(8,128)(2,1)} %get-tuple-element.14.refs_0_), channel_id=1, source_target_pairs={{0,48},{16,0},{32,16},{48,32},{1,49},{17,1},{33,17},{49,33},{2,50}... | collective-permute-start | bytes 2359304 | tf_op jit(solution)/shard_map/ppermute | solution.py:164
  38.6 28.3 %all-to-all-start.1 = ((bf16[16,2,128,256]{3,2,1,0:T(8,128)(2,1)}), bf16[16,2,128,256]{3,2,1,0:T(8,128)(2,1)S(1)}, u32[]{:S(2)}, u32[]{:S(2)}) async-start(bf16[16,2,128,256]{3,2,1,0:T(8,128)(2,1)} %bitcast.13), calls=%async_computation.1 | async-start | bytes 4194304 | tf_op jit(solution)/shard_map/all_to_all | solution.py:168
  49.3 0.9 copy-start.2
  50.2 34.6 %collective-permute-start.1 = (bf16[16,2,48,256]{3,2,1,0:T(8,128)(2,1)}, bf16[16,2,48,256]{3,2,1,0:T(8,128)(2,1)S(1)}, u32[]{:S(2)}, u32[]{:S(2)}) collective-permute-start(bf16[16,2,48,256]{3,2,1,0:T(8,128)(2,1)} %shard_map.39.refs_2_), channel_id=1, source_target_pairs={{0,16},{16,32},{32,48},{48,0},{1,17},{17,33},{33,49},{49,1},{2,18}... | collective-permute-start | bytes 2359304 | tf_op jit(solution)/shard_map/ppermute | solution.py:164
  50.3 34.5 %collective-permute-start.3 = (bf16[16,2,48,256]{3,2,1,0:T(8,128)(2,1)}, bf16[16,2,48,256]{3,2,1,0:T(8,128)(2,1)}, u32[]{:S(2)}, u32[]{:S(2)}) collective-permute-start(bf16[16,2,48,256]{3,2,1,0:T(8,128)(2,1)} %shard_map.40.refs_5_), channel_id=1, source_target_pairs={{0,48},{16,0},{32,16},{48,32},{1,49},{17,1},{33,17},{49,33},{2,50}... | collective-permute-start | bytes 2359304 | tf_op jit(solution)/shard_map/ppermute | solution.py:164
  66.3 7.0 %copy-start.1 = (f32[2,16]{1,0:T(2,128)S(1)}, f32[2,16]{1,0:T(2,128)}, u32[]{:S(2)}) copy-start(f32[2,16]{1,0:T(2,128)} %wave.5) | copy-start | bytes 388
  66.8 12.4 %collective-permute-start.6 = (bf16[16,2,128,256]{3,2,1,0:T(8,128)(2,1)S(1)}, bf16[16,2,128,256]{3,2,1,0:T(8,128)(2,1)}, u32[]{:S(2)}, u32[]{:S(2)}) collective-permute-start(bf16[16,2,128,256]{3,2,1,0:T(8,128)(2,1)S(1)} %all-to-all-done.1.refs_6_), channel_id=1, source_target_pairs={{0,8},{8,0},{1,9},{9,1},{2,10},{10,2},{3,11},{11,3},{4,12},{12,4},... | collective-permute-start | bytes 6291464 | tf_op jit(solution)/shard_map/ppermute | solution.py:164
  73.3 1.1 copy-start.3
  74.4 4.9 %copy-start.4 = (bf16[16,2,48,256]{3,2,1,0:T(8,128)(2,1)S(1)}, bf16[16,2,48,256]{3,2,1,0:T(8,128)(2,1)}, u32[]{:S(2)}) copy-start(bf16[16,2,48,256]{3,2,1,0:T(8,128)(2,1)} %shard_map.39.refs_2_) | copy-start | bytes 2359300

commit v11 on v10

--- a/solution.py
+++ b/solution.py
@@ -113,7 +113,7 @@
         in_specs=[smem, smem] + [vmem] * (len(operands) - 2),
         out_specs=[vmem] * len(shapes),
         input_output_aliases=aliases,
-        compiler_params=pltpu.CompilerParams(vmem_limit_bytes=28 * 2**20),
+        compiler_params=pltpu.CompilerParams(vmem_limit_bytes=14 * 2**20),
         cost_estimate=pl.CostEstimate(flops=flops, bytes_accessed=2**20, transcendentals=0),
     )(*operands)
 

time: 118 us -> 118 us (level)
  no operation moved by 1% of the time
where the time goes in v11:
time: 118 us; the launch traced here: 117 us
  blocking collectives  57 us (48%)
  waiting for transfers between devices  20.4 us (17%)
  starting transfers between devices  18.9 us (16%)
  Pallas kernels  15.8 us (13%)
  local copies, waits for them, and re-layouts  4.92 us (4%)
    all_to_all x1, blocking collectives, by_frequency(): return lax.all_to_all(value, FREQUENCY, 0, 0, tiled=True)  28.8 us
    all_to_all x1, blocking collectives, back(): out = lax.all_to_all(out, PLACES, 0, 0, tiled=True)  28.2 us
    ppermute x7, waiting for transfers between devices, shift(): lax.ppermute(value, axis, [(i, (i + step) % size) for i in range(size)])  19.8 us
    ppermute x7, starting transfers between devices, shift(): lax.ppermute(value, axis, [(i, (i + step) % size) for i in range(size)])  14.5 us
    pallas_call x3, Pallas kernels, product(): pl.pallas_call(functools.partial(product_kernel, spots, distances, pack,...  13.3 us
    all_to_all x1, starting transfers between devices, by_frequency(): return lax.all_to_all(value, FREQUENCY, 0, 0, tiled=True)  4.33 us
    unnamed x12, local copies, waits for them, and re-layouts  3.43 us
    pallas_call x3, Pallas kernels, moves(): pl.pallas_call(functools.partial(moves_kernel, pairs, len(values)), out_s...  2.49 us
  transfers between devices with their start and end apart: 8, of which 3 were waited for; matrix products, arithmetic and copies ran while one was open for 1% of the time, Pallas kernels for 9%

profile of v11, /device:TPU:1, one launch (start us, length us, event | category | flops | bytes accessed | tf_op | source)
XLA Modules:
  0.0 117.2 jit_solution(18084133205036187503)
XLA Ops:
  0.0 1.4 %copy-done = bf16[2,16,96,256]{3,2,1,0:T(8,128)(2,1)S(1)} copy-done((bf16[2,16,96,256]{3,2,1,0:T(8,128)(2,1)S(1)}, bf16[2,16,96,256]{3,2,1,0:T(8,128)(2,1)}, u32[]{:S(2)}) %copy-start) | copy-done | bytes 1572888
  1.4 0.1 shard_map.37
  1.5 0.0 copy-start.5
  1.6 28.8 %all_to_all.15.refs_0_ = bf16[16,2,96,256]{3,2,1,0:T(8,128)(2,1)S(1)} all-to-all(bf16[16,2,96,256]{3,2,1,0:T(8,128)(2,1)S(1)} %shard_map.37), channel_id=1, replica_groups=mesh['yh'=2,'x'=4,'c'=2,'yl'=2,'z'=4] {'z','yl','yh'}, dimensions={0} | all-to-all | bytes 3145728 | tf_op jit(solution)/shard_map/all_to_all | solution.py:168
  30.4 1.2 shard_map.38
  31.6 1.3 %collective-permute-start = (bf16[16,2,48,256]{3,2,1,0:T(8,128)(2,1)}, bf16[16,2,48,256]{3,2,1,0:T(8,128)(2,1)S(1)}, u32[]{:S(2)}, u32[]{:S(2)}) collective-permute-start(bf16[16,2,48,256]{3,2,1,0:T(8,128)(2,1)} %get-tuple-element.14.refs_0_), channel_id=1, source_target_pairs={{0,16},{16,32},{32,48},{48,0},{1,17},{17,33},{33,49},{49,1},{2,18}... | collective-permute-start | bytes 2359304 | tf_op jit(solution)/shard_map/ppermute | solution.py:164
  32.8 0.1 pad_add_fusion.place
  32.9 1.5 %collective-permute-start.2 = (bf16[16,2,48,256]{3,2,1,0:T(8,128)(2,1)}, bf16[16,2,48,256]{3,2,1,0:T(8,128)(2,1)}, u32[]{:S(2)}, u32[]{:S(2)}) collective-permute-start(bf16[16,2,48,256]{3,2,1,0:T(8,128)(2,1)} %get-tuple-element.15.refs_1_), channel_id=1, source_target_pairs={{0,48},{16,0},{32,16},{48,32},{1,49},{17,1},{33,17},{49,33},{2,50}... | collective-permute-start | bytes 2359304 | tf_op jit(solution)/shard_map/ppermute | solution.py:164
  34.4 0.0 collective-permute-start.4
  34.4 2.7 %collective-permute-start.5 = (bf16[16,2,48,256]{3,2,1,0:T(8,128)(2,1)}, bf16[16,2,48,256]{3,2,1,0:T(8,128)(2,1)}, u32[]{:S(2)}, u32[]{:S(2)}) collective-permute-start(bf16[16,2,48,256]{3,2,1,0:T(8,128)(2,1)} %get-tuple-element.14.refs_0_), channel_id=1, source_target_pairs={{0,48},{16,0},{32,16},{48,32},{1,49},{17,1},{33,17},{49,33},{2,50}... | collective-permute-start | bytes 2359304 | tf_op jit(solution)/shard_map/ppermute | solution.py:164
  37.1 0.0 copy-done.5
  37.1 1.5 %copy.12 = bf16[2,16,128,256]{3,2,0,1:T(8,128)(2,1)} copy(bf16[2,16,128,256]{3,2,1,0:T(8,128)(2,1)S(1)} %copy-done.5) | data formatting | bytes 4194304 | tf_op jit(solution)/shard_map/optimization_barrier | solution.py:185
  38.6 4.3 %all-to-all-start.1 = ((bf16[16,2,128,256]{3,2,1,0:T(8,128)(2,1)}), bf16[16,2,128,256]{3,2,1,0:T(8,128)(2,1)S(1)}, u32[]{:S(2)}, u32[]{:S(2)}) async-start(bf16[16,2,128,256]{3,2,1,0:T(8,128)(2,1)} %bitcast.13), calls=%async_computation.1 | async-start | bytes 4194304 | tf_op jit(solution)/shard_map/all_to_all | solution.py:168
  42.9 6.4 %collective-permute-done.source = bf16[16,2,48,256]{3,2,1,0:T(8,128)(2,1)S(1)} collective-permute-done((bf16[16,2,48,256]{3,2,1,0:T(8,128)(2,1)}, bf16[16,2,48,256]{3,2,1,0:T(8,128)(2,1)S(1)}, u32[]{:S(2)}, u32[]{:S(2)}) %collective-permute-start) | collective-permute-done | bytes 786464 | tf_op jit(solution)/shard_map/ppermute | solution.py:164
  49.3 0.9 copy-done.2
  50.2 0.1 collective-permute-start.1
  50.3 0.0 collective-permute-done.2.source
  50.3 2.6 %collective-permute-start.3 = (bf16[16,2,48,256]{3,2,1,0:T(8,128)(2,1)}, bf16[16,2,48,256]{3,2,1,0:T(8,128)(2,1)}, u32[]{:S(2)}, u32[]{:S(2)}) collective-permute-start(bf16[16,2,48,256]{3,2,1,0:T(8,128)(2,1)} %shard_map.40.refs_5_), channel_id=1, source_target_pairs={{0,48},{16,0},{32,16},{48,32},{1,49},{17,1},{33,17},{49,33},{2,50}... | collective-permute-start | bytes 2359304 | tf_op jit(solution)/shard_map/ppermute | solution.py:164
  52.9 13.4 %collective-permute-done.4.source = bf16[16,2,48,256]{3,2,1,0:T(8,128)(2,1)} collective-permute-done((bf16[16,2,48,256]{3,2,1,0:T(8,128)(2,1)}, bf16[16,2,48,256]{3,2,1,0:T(8,128)(2,1)}, u32[]{:S(2)}, u32[]{:S(2)}) %collective-permute-start.4) | collective-permute-done | bytes 786464 | tf_op jit(solution)/shard_map/ppermute | solution.py:164
  66.3 0.5 all-to-all-done.1.refs_6_
  66.8 6.4 %collective-permute-start.6 = (bf16[16,2,128,256]{3,2,1,0:T(8,128)(2,1)S(1)}, bf16[16,2,128,256]{3,2,1,0:T(8,128)(2,1)}, u32[]{:S(2)}, u32[]{:S(2)}) collective-permute-start(bf16[16,2,128,256]{3,2,1,0:T(8,128)(2,1)S(1)} %all-to-all-done.1.refs_6_), channel_id=1, source_target_pairs={{0,8},{8,0},{1,9},{9,1},{2,10},{10,2},{3,11},{11,3},{4,12},{12,4},... | collective-permute-start | bytes 6291464 | tf_op jit(solution)/shard_map/ppermute | solution.py:164
  73.3 0.0 collective-permute-done.5.source
  73.3 0.0 copy-done.1
  73.3 1.1 copy-done.3
  74.4 4.9 %shard_map.43 = (bf16[4,2,2,2,2,96,128]{6,5,4,3,2,1,0:T(8,128)(2,1)S(1)}, bf16[2,256,2048]{2,1,0:T(8,128)(2,1)S(1)}) custom-call(s32[3]{0:T(128)S(1)} %pad_add_fusion.place, f32[2,16]{1,0:T(2,128)S(1)} %copy-done.1, bf16[16,2,48,256]{3,2,1,0:T(8,128)(2,1)} %get-tuple-element.14.refs_0_, bf16[16,2,48,256]{3,2,1,0:T(8,128)(2,1)} %get-tuple-element.15.refs_1_, ...), custom_call_target="tpu_custom_call" | custom-call | flops 2415919104 | bytes 1048576 | tf_op jit(solution)/shard_map/pallas_call | solution.py:110
  79.3 0.0 collective-permute-done.6.refs_6_
  79.3 5.5 %shard_map.44 = (bf16[4,2,2,2,2,96,128]{6,5,4,3,2,1,0:T(8,128)(2,1)S(1)}, bf16[2,256,2048]{2,1,0:T(8,128)(2,1)S(1)}) custom-call(s32[3]{0:T(128)S(1)} %pad_add_fusion.place, f32[2,16]{1,0:T(2,128)S(1)} %copy-done.1, bf16[16,2,48,256]{3,2,1,0:T(8,128)(2,1)} %get-tuple-element.14.refs_0_, ...), custom_call_target="tpu_custom_call", output_to_operand_aliasing={{0}: (9, {})} | custom-call | flops 2415919104 | bytes 1048576 | tf_op jit(solution)/shard_map/pallas_call | solution.py:110
  84.8 0.0 collective-permute-done.1.refs_0_
  84.8 0.0 collective-permute-done.3.refs_1_
  84.8 3.0 %shard_map.45 = bf16[4,2,2,2,2,96,128]{6,5,4,3,2,1,0:T(8,128)(2,1)S(1)} custom-call(s32[3]{0:T(128)S(1)} %pad_add_fusion.place, f32[2,16]{1,0:T(2,128)S(1)} %copy-done.1, bf16[16,2,48,256]{3,2,1,0:T(8,128)(2,1)S(1)} %collective-permute-done.1.refs_0_, bf16[16,2,48,256]{3,2,1,0:T(8,128)(2,1)} %collective-permute-done.3.refs_1_, ...), custom_call_target="tpu_custom_call", output_to_operand_aliasing={{}: (6, {})} | custom-call | flops 1610612736 | bytes 1048576 | tf_op jit(solution)/shard_map/pallas_call | solution.py:110
  87.8 28.2 %all_to_all.16 = bf16[32,2,96,128]{3,2,1,0:T(8,128)(2,1)S(1)} all-to-all(bf16[32,2,96,128]{3,2,1,0:T(8,128)(2,1)S(1)} %bitcast.11), channel_id=1, replica_groups=mesh['yh'=2,'x'=4,'c'=2,'yl'=2,'z'=4] {'z','yh','c','yl'}, dimensions={0} | all-to-all | bytes 3145728 | tf_op jit(solution)/shard_map/all_to_all | solution.py:226
  116.0 1.2 %shard_map.46 = bf16[2,4,2,2,2,96,128]{6,5,4,3,2,1,0:T(8,128)(2,1)} custom-call(bf16[4,2,2,2,2,96,128]{6,5,4,3,2,1,0:T(8,128)(2,1)S(1)} %bitcast.12), custom_call_target="tpu_custom_call" | custom-call | bytes 3145728 | tf_op jit(solution)/shard_map/pallas_call | solution.py:135
  (10 shorter events, 0.0 us)
Async XLA Ops:
  0.0 1.4 %copy-start = (bf16[2,16,96,256]{3,2,1,0:T(8,128)(2,1)S(1)}, bf16[2,16,96,256]{3,2,1,0:T(8,128)(2,1)}, u32[]{:S(2)}) copy-start(bf16[2,16,96,256]{3,2,1,0:T(8,128)(2,1)} %refs_0_.1) | copy-start | bytes 4718596
  1.5 35.5 %copy-start.5 = (bf16[2,16,128,256]{3,2,1,0:T(8,128)(2,1)S(1)}, bf16[2,16,128,256]{3,2,1,0:T(8,128)(2,1)}, u32[]{:S(2)}) copy-start(bf16[2,16,128,256]{3,2,1,0:T(8,128)(2,1)} %param.3) | copy-start | bytes 6291460
  31.6 17.8 %collective-permute-start = (bf16[16,2,48,256]{3,2,1,0:T(8,128)(2,1)}, bf16[16,2,48,256]{3,2,1,0:T(8,128)(2,1)S(1)}, u32[]{:S(2)}, u32[]{:S(2)}) collective-permute-start(bf16[16,2,48,256]{3,2,1,0:T(8,128)(2,1)} %get-tuple-element.14.refs_0_), channel_id=1, source_target_pairs={{0,16},{16,32},{32,48},{48,0},{1,17},{17,33},{33,49},{49,1},{2,18}... | collective-permute-start | bytes 2359304 | tf_op jit(solution)/shard_map/ppermute | solution.py:164
  32.9 17.4 %collective-permute-start.2 = (bf16[16,2,48,256]{3,2,1,0:T(8,128)(2,1)}, bf16[16,2,48,256]{3,2,1,0:T(8,128)(2,1)}, u32[]{:S(2)}, u32[]{:S(2)}) collective-permute-start(bf16[16,2,48,256]{3,2,1,0:T(8,128)(2,1)} %get-tuple-element.15.refs_1_), channel_id=1, source_target_pairs={{0,48},{16,0},{32,16},{48,32},{1,49},{17,1},{33,17},{49,33},{2,50}... | collective-permute-start | bytes 2359304 | tf_op jit(solution)/shard_map/ppermute | solution.py:164
  34.4 31.9 %collective-permute-start.4 = (bf16[16,2,48,256]{3,2,1,0:T(8,128)(2,1)}, bf16[16,2,48,256]{3,2,1,0:T(8,128)(2,1)}, u32[]{:S(2)}, u32[]{:S(2)}) collective-permute-start(bf16[16,2,48,256]{3,2,1,0:T(8,128)(2,1)} %get-tuple-element.15.refs_1_), channel_id=1, source_target_pairs={{0,16},{16,32},{32,48},{48,0},{1,17},{17,33},{33,49},{49,1},{2,18}... | collective-permute-start | bytes 2359304 | tf_op jit(solution)/shard_map/ppermute | solution.py:164
  34.4 38.9 %collective-permute-start.5 = (bf16[16,2,48,256]{3,2,1,0:T(8,128)(2,1)}, bf16[16,2,48,256]{3,2,1,0:T(8,128)(2,1)}, u32[]{:S(2)}, u32[]{:S(2)}) collective-permute-start(bf16[16,2,48,256]{3,2,1,0:T(8,128)(2,1)} %get-tuple-element.14.refs_0_), channel_id=1, source_target_pairs={{0,48},{16,0},{32,16},{48,32},{1,49},{17,1},{33,17},{49,33},{2,50}... | collective-permute-start | bytes 2359304 | tf_op jit(solution)/shard_map/ppermute | solution.py:164
  38.6 28.3 %all-to-all-start.1 = ((bf16[16,2,128,256]{3,2,1,0:T(8,128)(2,1)}), bf16[16,2,128,256]{3,2,1,0:T(8,128)(2,1)S(1)}, u32[]{:S(2)}, u32[]{:S(2)}) async-start(bf16[16,2,128,256]{3,2,1,0:T(8,128)(2,1)} %bitcast.13), calls=%async_computation.1 | async-start | bytes 4194304 | tf_op jit(solution)/shard_map/all_to_all | solution.py:168
  49.3 0.9 copy-start.2
  50.2 34.6 %collective-permute-start.1 = (bf16[16,2,48,256]{3,2,1,0:T(8,128)(2,1)}, bf16[16,2,48,256]{3,2,1,0:T(8,128)(2,1)S(1)}, u32[]{:S(2)}, u32[]{:S(2)}) collective-permute-start(bf16[16,2,48,256]{3,2,1,0:T(8,128)(2,1)} %shard_map.39.refs_2_), channel_id=1, source_target_pairs={{0,16},{16,32},{32,48},{48,0},{1,17},{17,33},{33,49},{49,1},{2,18}... | collective-permute-start | bytes 2359304 | tf_op jit(solution)/shard_map/ppermute | solution.py:164
  50.3 34.5 %collective-permute-start.3 = (bf16[16,2,48,256]{3,2,1,0:T(8,128)(2,1)}, bf16[16,2,48,256]{3,2,1,0:T(8,128)(2,1)}, u32[]{:S(2)}, u32[]{:S(2)}) collective-permute-start(bf16[16,2,48,256]{3,2,1,0:T(8,128)(2,1)} %shard_map.40.refs_5_), channel_id=1, source_target_pairs={{0,48},{16,0},{32,16},{48,32},{1,49},{17,1},{33,17},{49,33},{2,50}... | collective-permute-start | bytes 2359304 | tf_op jit(solution)/shard_map/ppermute | solution.py:164
  66.3 7.0 %copy-start.1 = (f32[2,16]{1,0:T(2,128)S(1)}, f32[2,16]{1,0:T(2,128)}, u32[]{:S(2)}) copy-start(f32[2,16]{1,0:T(2,128)} %wave.5) | copy-start | bytes 388
  66.8 12.4 %collective-permute-start.6 = (bf16[16,2,128,256]{3,2,1,0:T(8,128)(2,1)S(1)}, bf16[16,2,128,256]{3,2,1,0:T(8,128)(2,1)}, u32[]{:S(2)}, u32[]{:S(2)}) collective-permute-start(bf16[16,2,128,256]{3,2,1,0:T(8,128)(2,1)S(1)} %all-to-all-done.1.refs_6_), channel_id=1, source_target_pairs={{0,8},{8,0},{1,9},{9,1},{2,10},{10,2},{3,11},{11,3},{4,12},{12,4},... | collective-permute-start | bytes 6291464 | tf_op jit(solution)/shard_map/ppermute | solution.py:164
  73.3 1.1 copy-start.3
  74.4 4.9 %copy-start.4 = (bf16[16,2,48,256]{3,2,1,0:T(8,128)(2,1)S(1)}, bf16[16,2,48,256]{3,2,1,0:T(8,128)(2,1)}, u32[]{:S(2)}) copy-start(bf16[16,2,48,256]{3,2,1,0:T(8,128)(2,1)} %shard_map.39.refs_2_) | copy-start | bytes 2359300
